TPU v7x, 32 devices: a whole 2x2x4 slice. The times are simulated.
32 devices in a mesh: trade: 4 (over z), path: 8 (over y, x, core).
Axes of the slice: x: 2, y: 2, z: 4, core: 2. Of those that a mesh axis runs over, the one named last changes fastest.
Arguments:
- start_state: float32 [4096, 32], P('path'), may hold values from -6 to 6
- shocks: float32 [2, 4096, 32], P(None, 'path'), may hold values from -6 to 6
- loadings: float32 [32, 32768], P(None, 'trade'), may hold values from -1 to 1
- strikes: float32 [32768], P('trade'), may hold values from -0.5 to 1
- notionals: float32 [32768], P('trade'), may hold values from -1 to 1
- trade_set: int32 [32768], P('trade'), may hold values from 0 to 1023
- live_counts: int32 [4], replicated, may hold values from 1 to 8192, 24576 in all
- weights: int32 [4096], P('path'), may hold values from 1 to 16
- thresholds: int32 [1024], P('trade'), may hold values from 0 to 8
Outputs:
- exposure: float32 [2, 1024, 4096], P(None, 'trade', 'path')
- expected: float32 [2, 1024], P(None, 'trade')
Inputs may be any that keep to these rules, and one draw needn't show every extreme that they name: The live slots of group g are its first live_counts[g] slots; the counts sum to 24576 and some group is full.
All inputs are finite; a program needn't handle non-finite values.
Results may differ from a plain program's by a relative error of at most 0.0003.
Values sent between devices are 32-bit elements; how exact they have to be, the bound alone decides.
No kernel may reach another device: no remote copies, remote signals or barrier semaphores. Data moves between devices by JAX's collectives and lax.ppermute only.
A program may use at most 128 MiB of HBM per device.

v0:
```python
import functools

import jax
import jax.numpy as jnp
from jax import lax
from jax.experimental import pallas as pl
from jax.experimental.pallas import tpu as pltpu
from jax.sharding import PartitionSpec as P

HIGHEST_PREC = lax.Precision.HIGHEST
ROOT_HALF = 0.7071067811865476
F32 = jnp.float32
BF16 = jnp.bfloat16
TILE = 512
DEPTH = 256
PAD = 8
MIB = 1024 * 1024
NN = (((1,), (0,)), ((), ()))
NT = (((1,), (1,)), ((), ()))
VMEM = pl.BlockSpec(memory_space=pltpu.VMEM)
SMEM = pl.BlockSpec(memory_space=pltpu.SMEM)


def mm(a, b, dims=NN):
    return lax.dot_general(a, b, dims, preferred_element_type=F32)


def mm_full(a, b, dims=NN):
    return lax.dot_general(a, b, dims, preferred_element_type=F32, precision=HIGHEST_PREC)


def split2(x):
    hi = x.astype(BF16)
    return hi, (x - hi.astype(F32)).astype(BF16)


def split3(x):
    hi = x.astype(BF16)
    rest = x - hi.astype(F32)
    mid = rest.astype(BF16)
    return hi, mid, (rest - mid.astype(F32)).astype(BF16)


def log2(n):
    assert n & (n - 1) == 0
    return n.bit_length() - 1


def basis_rows(state):
    return jnp.concatenate([state, (state * state - 1.0) * ROOT_HALF], axis=0)


def pick(core, first, second):
    return jnp.where(core == 0, first, second)


def states_of(ref, factors):
    state = ref[:factors, :]
    return state, 0.8 * state + 0.6 * ref[factors : 2 * factors, :]


def weights_of(ref, factors):
    return ref[2 * factors : 2 * factors + 1, :]


def prepare(block_ref, states_scr, wide_scr, load_scr, factors):
    core = lax.axis_index("path") & 1
    first, second = states_of(block_ref, factors)
    third = 0.8 * second + 0.6 * block_ref[2 * factors + PAD :, :]
    hi, lo = split2(basis_rows(pick(core, first, second)) * weights_of(block_ref, factors))
    wide_scr[...] = jnp.concatenate([hi, lo], axis=0)
    hi, mid, low = split3(pick(core, second, third))
    hi, mid, low = hi.astype(F32), mid.astype(F32), low.astype(F32)
    paths = block_ref.shape[1]
    ones = jnp.where(lax.broadcasted_iota(jnp.int32, (DEPTH - 6 * factors, paths), 0) < 3, 1.0, 0.0)
    states_scr[...] = jnp.concatenate([hi, hi, mid, mid, hi, low, ones], axis=0).T.astype(BF16)
    load_scr[...] = jnp.zeros_like(load_scr)


def path_moments(cols, load_ref, strike_ref, states_scr, wide_scr, load_scr, slot):
    factors = load_ref.shape[0]
    wide = 2 * factors
    hi, mid, low = split3(load_ref[:, cols])
    for part, piece in enumerate((hi, mid, hi, mid, low, hi)):
        load_scr[slot, pl.ds(part * factors, factors), :] = piece
    s_hi, s_mid, s_low = split3(-strike_ref[:, cols])
    rows = lax.broadcasted_iota(jnp.int32, (16, TILE), 0)
    strike_rows = jnp.where(rows == 1, s_mid.astype(F32), jnp.where(rows == 2, s_low.astype(F32), 0.0))
    strike_rows = jnp.where(rows == 0, s_hi.astype(F32), strike_rows)
    load_scr[slot, pl.ds(6 * factors, 16), :] = strike_rows.astype(BF16)
    hi, lo = split2(jnp.maximum(mm(states_scr[...], load_scr[slot]), 0.0))
    both = mm(wide_scr[...], hi)
    return both[:wide] + both[wide:] + mm(wide_scr[:wide], lo)


def tile_at(index):
    return pl.ds(pl.multiple_of(index * TILE, TILE), TILE)


def first_kernel(block_ref, load_ref, strike_ref, moment_ref, states_scr, wide_scr, load_scr):
    prepare(block_ref, states_scr, wide_scr, load_scr, load_ref.shape[0])

    def step(pair, carry):
        for slot in range(2):
            cols = tile_at(2 * pair + slot)
            moment_ref[:, cols] = path_moments(cols, load_ref, strike_ref, states_scr, wide_scr, load_scr, slot)
        return carry

    lax.fori_loop(0, load_ref.shape[1] // (2 * TILE), step, 0)


def second_kernel(groups, counts_ref, block_ref, moment_ref, load_ref, strike_ref, notional_ref, set_ref, *refs):
    outs, (net_scr, states_scr, wide_scr, load_scr) = refs[:groups], refs[groups:]
    group = lax.axis_index("trade")
    filled = counts_ref[group]
    sets = net_scr.shape[0]
    owned = sets // groups
    bits = log2(owned)
    prepare(block_ref, states_scr, wide_scr, load_scr, load_ref.shape[0])
    net_scr[...] = jnp.zeros_like(net_scr)

    def step(pair, carry):
        for slot in range(2):
            index = 2 * pair + slot
            cols = tile_at(index)
            moment = moment_ref[:, cols]
            moment = moment + path_moments(cols, load_ref, strike_ref, states_scr, wide_scr, load_scr, slot)
            slot_ids = index * TILE + lax.broadcasted_iota(jnp.int32, (1, TILE), 1)
            hi, lo = split2(moment * jnp.where(slot_ids < filled, notional_ref[:, cols], 0.0))
            places = set_ref[:, cols] ^ (group << bits)
            one_hot = lax.broadcasted_iota(jnp.int16, (sets, TILE), 0) == places.astype(jnp.int16)
            one_hot = jnp.where(one_hot, jnp.ones((), BF16), jnp.zeros((), BF16))
            net_scr[...] += mm(one_hot, jnp.concatenate([hi, lo], axis=0), NT)
        return carry

    lax.fori_loop(0, load_ref.shape[1] // (2 * TILE), step, 0)
    wide = net_scr.shape[1] // 2
    half = owned // 2
    for away, out in enumerate(outs):
        net = net_scr[away * owned : (away + 1) * owned, :]
        net = net[:, :wide] + net[:, wide:]
        out[...] = jnp.concatenate([net[:half], net[half:]], axis=1)


def inverse_kernel(factors, *refs):
    blocks, inverse_ref = refs[:-1], refs[-1]
    core = lax.axis_index("path") & 1
    wide = 2 * factors
    sub = lax.broadcasted_iota(jnp.int32, (wide, wide), 0)
    lane = lax.broadcasted_iota(jnp.int32, (wide, wide), 1)
    gram = jnp.zeros((wide, wide), F32)
    for block in path_blocks(blocks):
        basis = basis_rows(pick(core, *states_of(block, factors)))
        gram = gram + mm_full(basis * weights_of(block, factors), basis, NT)
    mat = gram
    for k in range(wide):
        row = mat[k : k + 1, :]
        col = mat[:, k : k + 1]
        pivot = 1.0 / mat[k : k + 1, k : k + 1]
        row = jnp.where(lane[:1] == k, 1.0, row) * pivot
        mat = jnp.where(sub == k, row, jnp.where(lane == k, 0.0, mat) - col * row)
    eye = jnp.where(sub == lane, 1.0, 0.0)
    mat = mat + mm_full(mat, eye - mm_full(gram, mat))
    zero = jnp.zeros_like(mat)
    upper = jnp.concatenate([mat, zero], axis=1)
    inverse_ref[...] = jnp.concatenate([upper, jnp.concatenate([zero, mat], axis=1)], axis=0)


def path_blocks(refs):
    for ref in refs:
        if len(ref.shape) == 2:
            yield ref
        else:
            for index in range(ref.shape[0]):
                yield ref.at[index]


def sum_kernel(*refs):
    total = refs[0][...]
    for ref in refs[1:-1]:
        total = total + ref[...]
    refs[-1][...] = total


def coeff_kernel(*refs):
    total = refs[0][...]
    for ref in refs[1:-2]:
        total = total + ref[...]
    refs[-1][...] = mm_full(total, refs[-2][...])


def exposure_kernel(factors, mine_ref, other_ref, limits_ref, *refs):
    blocks, (exposure_ref, expected_ref) = refs[:-2], refs[-2:]
    core = lax.axis_index("path") & 1
    wide = 2 * factors
    paths = blocks[0].shape[1]
    limits = 0.25 * limits_ref[...].astype(F32)
    mine, other = mine_ref[...], other_ref[...]
    coeffs = []
    for packed in (pick(core, mine, other), pick(core, other, mine)):
        hi, lo = split2(jnp.concatenate([packed[:, :wide], packed[:, wide:]], axis=0))
        coeffs.append(jnp.concatenate([hi, hi, lo], axis=1))
    sums = [jnp.zeros((limits.shape[0], 128), F32) for _ in coeffs]
    total = jnp.zeros((1, 1), F32)
    for number, block in enumerate(path_blocks(blocks)):
        weight_row = weights_of(block, factors)
        total = total + jnp.sum(weight_row, keepdims=True)
        for date, state in enumerate(states_of(block, factors)):
            hi, lo = split2(basis_rows(state))
            value = jnp.maximum(mm(coeffs[date], jnp.concatenate([hi, lo, hi], axis=0)) - limits, 0.0)
            if number == 0:
                exposure_ref[date] = value
            product = value * weight_row
            for c in range(paths // 128):
                sums[date] = sums[date] + product[:, c * 128 : (c + 1) * 128]
    for date, partial in enumerate(sums):
        expected_ref[date : date + 1, :] = jnp.sum(partial.T, axis=0, keepdims=True) / total


def swap(x, axis, away):
    return lax.ppermute(x, axis, [(i, i ^ away) for i in range(lax.axis_size(axis))])


def run(kernel, name, out, specs, args, mib, scratch=(), gflops=0.0):
    return pl.pallas_call(
        kernel,
        out_shape=out,
        in_specs=specs,
        out_specs=jax.tree.map(lambda _: VMEM, out),
        scratch_shapes=list(scratch),
        compiler_params=pltpu.CompilerParams(vmem_limit_bytes=mib * MIB),
        cost_estimate=pl.CostEstimate(flops=int(gflops * 1e9), bytes_accessed=10**5, transcendentals=0),
        name=name,
    )(*args)


def body(
    start_state, shocks, loadings, strikes, notionals, trade_set, live_counts, weights, thresholds
):
    paths, factors = start_state.shape
    dates = shocks.shape[0]
    slots = loadings.shape[1]
    owned = thresholds.shape[0]
    groups = lax.axis_size("trade")
    ranks = lax.axis_size("path")
    sets = owned * groups
    wide = 2 * factors
    assert dates == 2

    shocks_t = jnp.swapaxes(shocks, 1, 2)
    weight_rows = jnp.broadcast_to(weights.astype(F32), (PAD, paths))
    short = jnp.concatenate([start_state.T, shocks_t[0], weight_rows], axis=0)
    whole = jnp.concatenate([start_state.T, shocks_t[0], weight_rows, shocks_t[1]], axis=0)
    other = swap(whole, "path", 1)
    across = jnp.stack([swap(short, "path", 2 * away) for away in range(1, ranks // 2)])

    shape = jax.ShapeDtypeStruct
    scratch = [
        pltpu.VMEM((paths, DEPTH), BF16),
        pltpu.VMEM((2 * wide, paths), BF16),
        pltpu.VMEM((2, DEPTH, TILE), BF16),
    ]
    strike_row, notional_row, set_row = strikes[None, :], notionals[None, :], trade_set[None, :]
    moment = run(
        first_kernel, "own_path_moments", shape((wide, slots), F32), [VMEM] * 3,
        (whole, loadings, strike_row), 48, scratch, 8.0,
    )
    other, across = lax.optimization_barrier((other, across))
    others = swap(across, "path", 1)
    nets = run(
        functools.partial(second_kernel, groups), "other_path_moments",
        [shape((owned // 2, 2 * wide), F32)] * groups, [SMEM] + [VMEM] * 6,
        (live_counts, other, moment, loadings, strike_row, notional_row, set_row), 48,
        [pltpu.VMEM((sets, 2 * wide), F32)] + scratch, 12.0,
    )
    got = [swap(nets[away], "trade", away) for away in range(1, groups)]
    blocks = (whole, other, across, others)
    inverse = run(
        functools.partial(inverse_kernel, factors), "gram_inverse", shape((2 * wide, 2 * wide), F32),
        [VMEM] * 4, blocks, 8, (), 6.0,
    )
    part = run(
        sum_kernel, "group_sum", shape((owned // 2, 2 * wide), F32), [VMEM] * groups, [nets[0]] + got, 4
    )
    got = [swap(part, "path", 2 * away) for away in range(1, ranks // 2)]
    mine = run(
        coeff_kernel, "set_coeffs", shape((owned // 2, 2 * wide), F32), [VMEM] * (ranks // 2 + 1),
        [part] + got + [inverse], 4,
    )
    partner = swap(mine, "path", 1)
    exposure, expected = run(
        functools.partial(exposure_kernel, factors), "set_exposure",
        (shape((dates, owned, paths), F32), shape((dates, owned), F32)), [VMEM] * 7,
        (mine, partner, thresholds[:, None], *blocks), 16, (), 2.0,
    )
    return (exposure, expected)


def solution(mesh):
    placed = (
        P("path", None),
        P(None, "path", None),
        P(None, "trade"),
        P("trade"),
        P("trade"),
        P("trade"),
        P(),
        P("path"),
        P("trade"),
    )
    return jax.shard_map(
        body,
        mesh=mesh,
        in_specs=placed,
        out_specs=(P(None, "trade", "path"), P(None, "trade")),
        check_vma=False,
    )
```

profile of v0, /device:TPU:0, one launch (start us, length us, event | category | flops | bytes accessed | tf_op | source)
XLA Modules:
  0.0 63.1 jit_solution(12710815576228855630)
XLA Ops:
  0.6 0.9 %slice_bitcast_fusion.1 = (f32[32,512]{1,0:T(8,128)S(1)}, f32[32,512]{1,0:T(8,128)S(1)}) fusion(f32[2,32,512]{2,1,0:T(8,128)} %bitcast.22), kind=kLoop, calls=%fused_computation.4 | loop fusion | bytes 262144 | tf_op jit(solution)/shard_map/squeeze | solution.py:253
  1.5 0.7 %convert_element_type.3 = f32[512]{0:T(512)S(1)} convert(s32[512]{0:T(512)} %param.16) | non-fusion elementwise | flops 512 | bytes 4096 | tf_op jit(solution)/shard_map/convert_element_type | solution.py:251
  2.2 0.8 %pad_maximum_fusion.2 = f32[72,512]{1,0:T(8,128)S(1)} fusion(f32[8,512]{1,0:T(8,128)S(1)} %broadcast_in_dim.15, f32[32,512]{1,0:T(8,128)S(1)} %get-tuple-element.14, f32[32,512]{1,0:T(8,128)} %bitcast.17), kind=kLoop, calls=%fused_computation.2 | loop fusion | flops 73728 | bytes 294912 | tf_op jit(solution)/shard_map/concatenate | solution.py:252
  3.1 4.0 %collective-permute-start.3 = (f32[72,512]{1,0:T(8,128)S(1)}, f32[72,512]{1,0:T(8,128)S(1)}, u32[]{:S(2)}, u32[]{:S(2)}) collective-permute-start(f32[72,512]{1,0:T(8,128)S(1)} %pad_maximum_fusion.2), channel_id=1, source_target_pairs={{0,6},{1,7},{2,4},{3,5},{4,2},{5,3},{6,0},{7,1},{8,14},{9,15},{10,... | collective-permute-start | bytes 442376 | tf_op jit(solution)/shard_map/ppermute | solution.py:221
  7.0 0.5 collective-permute-start.2
  7.5 0.1 collective-permute-start.1
  7.7 0.9 %pad_maximum_fusion.1.block_ref.refs_0_ = f32[104,512]{1,0:T(8,128)S(1)} fusion(f32[32,512]{1,0:T(8,128)S(1)} %get-tuple-element.15, f32[8,512]{1,0:T(8,128)S(1)} %broadcast_in_dim.15, f32[32,512]{1,0:T(8,128)S(1)} %get-tuple-element.14, f32[32,512]{1,0:T(8,128)} %bitcast.18), kind=kLoop, calls=%fused_computation.1 | loop fusion | flops 159744 | bytes 425984 | tf_op jit(solution)/shard_map/concatenate | solution.py:253
  8.5 0.1 collective-permute-start
  8.6 0.0 copy-start
  8.6 1.2 %copy-done = f32[32,8192]{1,0:T(8,128)S(1)} copy-done((f32[32,8192]{1,0:T(8,128)S(1)}, f32[32,8192]{1,0:T(8,128)}, u32[]{:S(2)}) %copy-start) | copy-done | bytes 1048600
  9.8 0.0 copy-start.1
  9.8 0.8 %copy-done.1 = f32[8192]{0:T(1024)S(1)} copy-done((f32[8192]{0:T(1024)S(1)}, f32[8192]{0:T(1024)}, u32[]{:S(2)}) %copy-start.1) | copy-done | bytes 32792
  10.6 0.0 copy-start.2
  10.6 0.0 copy-start.3
  10.6 0.0 copy-start.4
  10.6 8.0 %own_path_moments.1.moment_ref = f32[64,8192]{1,0:T(8,128)S(1)} custom-call(f32[104,512]{1,0:T(8,128)S(1)} %pad_maximum_fusion.1.block_ref.refs_0_, f32[32,8192]{1,0:T(8,128)S(1)} %copy-done, f32[1,8192]{1,0:T(1,128)S(1)} %bitcast.13), custom_call_target="tpu_custom_call" | custom-call | flops 8000000000 | bytes 100000 | tf_op jit(solution)/shard_map/own_path_moments/pallas_call | solution.py:225
  18.6 0.0 collective-permute-done.3
  18.6 0.0 collective-permute-done.2
  18.7 0.0 collective-permute-done.1
  18.7 0.0 collective-permute-done.block_ref.refs_1_
  18.7 0.6 collective-permute-start.10
  19.3 0.0 copy-done.2
  19.3 0.0 copy-done.3
  19.3 0.0 copy-done.4
  19.3 18.3 %other_path_moments.1 = (f32[128,128]{1,0:T(8,128)S(1)}, f32[128,128]{1,0:T(8,128)S(1)}, f32[128,128]{1,0:T(8,128)S(1)}, f32[128,128]{1,0:T(8,128)S(1)}) custom-call(s32[4]{0:T(128)S(1)} %copy-done.4, f32[104,512]{1,0:T(8,128)S(1)} %collective-permute-done.block_ref.refs_1_, f32[64,8192]{1,0:T(8,128)S(1)} %own_path_moments.1.moment_ref, ...), custom_call_target="tpu_custom_call" | custom-call | flops 12000000000 | bytes 100000 | tf_op jit(solution)/shard_map/other_path_moments/pallas_call | solution.py:225
  37.5 2.0 %collective-permute-start.4 = (f32[128,128]{1,0:T(8,128)S(1)}, f32[128,128]{1,0:T(8,128)S(1)}, u32[]{:S(2)}, u32[]{:S(2)}) collective-permute-start(f32[128,128]{1,0:T(8,128)S(1)} %get-tuple-element.10), channel_id=1, source_target_pairs={{0,8},{8,0},{16,24},{24,16},{1,9},{9,1},{17,25},{25,17},{2,10},{10... | collective-permute-start | bytes 196616 | tf_op jit(solution)/shard_map/ppermute | solution.py:221
  39.6 2.6 %collective-permute-start.5 = (f32[128,128]{1,0:T(8,128)S(1)}, f32[128,128]{1,0:T(8,128)S(1)}, u32[]{:S(2)}, u32[]{:S(2)}) collective-permute-start(f32[128,128]{1,0:T(8,128)S(1)} %get-tuple-element.11), channel_id=1, source_target_pairs={{0,16},{8,24},{16,0},{24,8},{1,17},{9,25},{17,1},{25,9},{2,18},{10... | collective-permute-start | bytes 196616 | tf_op jit(solution)/shard_map/ppermute | solution.py:221
  42.2 0.0 collective-permute-start.6
  42.2 0.0 collective-permute-done.4.refs_1_
  42.2 4.9 %collective-permute-done.5.refs_2_ = f32[128,128]{1,0:T(8,128)S(1)} collective-permute-done((f32[128,128]{1,0:T(8,128)S(1)}, f32[128,128]{1,0:T(8,128)S(1)}, u32[]{:S(2)}, u32[]{:S(2)}) %collective-permute-start.5) | collective-permute-done | bytes 65568 | tf_op jit(solution)/shard_map/ppermute | solution.py:221
  47.1 1.3 %collective-permute-done.6.refs_3_ = f32[128,128]{1,0:T(8,128)S(1)} collective-permute-done((f32[128,128]{1,0:T(8,128)S(1)}, f32[128,128]{1,0:T(8,128)S(1)}, u32[]{:S(2)}, u32[]{:S(2)}) %collective-permute-start.6) | collective-permute-done | bytes 65568 | tf_op jit(solution)/shard_map/ppermute | solution.py:221
  48.4 0.0 copy-start.5
  48.4 1.6 %collective-permute-start.7 = (f32[128,128]{1,0:T(8,128)S(1)}, f32[128,128]{1,0:T(8,128)S(1)}, u32[]{:S(2)}, u32[]{:S(2)}) collective-permute-start(f32[128,128]{1,0:T(8,128)S(1)} %group_sum.1.refs_0_), channel_id=1, source_target_pairs={{0,2},{1,3},{2,0},{3,1},{4,6},{5,7},{6,4},{7,5},{8,10},{9,11},{10,... | collective-permute-start | bytes 196616 | tf_op jit(solution)/shard_map/ppermute | solution.py:221
  49.9 1.5 %collective-permute-start.8 = (f32[128,128]{1,0:T(8,128)S(1)}, f32[128,128]{1,0:T(8,128)S(1)}, u32[]{:S(2)}, u32[]{:S(2)}) collective-permute-start(f32[128,128]{1,0:T(8,128)S(1)} %group_sum.1.refs_0_), channel_id=1, source_target_pairs={{0,4},{1,5},{2,6},{3,7},{4,0},{5,1},{6,2},{7,3},{8,12},{9,13},{10,... | collective-permute-start | bytes 196616 | tf_op jit(solution)/shard_map/ppermute | solution.py:221
  51.4 0.5 collective-permute-start.9
  51.9 0.0 collective-permute-done.10.refs_3_
  51.9 6.9 %gram_inverse.1.refs_4_ = f32[128,128]{1,0:T(8,128)S(1)} custom-call(f32[104,512]{1,0:T(8,128)S(1)} %pad_maximum_fusion.1.block_ref.refs_0_, f32[104,512]{1,0:T(8,128)S(1)} %collective-permute-done.block_ref.refs_1_, f32[3,72,512]{2,1,0:T(8,128)S(1)} %pad_maximum_fusion.refs_2_, f32[3,72,512]{2,1,0:T(8,128)S(1)} %collective-permute-done.10.refs_3_), custom_call_target="tpu_custom_call" | custom-call | flops 6000000000 | bytes 100000 | tf_op jit(solution)/shard_map/gram_inverse/pallas_call | solution.py:225
  58.8 0.0 collective-permute-done.7.refs_1_
  58.8 0.0 collective-permute-done.8.refs_2_
  58.8 0.0 collective-permute-done.9.refs_3_
  58.8 0.2 set_coeffs.1.mine_ref
  59.0 0.1 collective-permute-start.11
  59.1 0.0 copy-done.5
  59.1 0.1 copy.11.limits_ref
  59.3 1.1 %collective-permute-done.11.other_ref = f32[128,128]{1,0:T(8,128)S(1)} collective-permute-done((f32[128,128]{1,0:T(8,128)S(1)}, f32[128,128]{1,0:T(8,128)S(1)}, u32[]{:S(2)}, u32[]{:S(2)}) %collective-permute-start.11) | collective-permute-done | bytes 65568 | tf_op jit(solution)/shard_map/ppermute | solution.py:221
  60.4 2.8 %set_exposure.1 = (f32[2,256,512]{2,1,0:T(8,128)}, f32[2,256]{1,0:T(2,128)}) custom-call(f32[128,128]{1,0:T(8,128)S(1)} %set_coeffs.1.mine_ref, f32[128,128]{1,0:T(8,128)S(1)} %collective-permute-done.11.other_ref, s32[256,1]{1,0:T(8,128)S(1)} %copy.11.limits_ref, f32[104,512]{1,0:T(8,128)S(1)} %pad_maximum_fusion.1.block_ref.refs_0_, ...), custom_call_target="tpu_custom_call" | custom-call | flops 2000000000 | bytes 100000 | tf_op jit(solution)/shard_map/set_exposure/pallas_call | solution.py:225
  (3 shorter events, 0.1 us)
Async XLA Ops:
  3.1 15.6 %collective-permute-start.3 = (f32[72,512]{1,0:T(8,128)S(1)}, f32[72,512]{1,0:T(8,128)S(1)}, u32[]{:S(2)}, u32[]{:S(2)}) collective-permute-start(f32[72,512]{1,0:T(8,128)S(1)} %pad_maximum_fusion.2), channel_id=1, source_target_pairs={{0,6},{1,7},{2,4},{3,5},{4,2},{5,3},{6,0},{7,1},{8,14},{9,15},{10,... | collective-permute-start | bytes 442376 | tf_op jit(solution)/shard_map/ppermute | solution.py:221
  7.0 11.6 %collective-permute-start.2 = (f32[72,512]{1,0:T(8,128)S(1)}, f32[72,512]{1,0:T(8,128)S(1)}, u32[]{:S(2)}, u32[]{:S(2)}) collective-permute-start(f32[72,512]{1,0:T(8,128)S(1)} %pad_maximum_fusion.2), channel_id=1, source_target_pairs={{0,4},{1,5},{2,6},{3,7},{4,0},{5,1},{6,2},{7,3},{8,12},{9,13},{10,... | collective-permute-start | bytes 442376 | tf_op jit(solution)/shard_map/ppermute | solution.py:221
  7.5 11.1 %collective-permute-start.1 = (f32[72,512]{1,0:T(8,128)S(1)}, f32[72,512]{1,0:T(8,128)S(1)}, u32[]{:S(2)}, u32[]{:S(2)}) collective-permute-start(f32[72,512]{1,0:T(8,128)S(1)} %pad_maximum_fusion.2), channel_id=1, source_target_pairs={{0,2},{1,3},{2,0},{3,1},{4,6},{5,7},{6,4},{7,5},{8,10},{9,11},{10,... | collective-permute-start | bytes 442376 | tf_op jit(solution)/shard_map/ppermute | solution.py:221
  8.5 10.2 %collective-permute-start = (f32[104,512]{1,0:T(8,128)S(1)}, f32[104,512]{1,0:T(8,128)S(1)}, u32[]{:S(2)}, u32[]{:S(2)}) collective-permute-start(f32[104,512]{1,0:T(8,128)S(1)} %pad_maximum_fusion.1.block_ref.refs_0_), channel_id=1, source_target_pairs={{0,1},{1,0},{2,3},{3,2},{4,5},{5,4},{6,7},{7,6},{8,9},{9,8},{10,11... | collective-permute-start | bytes 638984 | tf_op jit(solution)/shard_map/ppermute | solution.py:221
  8.6 1.2 %copy-start = (f32[32,8192]{1,0:T(8,128)S(1)}, f32[32,8192]{1,0:T(8,128)}, u32[]{:S(2)}) copy-start(f32[32,8192]{1,0:T(8,128)} %load_ref.3) | copy-start | bytes 3145732
  9.8 0.8 %copy-start.1 = (f32[8192]{0:T(1024)S(1)}, f32[8192]{0:T(1024)}, u32[]{:S(2)}) copy-start(f32[8192]{0:T(1024)} %param.12) | copy-start | bytes 98308
  10.6 8.7 %copy-start.2 = (f32[8192]{0:T(1024)S(1)}, f32[8192]{0:T(1024)}, u32[]{:S(2)}) copy-start(f32[8192]{0:T(1024)} %param.13) | copy-start | bytes 98308
  10.6 8.7 %copy-start.3 = (s32[8192]{0:T(1024)S(1)}, s32[8192]{0:T(1024)}, u32[]{:S(2)}) copy-start(s32[8192]{0:T(1024)} %param.14) | copy-start | bytes 98308
  10.6 8.7 %copy-start.4 = (s32[4]{0:T(128)S(1)}, s32[4]{0:T(128)}, u32[]{:S(2)}) copy-start(s32[4]{0:T(128)} %counts_ref.1) | copy-start | bytes 52
  18.7 33.2 %collective-permute-start.10 = (f32[3,72,512]{2,1,0:T(8,128)S(1)}, f32[3,72,512]{2,1,0:T(8,128)S(1)}, u32[]{:S(2)}, u32[]{:S(2)}) collective-permute-start(f32[3,72,512]{2,1,0:T(8,128)S(1)} %pad_maximum_fusion.refs_2_), channel_id=1, source_target_pairs={{0,1},{1,0},{2,3},{3,2},{4,5},{5,4},{6,7},{7,6},{8,9},{9,8},{10,11... | collective-permute-start | bytes 1327112 | tf_op jit(solution)/shard_map/ppermute | solution.py:221
  37.5 4.6 %collective-permute-start.4 = (f32[128,128]{1,0:T(8,128)S(1)}, f32[128,128]{1,0:T(8,128)S(1)}, u32[]{:S(2)}, u32[]{:S(2)}) collective-permute-start(f32[128,128]{1,0:T(8,128)S(1)} %get-tuple-element.10), channel_id=1, source_target_pairs={{0,8},{8,0},{16,24},{24,16},{1,9},{9,1},{17,25},{25,17},{2,10},{10... | collective-permute-start | bytes 196616 | tf_op jit(solution)/shard_map/ppermute | solution.py:221
  39.6 7.5 %collective-permute-start.5 = (f32[128,128]{1,0:T(8,128)S(1)}, f32[128,128]{1,0:T(8,128)S(1)}, u32[]{:S(2)}, u32[]{:S(2)}) collective-permute-start(f32[128,128]{1,0:T(8,128)S(1)} %get-tuple-element.11), channel_id=1, source_target_pairs={{0,16},{8,24},{16,0},{24,8},{1,17},{9,25},{17,1},{25,9},{2,18},{10... | collective-permute-start | bytes 196616 | tf_op jit(solution)/shard_map/ppermute | solution.py:221
  42.2 6.2 %collective-permute-start.6 = (f32[128,128]{1,0:T(8,128)S(1)}, f32[128,128]{1,0:T(8,128)S(1)}, u32[]{:S(2)}, u32[]{:S(2)}) collective-permute-start(f32[128,128]{1,0:T(8,128)S(1)} %get-tuple-element.12), channel_id=1, source_target_pairs={{0,24},{8,16},{16,8},{24,0},{1,25},{9,17},{17,9},{25,1},{2,26},{10... | collective-permute-start | bytes 196616 | tf_op jit(solution)/shard_map/ppermute | solution.py:221
  48.4 10.8 %copy-start.5 = (s32[256]{0:T(256)S(1)}, s32[256]{0:T(256)}, u32[]{:S(2)}) copy-start(s32[256]{0:T(256)} %param.17) | copy-start | bytes 3076
  48.4 10.4 %collective-permute-start.7 = (f32[128,128]{1,0:T(8,128)S(1)}, f32[128,128]{1,0:T(8,128)S(1)}, u32[]{:S(2)}, u32[]{:S(2)}) collective-permute-start(f32[128,128]{1,0:T(8,128)S(1)} %group_sum.1.refs_0_), channel_id=1, source_target_pairs={{0,2},{1,3},{2,0},{3,1},{4,6},{5,7},{6,4},{7,5},{8,10},{9,11},{10,... | collective-permute-start | bytes 196616 | tf_op jit(solution)/shard_map/ppermute | solution.py:221
  49.9 8.9 %collective-permute-start.8 = (f32[128,128]{1,0:T(8,128)S(1)}, f32[128,128]{1,0:T(8,128)S(1)}, u32[]{:S(2)}, u32[]{:S(2)}) collective-permute-start(f32[128,128]{1,0:T(8,128)S(1)} %group_sum.1.refs_0_), channel_id=1, source_target_pairs={{0,4},{1,5},{2,6},{3,7},{4,0},{5,1},{6,2},{7,3},{8,12},{9,13},{10,... | collective-permute-start | bytes 196616 | tf_op jit(solution)/shard_map/ppermute | solution.py:221
  51.4 7.4 %collective-permute-start.9 = (f32[128,128]{1,0:T(8,128)S(1)}, f32[128,128]{1,0:T(8,128)S(1)}, u32[]{:S(2)}, u32[]{:S(2)}) collective-permute-start(f32[128,128]{1,0:T(8,128)S(1)} %group_sum.1.refs_0_), channel_id=1, source_target_pairs={{0,6},{1,7},{2,4},{3,5},{4,2},{5,3},{6,0},{7,1},{8,14},{9,15},{10,... | collective-permute-start | bytes 196616 | tf_op jit(solution)/shard_map/ppermute | solution.py:221
  59.0 1.3 %collective-permute-start.11 = (f32[128,128]{1,0:T(8,128)S(1)}, f32[128,128]{1,0:T(8,128)S(1)}, u32[]{:S(2)}, u32[]{:S(2)}) collective-permute-start(f32[128,128]{1,0:T(8,128)S(1)} %set_coeffs.1.mine_ref), channel_id=1, source_target_pairs={{0,1},{1,0},{2,3},{3,2},{4,5},{5,4},{6,7},{7,6},{8,9},{9,8},{10,11... | collective-permute-start | bytes 196616 | tf_op jit(solution)/shard_map/ppermute | solution.py:221
where the time goes:
time: 63.5 us; the launch traced here: 63.1 us
  Pallas kernels  36.1 us (57%)
  starting transfers between devices  13.5 us (21%)
  waiting for transfers between devices  7.28 us (11%)
  local copies, waits for them, and re-layouts  3.01 us (5%)
  other arithmetic  2.42 us (4%)
  between operations  0.79 us (1%)
    pallas_call x6, Pallas kernels, run(): pl.pallas_call(kernel, out_shape=out, in_specs=specs, out_specs=jax.tree....  36.1 us
    ppermute x12, starting transfers between devices, swap(): lax.ppermute(x, axis, [(i, i ^ away) for i in range(lax.axis_size(axis))])  13.5 us
    ppermute x12, waiting for transfers between devices, swap(): lax.ppermute(x, axis, [(i, i ^ away) for i in range(lax.axis_size(axis))])  7.28 us
    unnamed x12, local copies, waits for them, and re-layouts  1.99 us
  transfers between devices with their start and end apart: 12, of which 3 were waited for; matrix products, arithmetic and copies ran while one was open for 2% of the time, Pallas kernels for 53%

commit v1 on v0

--- a/solution.py
+++ b/solution.py
@@ -19,6 +19,7 @@
 NT = (((1,), (1,)), ((), ()))
 VMEM = pl.BlockSpec(memory_space=pltpu.VMEM)
 SMEM = pl.BlockSpec(memory_space=pltpu.SMEM)
+ANY = pl.BlockSpec(memory_space=pl.ANY)
 
 
 def mm(a, b, dims=NN):
@@ -63,18 +64,30 @@
     return ref[2 * factors : 2 * factors + 1, :]
 
 
-def prepare(block_ref, states_scr, wide_scr, load_scr, factors):
+def pack_kernel(start_ref, shocks_ref, weights_ref, short_ref, whole_ref):
+    factors = start_ref.shape[0]
+    for ref in (short_ref, whole_ref):
+        ref[:factors, :] = start_ref[...]
+        ref[factors : 2 * factors, :] = shocks_ref[0]
+        ref[2 * factors : 2 * factors + PAD, :] = jnp.broadcast_to(weights_ref[...].astype(F32), (PAD, ref.shape[1]))
+    whole_ref[2 * factors + PAD :, :] = shocks_ref[1]
+
+
+def prepare(blocks, states_scr, wide_scr, load_scr, factors):
     core = lax.axis_index("path") & 1
-    first, second = states_of(block_ref, factors)
-    third = 0.8 * second + 0.6 * block_ref[2 * factors + PAD :, :]
-    hi, lo = split2(basis_rows(pick(core, first, second)) * weights_of(block_ref, factors))
-    wide_scr[...] = jnp.concatenate([hi, lo], axis=0)
-    hi, mid, low = split3(pick(core, second, third))
-    hi, mid, low = hi.astype(F32), mid.astype(F32), low.astype(F32)
-    paths = block_ref.shape[1]
-    ones = jnp.where(lax.broadcasted_iota(jnp.int32, (DEPTH - 6 * factors, paths), 0) < 3, 1.0, 0.0)
-    states_scr[...] = jnp.concatenate([hi, hi, mid, mid, hi, low, ones], axis=0).T.astype(BF16)
     load_scr[...] = jnp.zeros_like(load_scr)
+    for number, block_ref in enumerate(blocks):
+        paths = block_ref.shape[1]
+        mine = pl.ds(number * paths, paths)
+        first, second = states_of(block_ref, factors)
+        third = 0.8 * second + 0.6 * block_ref[2 * factors + PAD :, :]
+        hi, lo = split2(basis_rows(pick(core, first, second)) * weights_of(block_ref, factors))
+        wide_scr[:, mine] = jnp.concatenate([hi, lo], axis=0)
+        hi, mid, low = split3(pick(core, second, third))
+        hi, mid, low = hi.astype(F32), mid.astype(F32), low.astype(F32)
+        ones = jnp.where(lax.broadcasted_iota(jnp.int32, (DEPTH - 6 * factors, paths), 0) < 3, 1.0, 0.0)
+        stacked = jnp.concatenate([hi, hi, mid, mid, hi, low, ones], axis=0)
+        states_scr[mine, :] = stacked.T.astype(BF16)
 
 
 def path_moments(cols, load_ref, strike_ref, states_scr, wide_scr, load_scr, slot):
@@ -97,47 +110,55 @@
     return pl.ds(pl.multiple_of(index * TILE, TILE), TILE)
 
 
-def first_kernel(block_ref, load_ref, strike_ref, moment_ref, states_scr, wide_scr, load_scr):
-    prepare(block_ref, states_scr, wide_scr, load_scr, load_ref.shape[0])
-
-    def step(pair, carry):
-        for slot in range(2):
-            cols = tile_at(2 * pair + slot)
-            moment_ref[:, cols] = path_moments(cols, load_ref, strike_ref, states_scr, wide_scr, load_scr, slot)
-        return carry
-
-    lax.fori_loop(0, load_ref.shape[1] // (2 * TILE), step, 0)
-
-
-def second_kernel(groups, counts_ref, block_ref, moment_ref, load_ref, strike_ref, notional_ref, set_ref, *refs):
-    outs, (net_scr, states_scr, wide_scr, load_scr) = refs[:groups], refs[groups:]
+def copies(sources, targets, sems):
+    return [pltpu.make_async_copy(src, dst, sems.at[i]) for i, (src, dst) in enumerate(zip(sources, targets))]
+
+
+def moment_kernel(
+    groups, counts_ref, own_ref, other_ref, load_hbm, strike_hbm, notional_hbm, set_hbm, *refs
+):
+    outs = refs[:groups]
+    load_ref, strike_ref, notional_ref, set_ref, sems, net_scr, *scratch = refs[groups:]
+    moves = copies(
+        (load_hbm, strike_hbm, notional_hbm, set_hbm), (load_ref, strike_ref, notional_ref, set_ref), sems
+    )
+    for move in moves:
+        move.start()
     group = lax.axis_index("trade")
     filled = counts_ref[group]
-    sets = net_scr.shape[0]
-    owned = sets // groups
+    owned = net_scr.shape[0]
     bits = log2(owned)
-    prepare(block_ref, states_scr, wide_scr, load_scr, load_ref.shape[0])
+    rows = 16
+    prepare((own_ref, other_ref), *scratch, load_ref.shape[0])
     net_scr[...] = jnp.zeros_like(net_scr)
+    for move in moves:
+        move.wait()
 
     def step(pair, carry):
         for slot in range(2):
             index = 2 * pair + slot
             cols = tile_at(index)
-            moment = moment_ref[:, cols]
-            moment = moment + path_moments(cols, load_ref, strike_ref, states_scr, wide_scr, load_scr, slot)
+            moment = path_moments(cols, load_ref, strike_ref, *scratch, slot)
             slot_ids = index * TILE + lax.broadcasted_iota(jnp.int32, (1, TILE), 1)
             hi, lo = split2(moment * jnp.where(slot_ids < filled, notional_ref[:, cols], 0.0))
-            places = set_ref[:, cols] ^ (group << bits)
-            one_hot = lax.broadcasted_iota(jnp.int16, (sets, TILE), 0) == places.astype(jnp.int16)
-            one_hot = jnp.where(one_hot, jnp.ones((), BF16), jnp.zeros((), BF16))
-            net_scr[...] += mm(one_hot, jnp.concatenate([hi, lo], axis=0), NT)
+            both = jnp.concatenate([hi, lo], axis=0)
+            both = both.reshape(both.shape[0] // rows, rows, TILE)
+            sets = set_ref[:, cols]
+            to_group = jnp.broadcast_to((sets >> bits) ^ group, (rows, TILE))
+            parts = []
+            for away in range(groups):
+                mask = jnp.where(to_group == away, 1.0, 0.0).astype(BF16)
+                parts.append((both * mask[None]).reshape(-1, TILE))
+            one_hot = lax.broadcasted_iota(jnp.int32, (owned, TILE), 0) == (sets & (owned - 1))
+            one_hot = jnp.where(one_hot, 1.0, 0.0).astype(BF16)
+            net_scr[...] += mm(one_hot, jnp.concatenate(parts, axis=0), NT)
         return carry
 
     lax.fori_loop(0, load_ref.shape[1] // (2 * TILE), step, 0)
-    wide = net_scr.shape[1] // 2
+    wide = net_scr.shape[1] // (2 * groups)
     half = owned // 2
     for away, out in enumerate(outs):
-        net = net_scr[away * owned : (away + 1) * owned, :]
+        net = net_scr[:, 2 * wide * away : 2 * wide * (away + 1)]
         net = net[:, :wide] + net[:, wide:]
         out[...] = jnp.concatenate([net[:half], net[half:]], axis=1)
 
@@ -243,44 +264,47 @@
     owned = thresholds.shape[0]
     groups = lax.axis_size("trade")
     ranks = lax.axis_size("path")
-    sets = owned * groups
     wide = 2 * factors
     assert dates == 2
 
-    shocks_t = jnp.swapaxes(shocks, 1, 2)
-    weight_rows = jnp.broadcast_to(weights.astype(F32), (PAD, paths))
-    short = jnp.concatenate([start_state.T, shocks_t[0], weight_rows], axis=0)
-    whole = jnp.concatenate([start_state.T, shocks_t[0], weight_rows, shocks_t[1]], axis=0)
+    shape = jax.ShapeDtypeStruct
+    short, whole = run(
+        pack_kernel, "pack_states",
+        [shape(((dates - 1) * factors + factors + PAD, paths), F32), shape(((dates + 1) * factors + PAD, paths), F32)],
+        [VMEM] * 3, (start_state.T, jnp.swapaxes(shocks, 1, 2), weights[None, :]), 58,
+    )
     other = swap(whole, "path", 1)
-    across = jnp.stack([swap(short, "path", 2 * away) for away in range(1, ranks // 2)])
-
-    shape = jax.ShapeDtypeStruct
-    scratch = [
-        pltpu.VMEM((paths, DEPTH), BF16),
-        pltpu.VMEM((2 * wide, paths), BF16),
-        pltpu.VMEM((2, DEPTH, TILE), BF16),
-    ]
+    across = [swap(short, "path", 2 * away) for away in range(1, ranks // 2)]
+
     strike_row, notional_row, set_row = strikes[None, :], notionals[None, :], trade_set[None, :]
-    moment = run(
-        first_kernel, "own_path_moments", shape((wide, slots), F32), [VMEM] * 3,
-        (whole, loadings, strike_row), 48, scratch, 8.0,
-    )
-    other, across = lax.optimization_barrier((other, across))
-    others = swap(across, "path", 1)
     nets = run(
-        functools.partial(second_kernel, groups), "other_path_moments",
-        [shape((owned // 2, 2 * wide), F32)] * groups, [SMEM] + [VMEM] * 6,
-        (live_counts, other, moment, loadings, strike_row, notional_row, set_row), 48,
-        [pltpu.VMEM((sets, 2 * wide), F32)] + scratch, 12.0,
-    )
+        functools.partial(moment_kernel, groups), "net_moments",
+        [shape((owned // 2, 2 * wide), F32)] * groups, [SMEM, VMEM, VMEM] + [ANY] * 4,
+        (live_counts, whole, other, loadings, strike_row, notional_row, set_row), 56,
+        [
+            pltpu.VMEM((factors, slots), F32),
+            pltpu.VMEM((1, slots), F32),
+            pltpu.VMEM((1, slots), F32),
+            pltpu.VMEM((1, slots), jnp.int32),
+            pltpu.SemaphoreType.DMA((4,)),
+            pltpu.VMEM((owned, 2 * wide * groups), F32),
+            pltpu.VMEM((2 * paths, DEPTH), BF16),
+            pltpu.VMEM((2 * wide, 2 * paths), BF16),
+            pltpu.VMEM((2, DEPTH, TILE), BF16),
+        ],
+        20.0,
+    )
+    *across, net = lax.optimization_barrier((*across, nets[0]))
+    others = swap(jnp.stack(across), "path", 1)
     got = [swap(nets[away], "trade", away) for away in range(1, groups)]
-    blocks = (whole, other, across, others)
+    blocks = (whole, other, *across, others)
     inverse = run(
         functools.partial(inverse_kernel, factors), "gram_inverse", shape((2 * wide, 2 * wide), F32),
-        [VMEM] * 4, blocks, 8, (), 6.0,
-    )
+        [VMEM] * len(blocks), blocks, 8, (), 6.0,
+    )
+    inverse, net = lax.optimization_barrier((inverse, net))
     part = run(
-        sum_kernel, "group_sum", shape((owned // 2, 2 * wide), F32), [VMEM] * groups, [nets[0]] + got, 4
+        sum_kernel, "group_sum", shape((owned // 2, 2 * wide), F32), [VMEM] * groups, [net] + got, 4
     )
     got = [swap(part, "path", 2 * away) for away in range(1, ranks // 2)]
     mine = run(
@@ -290,7 +314,7 @@
     partner = swap(mine, "path", 1)
     exposure, expected = run(
         functools.partial(exposure_kernel, factors), "set_exposure",
-        (shape((dates, owned, paths), F32), shape((dates, owned), F32)), [VMEM] * 7,
+        (shape((dates, owned, paths), F32), shape((dates, owned), F32)), [VMEM] * (3 + len(blocks)),
         (mine, partner, thresholds[:, None], *blocks), 16, (), 2.0,
     )
     return (exposure, expected)

time: 63.5 us -> 51.8 us (0.82)
  Pallas kernels: 36.1 us -> 31.3 us
  waiting for transfers between devices: 7.28 us -> 4.47 us
  other arithmetic: 2.42 us -> 0.03 us
  local copies, waits for them, and re-layouts: 3.01 us -> 2.1 us
  starting transfers between devices: 13.5 us -> 12.8 us
    pallas_call x6, Pallas kernels: 36.1 us -> 31.3 us  [run(): pl.pallas_call(kernel, out_shape=out, in_specs=specs, out_specs=jax.tree....]
    ppermute x12, waiting for transfers between devices: 7.28 us -> 4.47 us  [swap(): lax.ppermute(x, axis, [(i, i ^ away) for i in range(lax.axis_size(axis))])]
    concatenate x2 -> x0, other arithmetic: 1.7 us -> none  [the longest x1 0.85 us: body(): jnp.concatenate([start_state.T, shocks_t[0], weight_rows, shocks_t[1]], a...]
    squeeze x1 -> x0, local copies, waits for them, and re-layouts: 0.88 us -> none  [body(): shocks_t[0]]
    ppermute x12, starting transfers between devices: 13.5 us -> 12.8 us  [swap(): lax.ppermute(x, axis, [(i, i ^ away) for i in range(lax.axis_size(axis))])]
    convert_element_type x1 -> x0, other arithmetic: 0.69 us -> none  [body(): weight_rows = jnp.broadcast_to(weights.astype(F32), (PAD, paths))]
    unnamed x12 -> x16, local copies, waits for them, and re-layouts: 1.99 us -> 1.97 us
  transfers between devices with their start and end apart: 12 -> 12, of which waited for: 3 -> 4; matrix products, arithmetic and copies ran while one was open for 2% -> 0% of each run, Pallas kernels for 53% -> 52%
where the time goes in v1:
time: 51.8 us; the launch traced here: 51.6 us
  Pallas kernels  31.3 us (60%)
  starting transfers between devices  12.8 us (25%)
  waiting for transfers between devices  4.47 us (9%)
  local copies, waits for them, and re-layouts  2.1 us (4%)
  between operations  0.82 us (2%)
    pallas_call x6, Pallas kernels, run(): pl.pallas_call(kernel, out_shape=out, in_specs=specs, out_specs=jax.tree....  31.3 us
    ppermute x12, starting transfers between devices, swap(): lax.ppermute(x, axis, [(i, i ^ away) for i in range(lax.axis_size(axis))])  12.8 us
    ppermute x12, waiting for transfers between devices, swap(): lax.ppermute(x, axis, [(i, i ^ away) for i in range(lax.axis_size(axis))])  4.47 us
    unnamed x16, local copies, waits for them, and re-layouts  1.97 us
  transfers between devices with their start and end apart: 12, of which 4 were waited for; matrix products, arithmetic and copies ran while one was open for 0% of the time, Pallas kernels for 52%

profile of v1, /device:TPU:0, one launch (start us, length us, event | category | flops | bytes accessed | tf_op | source)
XLA Modules:
  0.0 51.6 jit_solution(14163019822513816269)
XLA Ops:
  0.6 1.7 %pack_states.1 = (f32[72,512]{1,0:T(8,128)}, f32[104,512]{1,0:T(8,128)}) custom-call(f32[32,512]{1,0:T(8,128)} %bitcast.14, f32[2,32,512]{2,1,0:T(8,128)} %bitcast.13, s32[1,512]{1,0:T(1,128)} %bitcast.15), custom_call_target="tpu_custom_call" | custom-call | bytes 100000 | tf_op jit(solution)/shard_map/pack_states/pallas_call | solution.py:246
  2.3 0.5 collective-permute-start
  2.7 3.4 %collective-permute-start.3 = (f32[72,512]{1,0:T(8,128)}, f32[72,512]{1,0:T(8,128)S(1)}, u32[]{:S(2)}, u32[]{:S(2)}) collective-permute-start(f32[72,512]{1,0:T(8,128)} %get-tuple-element.15), channel_id=1, source_target_pairs={{0,6},{1,7},{2,4},{3,5},{4,2},{5,3},{6,0},{7,1},{8,14},{9,15},{10,... | collective-permute-start | bytes 442376 | tf_op jit(solution)/shard_map/ppermute | solution.py:242
  6.2 0.5 collective-permute-start.2
  6.7 0.1 collective-permute-start.1
  6.8 0.0 collective-permute-done.other_ref.refs_1_
  6.8 0.0 copy-start.2
  6.8 0.7 %copy-done.2 = f32[104,512]{1,0:T(8,128)} copy-done((f32[104,512]{1,0:T(8,128)}, f32[104,512]{1,0:T(8,128)S(1)}, u32[]{:S(2)}) %copy-start.2) | copy-done | bytes 213016
  7.5 19.8 %net_moments.1 = (f32[128,128]{1,0:T(8,128)}, f32[128,128]{1,0:T(8,128)}, f32[128,128]{1,0:T(8,128)}, f32[128,128]{1,0:T(8,128)}) custom-call(s32[4]{0:T(128)} %counts_ref.1, f32[104,512]{1,0:T(8,128)} %get-tuple-element.14.own_ref.refs_0_, f32[104,512]{1,0:T(8,128)} %copy-done.2, f32[32,8192]{1,0:T(8,128)} %load_hbm.1, f32[1,8192]{1,0:T(1,128)} %bitcast.17, ...), custom_call_target="tpu_custom_call" | custom-call | flops 20000000000 | bytes 100000 | tf_op jit(solution)/shard_map/net_moments/pallas_call | solution.py:246
  27.3 0.0 collective-permute-done.3.refs_4_
  27.3 0.0 collective-permute-done.2.refs_3_
  27.4 0.0 collective-permute-done.1.refs_2_
  27.4 0.0 copy-start.7
  27.4 0.0 copy-start.6
  27.4 0.0 copy-start.5
  27.4 0.0 copy-start.1
  27.4 0.0 copy-start.3
  27.5 0.1 collective-permute-start.4
  27.5 0.7 %copy-done.7 = f32[128,128]{1,0:T(8,128)S(1)} copy-done((f32[128,128]{1,0:T(8,128)S(1)}, f32[128,128]{1,0:T(8,128)}, u32[]{:S(2)}) %copy-start.7) | copy-done | bytes 65560
  28.2 2.0 %collective-permute-start.5 = (f32[128,128]{1,0:T(8,128)S(1)}, f32[128,128]{1,0:T(8,128)S(1)}, u32[]{:S(2)}, u32[]{:S(2)}) collective-permute-start(f32[128,128]{1,0:T(8,128)S(1)} %copy-done.7), channel_id=1, source_target_pairs={{0,8},{8,0},{16,24},{24,16},{1,9},{9,1},{17,25},{25,17},{2,10},{10... | collective-permute-start | bytes 196616 | tf_op jit(solution)/shard_map/ppermute | solution.py:242
  30.2 0.0 copy-done.6
  30.2 2.6 %collective-permute-start.6 = (f32[128,128]{1,0:T(8,128)S(1)}, f32[128,128]{1,0:T(8,128)S(1)}, u32[]{:S(2)}, u32[]{:S(2)}) collective-permute-start(f32[128,128]{1,0:T(8,128)S(1)} %copy-done.6), channel_id=1, source_target_pairs={{0,16},{8,24},{16,0},{24,8},{1,17},{9,25},{17,1},{25,9},{2,18},{10... | collective-permute-start | bytes 196616 | tf_op jit(solution)/shard_map/ppermute | solution.py:242
  32.8 0.0 copy-done.5
  32.8 0.0 copy-start
  32.8 0.0 collective-permute-start.7
  32.8 0.0 collective-permute-done.4.refs_5_
  32.8 0.0 copy-done.1
  32.8 0.0 copy-done.3
  32.8 6.9 %gram_inverse.1.refs_4_ = f32[128,128]{1,0:T(8,128)S(1)} custom-call(f32[104,512]{1,0:T(8,128)S(1)} %copy-done.1, f32[104,512]{1,0:T(8,128)S(1)} %copy-done.3, f32[72,512]{1,0:T(8,128)S(1)} %collective-permute-done.1.refs_2_, f32[72,512]{1,0:T(8,128)S(1)} %collective-permute-done.2.refs_3_, f32[72,512]{1,0:T(8,128)S(1)} %collective-permute-done.3.refs_4_, ...), custom_call_target="tpu_custom_call" | custom-call | flops 6000000000 | bytes 100000 | tf_op jit(solution)/shard_map/gram_inverse/pallas_call | solution.py:246
  39.7 0.0 collective-permute-done.5.refs_1_
  39.7 0.0 collective-permute-done.6.refs_2_
  39.7 0.0 collective-permute-done.7.refs_3_
  39.7 0.0 copy-done
  39.8 2.7 %collective-permute-start.10 = (f32[128,128]{1,0:T(8,128)S(1)}, f32[128,128]{1,0:T(8,128)S(1)}, u32[]{:S(2)}, u32[]{:S(2)}) collective-permute-start(f32[128,128]{1,0:T(8,128)S(1)} %group_sum.1.refs_0_), channel_id=1, source_target_pairs={{0,6},{1,7},{2,4},{3,5},{4,2},{5,3},{6,0},{7,1},{8,14},{9,15},{10,... | collective-permute-start | bytes 196616 | tf_op jit(solution)/shard_map/ppermute | solution.py:242
  42.5 0.5 %collective-permute-start.9 = (f32[128,128]{1,0:T(8,128)S(1)}, f32[128,128]{1,0:T(8,128)S(1)}, u32[]{:S(2)}, u32[]{:S(2)}) collective-permute-start(f32[128,128]{1,0:T(8,128)S(1)} %group_sum.1.refs_0_), channel_id=1, source_target_pairs={{0,4},{1,5},{2,6},{3,7},{4,0},{5,1},{6,2},{7,3},{8,12},{9,13},{10,... | collective-permute-start | bytes 196616 | tf_op jit(solution)/shard_map/ppermute | solution.py:242
  43.0 0.3 collective-permute-start.8
  43.3 1.8 %collective-permute-done.10.refs_3_ = f32[128,128]{1,0:T(8,128)S(1)} collective-permute-done((f32[128,128]{1,0:T(8,128)S(1)}, f32[128,128]{1,0:T(8,128)S(1)}, u32[]{:S(2)}, u32[]{:S(2)}) %collective-permute-start.10) | collective-permute-done | bytes 65568 | tf_op jit(solution)/shard_map/ppermute | solution.py:242
  45.1 1.6 %collective-permute-done.9.refs_2_ = f32[128,128]{1,0:T(8,128)S(1)} collective-permute-done((f32[128,128]{1,0:T(8,128)S(1)}, f32[128,128]{1,0:T(8,128)S(1)}, u32[]{:S(2)}, u32[]{:S(2)}) %collective-permute-start.9) | collective-permute-done | bytes 65568 | tf_op jit(solution)/shard_map/ppermute | solution.py:242
  46.7 0.5 %collective-permute-done.8.refs_1_ = f32[128,128]{1,0:T(8,128)S(1)} collective-permute-done((f32[128,128]{1,0:T(8,128)S(1)}, f32[128,128]{1,0:T(8,128)S(1)}, u32[]{:S(2)}, u32[]{:S(2)}) %collective-permute-start.8) | collective-permute-done | bytes 65568 | tf_op jit(solution)/shard_map/ppermute | solution.py:242
  47.2 0.2 set_coeffs.1.mine_ref
  47.5 0.0 copy-start.4
  47.5 0.1 collective-permute-start.11
  47.5 0.6 %copy-done.4 = s32[256]{0:T(256)S(1)} copy-done((s32[256]{0:T(256)S(1)}, s32[256]{0:T(256)}, u32[]{:S(2)}) %copy-start.4) | copy-done | bytes 1048
  48.1 0.1 copy.11.limits_ref
  48.3 0.5 collective-permute-done.11.other_ref
  48.8 2.8 %set_exposure.1 = (f32[2,256,512]{2,1,0:T(8,128)}, f32[2,256]{1,0:T(2,128)}) custom-call(f32[128,128]{1,0:T(8,128)S(1)} %set_coeffs.1.mine_ref, f32[128,128]{1,0:T(8,128)S(1)} %collective-permute-done.11.other_ref, s32[256,1]{1,0:T(8,128)S(1)} %copy.11.limits_ref, f32[104,512]{1,0:T(8,128)S(1)} %copy-done.1, f32[104,512]{1,0:T(8,128)S(1)} %copy-done.3, ...), custom_call_target="tpu_custom_call" | custom-call | flops 2000000000 | bytes 100000 | tf_op jit(solution)/shard_map/set_exposure/pallas_call | solution.py:246
  (2 shorter events, 0.0 us)
Async XLA Ops:
  2.3 4.5 %collective-permute-start = (f32[104,512]{1,0:T(8,128)}, f32[104,512]{1,0:T(8,128)S(1)}, u32[]{:S(2)}, u32[]{:S(2)}) collective-permute-start(f32[104,512]{1,0:T(8,128)} %get-tuple-element.14.own_ref.refs_0_), channel_id=1, source_target_pairs={{0,1},{1,0},{2,3},{3,2},{4,5},{5,4},{6,7},{7,6},{8,9},{9,8},{10,11... | collective-permute-start | bytes 638984 | tf_op jit(solution)/shard_map/ppermute | solution.py:242
  2.7 24.6 %collective-permute-start.3 = (f32[72,512]{1,0:T(8,128)}, f32[72,512]{1,0:T(8,128)S(1)}, u32[]{:S(2)}, u32[]{:S(2)}) collective-permute-start(f32[72,512]{1,0:T(8,128)} %get-tuple-element.15), channel_id=1, source_target_pairs={{0,6},{1,7},{2,4},{3,5},{4,2},{5,3},{6,0},{7,1},{8,14},{9,15},{10,... | collective-permute-start | bytes 442376 | tf_op jit(solution)/shard_map/ppermute | solution.py:242
  6.2 21.2 %collective-permute-start.2 = (f32[72,512]{1,0:T(8,128)}, f32[72,512]{1,0:T(8,128)S(1)}, u32[]{:S(2)}, u32[]{:S(2)}) collective-permute-start(f32[72,512]{1,0:T(8,128)} %get-tuple-element.15), channel_id=1, source_target_pairs={{0,4},{1,5},{2,6},{3,7},{4,0},{5,1},{6,2},{7,3},{8,12},{9,13},{10,... | collective-permute-start | bytes 442376 | tf_op jit(solution)/shard_map/ppermute | solution.py:242
  6.7 20.7 %collective-permute-start.1 = (f32[72,512]{1,0:T(8,128)}, f32[72,512]{1,0:T(8,128)S(1)}, u32[]{:S(2)}, u32[]{:S(2)}) collective-permute-start(f32[72,512]{1,0:T(8,128)} %get-tuple-element.15), channel_id=1, source_target_pairs={{0,2},{1,3},{2,0},{3,1},{4,6},{5,7},{6,4},{7,5},{8,10},{9,11},{10,... | collective-permute-start | bytes 442376 | tf_op jit(solution)/shard_map/ppermute | solution.py:242
  6.8 0.7 %copy-start.2 = (f32[104,512]{1,0:T(8,128)}, f32[104,512]{1,0:T(8,128)S(1)}, u32[]{:S(2)}) copy-start(f32[104,512]{1,0:T(8,128)S(1)} %collective-permute-done.other_ref.refs_1_) | copy-start | bytes 638980
  27.4 0.8 %copy-start.7 = (f32[128,128]{1,0:T(8,128)S(1)}, f32[128,128]{1,0:T(8,128)}, u32[]{:S(2)}) copy-start(f32[128,128]{1,0:T(8,128)} %get-tuple-element.22) | copy-start | bytes 196612
  27.4 2.8 %copy-start.6 = (f32[128,128]{1,0:T(8,128)S(1)}, f32[128,128]{1,0:T(8,128)}, u32[]{:S(2)}) copy-start(f32[128,128]{1,0:T(8,128)} %get-tuple-element.23) | copy-start | bytes 196612
  27.4 5.4 %copy-start.5 = (f32[128,128]{1,0:T(8,128)S(1)}, f32[128,128]{1,0:T(8,128)}, u32[]{:S(2)}) copy-start(f32[128,128]{1,0:T(8,128)} %get-tuple-element.24) | copy-start | bytes 196612
  27.4 5.4 %copy-start.1 = (f32[104,512]{1,0:T(8,128)S(1)}, f32[104,512]{1,0:T(8,128)}, u32[]{:S(2)}) copy-start(f32[104,512]{1,0:T(8,128)} %get-tuple-element.14.own_ref.refs_0_) | copy-start | bytes 638980
  27.4 5.4 %copy-start.3 = (f32[104,512]{1,0:T(8,128)S(1)}, f32[104,512]{1,0:T(8,128)}, u32[]{:S(2)}) copy-start(f32[104,512]{1,0:T(8,128)} %copy-done.2) | copy-start | bytes 638980
  27.5 5.3 %collective-permute-start.4 = (f32[3,72,512]{2,1,0:T(8,128)S(1)}, f32[3,72,512]{2,1,0:T(8,128)S(1)}, u32[]{:S(2)}, u32[]{:S(2)}) collective-permute-start(f32[3,72,512]{2,1,0:T(8,128)S(1)} %pad_maximum_fusion), channel_id=1, source_target_pairs={{0,1},{1,0},{2,3},{3,2},{4,5},{5,4},{6,7},{7,6},{8,9},{9,8},{10,11... | collective-permute-start | bytes 1327112 | tf_op jit(solution)/shard_map/ppermute | solution.py:242
  28.2 11.5 %collective-permute-start.5 = (f32[128,128]{1,0:T(8,128)S(1)}, f32[128,128]{1,0:T(8,128)S(1)}, u32[]{:S(2)}, u32[]{:S(2)}) collective-permute-start(f32[128,128]{1,0:T(8,128)S(1)} %copy-done.7), channel_id=1, source_target_pairs={{0,8},{8,0},{16,24},{24,16},{1,9},{9,1},{17,25},{25,17},{2,10},{10... | collective-permute-start | bytes 196616 | tf_op jit(solution)/shard_map/ppermute | solution.py:242
  30.2 9.5 %collective-permute-start.6 = (f32[128,128]{1,0:T(8,128)S(1)}, f32[128,128]{1,0:T(8,128)S(1)}, u32[]{:S(2)}, u32[]{:S(2)}) collective-permute-start(f32[128,128]{1,0:T(8,128)S(1)} %copy-done.6), channel_id=1, source_target_pairs={{0,16},{8,24},{16,0},{24,8},{1,17},{9,25},{17,1},{25,9},{2,18},{10... | collective-permute-start | bytes 196616 | tf_op jit(solution)/shard_map/ppermute | solution.py:242
  32.8 6.9 %copy-start = (f32[128,128]{1,0:T(8,128)S(1)}, f32[128,128]{1,0:T(8,128)}, u32[]{:S(2)}) copy-start(f32[128,128]{1,0:T(8,128)} %get-tuple-element.21.refs_0_) | copy-start | bytes 196612
  32.8 6.9 %collective-permute-start.7 = (f32[128,128]{1,0:T(8,128)S(1)}, f32[128,128]{1,0:T(8,128)S(1)}, u32[]{:S(2)}, u32[]{:S(2)}) collective-permute-start(f32[128,128]{1,0:T(8,128)S(1)} %copy-done.5), channel_id=1, source_target_pairs={{0,24},{8,16},{16,8},{24,0},{1,25},{9,17},{17,9},{25,1},{2,26},{10... | collective-permute-start | bytes 196616 | tf_op jit(solution)/shard_map/ppermute | solution.py:242
  39.8 5.3 %collective-permute-start.10 = (f32[128,128]{1,0:T(8,128)S(1)}, f32[128,128]{1,0:T(8,128)S(1)}, u32[]{:S(2)}, u32[]{:S(2)}) collective-permute-start(f32[128,128]{1,0:T(8,128)S(1)} %group_sum.1.refs_0_), channel_id=1, source_target_pairs={{0,6},{1,7},{2,4},{3,5},{4,2},{5,3},{6,0},{7,1},{8,14},{9,15},{10,... | collective-permute-start | bytes 196616 | tf_op jit(solution)/shard_map/ppermute | solution.py:242
  42.5 4.3 %collective-permute-start.9 = (f32[128,128]{1,0:T(8,128)S(1)}, f32[128,128]{1,0:T(8,128)S(1)}, u32[]{:S(2)}, u32[]{:S(2)}) collective-permute-start(f32[128,128]{1,0:T(8,128)S(1)} %group_sum.1.refs_0_), channel_id=1, source_target_pairs={{0,4},{1,5},{2,6},{3,7},{4,0},{5,1},{6,2},{7,3},{8,12},{9,13},{10,... | collective-permute-start | bytes 196616 | tf_op jit(solution)/shard_map/ppermute | solution.py:242
  43.0 4.3 %collective-permute-start.8 = (f32[128,128]{1,0:T(8,128)S(1)}, f32[128,128]{1,0:T(8,128)S(1)}, u32[]{:S(2)}, u32[]{:S(2)}) collective-permute-start(f32[128,128]{1,0:T(8,128)S(1)} %group_sum.1.refs_0_), channel_id=1, source_target_pairs={{0,2},{1,3},{2,0},{3,1},{4,6},{5,7},{6,4},{7,5},{8,10},{9,11},{10,... | collective-permute-start | bytes 196616 | tf_op jit(solution)/shard_map/ppermute | solution.py:242
  47.5 0.7 %copy-start.4 = (s32[256]{0:T(256)S(1)}, s32[256]{0:T(256)}, u32[]{:S(2)}) copy-start(s32[256]{0:T(256)} %param.17) | copy-start | bytes 3076
  47.5 1.3 %collective-permute-start.11 = (f32[128,128]{1,0:T(8,128)S(1)}, f32[128,128]{1,0:T(8,128)S(1)}, u32[]{:S(2)}, u32[]{:S(2)}) collective-permute-start(f32[128,128]{1,0:T(8,128)S(1)} %set_coeffs.1.mine_ref), channel_id=1, source_target_pairs={{0,1},{1,0},{2,3},{3,2},{4,5},{5,4},{6,7},{7,6},{8,9},{9,8},{10,11... | collective-permute-start | bytes 196616 | tf_op jit(solution)/shard_map/ppermute | solution.py:242

commit v2 on v1

--- a/solution.py
+++ b/solution.py
@@ -12,6 +12,8 @@
 F32 = jnp.float32
 BF16 = jnp.bfloat16
 TILE = 512
+CHUNK = 512
+SLOTS = 2
 DEPTH = 256
 PAD = 8
 MIB = 1024 * 1024
@@ -90,9 +92,8 @@
         states_scr[mine, :] = stacked.T.astype(BF16)
 
 
-def path_moments(cols, load_ref, strike_ref, states_scr, wide_scr, load_scr, slot):
+def load_rows(cols, load_ref, strike_ref, load_scr, slot):
     factors = load_ref.shape[0]
-    wide = 2 * factors
     hi, mid, low = split3(load_ref[:, cols])
     for part, piece in enumerate((hi, mid, hi, mid, low, hi)):
         load_scr[slot, pl.ds(part * factors, factors), :] = piece
@@ -101,9 +102,13 @@
     strike_rows = jnp.where(rows == 1, s_mid.astype(F32), jnp.where(rows == 2, s_low.astype(F32), 0.0))
     strike_rows = jnp.where(rows == 0, s_hi.astype(F32), strike_rows)
     load_scr[slot, pl.ds(6 * factors, 16), :] = strike_rows.astype(BF16)
-    hi, lo = split2(jnp.maximum(mm(states_scr[...], load_scr[slot]), 0.0))
-    both = mm(wide_scr[...], hi)
-    return both[:wide] + both[wide:] + mm(wide_scr[:wide], lo)
+
+
+def chunk_moments(pay, rows, wide_scr):
+    wide = wide_scr.shape[0] // 2
+    hi, lo = split2(jnp.maximum(pay, 0.0))
+    both = mm(wide_scr[:, rows], hi)
+    return both[:wide] + (both[wide:] + mm(wide_scr[:wide, rows], lo))
 
 
 def tile_at(index):
@@ -134,27 +139,44 @@
     for move in moves:
         move.wait()
 
-    def step(pair, carry):
-        for slot in range(2):
-            index = 2 * pair + slot
-            cols = tile_at(index)
-            moment = path_moments(cols, load_ref, strike_ref, *scratch, slot)
-            slot_ids = index * TILE + lax.broadcasted_iota(jnp.int32, (1, TILE), 1)
-            hi, lo = split2(moment * jnp.where(slot_ids < filled, notional_ref[:, cols], 0.0))
-            both = jnp.concatenate([hi, lo], axis=0)
-            both = both.reshape(both.shape[0] // rows, rows, TILE)
-            sets = set_ref[:, cols]
-            to_group = jnp.broadcast_to((sets >> bits) ^ group, (rows, TILE))
-            parts = []
-            for away in range(groups):
-                mask = jnp.where(to_group == away, 1.0, 0.0).astype(BF16)
-                parts.append((both * mask[None]).reshape(-1, TILE))
-            one_hot = lax.broadcasted_iota(jnp.int32, (owned, TILE), 0) == (sets & (owned - 1))
-            one_hot = jnp.where(one_hot, 1.0, 0.0).astype(BF16)
-            net_scr[...] += mm(one_hot, jnp.concatenate(parts, axis=0), NT)
+    states_scr, wide_scr, load_scr = scratch
+    chunks = [pl.ds(start, CHUNK) for start in range(0, states_scr.shape[0], CHUNK)]
+
+    def add_tile(index, moment):
+        cols = tile_at(index)
+        slot_ids = index * TILE + lax.broadcasted_iota(jnp.int32, (1, TILE), 1)
+        hi, lo = split2(moment * jnp.where(slot_ids < filled, notional_ref[:, cols], 0.0))
+        both = jnp.concatenate([hi, lo], axis=0)
+        both = both.reshape(both.shape[0] // rows, rows, TILE)
+        sets = set_ref[:, cols]
+        to_group = jnp.broadcast_to((sets >> bits) ^ group, (rows, TILE))
+        parts = []
+        for away in range(groups):
+            mask = jnp.where(to_group == away, 1.0, 0.0).astype(BF16)
+            parts.append((both * mask[None]).reshape(-1, TILE))
+        one_hot = lax.broadcasted_iota(jnp.int32, (owned, TILE), 0) == (sets & (owned - 1))
+        one_hot = jnp.where(one_hot, 1.0, 0.0).astype(BF16)
+        net_scr[...] += mm(one_hot, jnp.concatenate(parts, axis=0), NT)
+
+    def step(turn, carry):
+        stages = [(slot, chunk) for slot in range(SLOTS) for chunk in chunks]
+        pays, moment = {}, None
+        for number in range(len(stages) + 1):
+            if number < len(stages):
+                slot, chunk = stages[number]
+                if number % len(chunks) == 0:
+                    load_rows(tile_at(SLOTS * turn + slot), load_ref, strike_ref, load_scr, slot)
+                pays[number] = mm(states_scr[chunk, :], load_scr[slot])
+            if number > 0:
+                slot, chunk = stages[number - 1]
+                part = chunk_moments(pays.pop(number - 1), chunk, wide_scr)
+                moment = part if moment is None else moment + part
+                if number % len(chunks) == 0:
+                    add_tile(SLOTS * turn + slot, moment)
+                    moment = None
         return carry
 
-    lax.fori_loop(0, load_ref.shape[1] // (2 * TILE), step, 0)
+    lax.fori_loop(0, load_ref.shape[1] // (SLOTS * TILE), step, 0)
     wide = net_scr.shape[1] // (2 * groups)
     half = owned // 2
     for away, out in enumerate(outs):
@@ -249,7 +271,7 @@
         in_specs=specs,
         out_specs=jax.tree.map(lambda _: VMEM, out),
         scratch_shapes=list(scratch),
-        compiler_params=pltpu.CompilerParams(vmem_limit_bytes=mib * MIB),
+        compiler_params=pltpu.CompilerParams(vmem_limit_bytes=int(mib * MIB)),
         cost_estimate=pl.CostEstimate(flops=int(gflops * 1e9), bytes_accessed=10**5, transcendentals=0),
         name=name,
     )(*args)
@@ -280,7 +302,7 @@
     nets = run(
         functools.partial(moment_kernel, groups), "net_moments",
         [shape((owned // 2, 2 * wide), F32)] * groups, [SMEM, VMEM, VMEM] + [ANY] * 4,
-        (live_counts, whole, other, loadings, strike_row, notional_row, set_row), 56,
+        (live_counts, whole, other, loadings, strike_row, notional_row, set_row), 52.75,
         [
             pltpu.VMEM((factors, slots), F32),
             pltpu.VMEM((1, slots), F32),
@@ -290,7 +312,7 @@
             pltpu.VMEM((owned, 2 * wide * groups), F32),
             pltpu.VMEM((2 * paths, DEPTH), BF16),
             pltpu.VMEM((2 * wide, 2 * paths), BF16),
-            pltpu.VMEM((2, DEPTH, TILE), BF16),
+            pltpu.VMEM((SLOTS, DEPTH, TILE), BF16),
         ],
         20.0,
     )

time: 51.8 us -> 50.9 us (0.983)
  Pallas kernels: 31.3 us -> 30.2 us
    pallas_call x6, Pallas kernels: 31.3 us -> 30.2 us  [run(): pl.pallas_call(kernel, out_shape=out, in_specs=specs, out_specs=jax.tree....]
    unnamed x16 -> x14, local copies, waits for them, and re-layouts: 1.97 us -> 2.18 us
  transfers between devices with their start and end apart: 12 -> 12, of which waited for: 4 -> 4; matrix products, arithmetic and copies ran while one was open for 0% -> 0% of each run, Pallas kernels for 52% -> 50%
where the time goes in v2:
time: 50.9 us; the launch traced here: 50.6 us
  Pallas kernels  30.2 us (59%)
  starting transfers between devices  12.9 us (25%)
  waiting for transfers between devices  4.49 us (9%)
  local copies, waits for them, and re-layouts  2.32 us (5%)
  between operations  0.8 us (2%)
    pallas_call x6, Pallas kernels, run(): pl.pallas_call(kernel, out_shape=out, in_specs=specs, out_specs=jax.tree....  30.2 us
    ppermute x12, starting transfers between devices, swap(): lax.ppermute(x, axis, [(i, i ^ away) for i in range(lax.axis_size(axis))])  12.9 us
    ppermute x12, waiting for transfers between devices, swap(): lax.ppermute(x, axis, [(i, i ^ away) for i in range(lax.axis_size(axis))])  4.49 us
    unnamed x14, local copies, waits for them, and re-layouts  2.18 us
  transfers between devices with their start and end apart: 12, of which 4 were waited for; matrix products, arithmetic and copies ran while one was open for 0% of the time, Pallas kernels for 50%

profile of v2, /device:TPU:0, one launch (start us, length us, event | category | flops | bytes accessed | tf_op | source)
XLA Modules:
  0.0 50.6 jit_solution(11402896588414929484)
XLA Ops:
  0.6 0.0 copy-start.2
  0.6 0.0 copy-start.3
  0.7 0.0 copy-start.4
  0.7 1.7 %pack_states.1 = (f32[72,512]{1,0:T(8,128)}, f32[104,512]{1,0:T(8,128)}) custom-call(f32[32,512]{1,0:T(8,128)} %bitcast.17, f32[2,32,512]{2,1,0:T(8,128)} %bitcast.16, s32[1,512]{1,0:T(1,128)} %bitcast.18), custom_call_target="tpu_custom_call" | custom-call | bytes 100000 | tf_op jit(solution)/shard_map/pack_states/pallas_call | solution.py:268
  2.3 0.5 collective-permute-start
  2.8 3.4 %collective-permute-start.3 = (f32[72,512]{1,0:T(8,128)}, f32[72,512]{1,0:T(8,128)S(1)}, u32[]{:S(2)}, u32[]{:S(2)}) collective-permute-start(f32[72,512]{1,0:T(8,128)} %get-tuple-element.15), channel_id=1, source_target_pairs={{0,6},{1,7},{2,4},{3,5},{4,2},{5,3},{6,0},{7,1},{8,14},{9,15},{10,... | collective-permute-start | bytes 442376 | tf_op jit(solution)/shard_map/ppermute | solution.py:264
  6.2 0.5 collective-permute-start.2
  6.7 0.1 collective-permute-start.1
  6.9 0.0 collective-permute-done.other_ref.refs_1_
  6.9 0.0 copy-start.5
  6.9 0.0 copy-done.2
  6.9 0.0 copy-done.3
  6.9 0.0 copy-done.4
  6.9 0.6 %copy-done.5 = s32[4]{0:T(128)S(1)} copy-done((s32[4]{0:T(128)S(1)}, s32[4]{0:T(128)}, u32[]{:S(2)}) %copy-start.5) | copy-done | bytes 40
  7.5 0.0 copy-start
  7.5 0.9 %copy-done = f32[104,512]{1,0:T(8,128)S(1)} copy-done((f32[104,512]{1,0:T(8,128)S(1)}, f32[104,512]{1,0:T(8,128)}, u32[]{:S(2)}) %copy-start) | copy-done | bytes 213016
  8.5 18.6 %net_moments.1 = (f32[128,128]{1,0:T(8,128)S(1)}, f32[128,128]{1,0:T(8,128)S(1)}, f32[128,128]{1,0:T(8,128)S(1)}, f32[128,128]{1,0:T(8,128)S(1)}) custom-call(s32[4]{0:T(128)S(1)} %copy-done.5, f32[104,512]{1,0:T(8,128)S(1)} %copy-done, f32[104,512]{1,0:T(8,128)S(1)} %collective-permute-done.other_ref.refs_1_, f32[32,8192]{1,0:T(8,128)} %load_hbm.1, ...), custom_call_target="tpu_custom_call" | custom-call | flops 20000000000 | bytes 100000 | tf_op jit(solution)/shard_map/net_moments/pallas_call | solution.py:268
  27.1 0.0 collective-permute-done.3.refs_4_
  27.1 0.0 collective-permute-done.2.refs_3_
  27.1 0.0 collective-permute-done.1.refs_2_
  27.2 0.1 collective-permute-start.4
  27.2 2.1 %collective-permute-start.5 = (f32[128,128]{1,0:T(8,128)S(1)}, f32[128,128]{1,0:T(8,128)S(1)}, u32[]{:S(2)}, u32[]{:S(2)}) collective-permute-start(f32[128,128]{1,0:T(8,128)S(1)} %get-tuple-element.22), channel_id=1, source_target_pairs={{0,8},{8,0},{16,24},{24,16},{1,9},{9,1},{17,25},{25,17},{2,10},{10... | collective-permute-start | bytes 196616 | tf_op jit(solution)/shard_map/ppermute | solution.py:264
  29.3 2.6 %collective-permute-start.6 = (f32[128,128]{1,0:T(8,128)S(1)}, f32[128,128]{1,0:T(8,128)S(1)}, u32[]{:S(2)}, u32[]{:S(2)}) collective-permute-start(f32[128,128]{1,0:T(8,128)S(1)} %get-tuple-element.23), channel_id=1, source_target_pairs={{0,16},{8,24},{16,0},{24,8},{1,17},{9,25},{17,1},{25,9},{2,18},{10... | collective-permute-start | bytes 196616 | tf_op jit(solution)/shard_map/ppermute | solution.py:264
  31.9 0.0 collective-permute-start.7
  31.9 0.0 collective-permute-done.4.refs_5_
  31.9 6.9 %gram_inverse.1.refs_4_ = f32[128,128]{1,0:T(8,128)S(1)} custom-call(f32[104,512]{1,0:T(8,128)S(1)} %copy-done, f32[104,512]{1,0:T(8,128)S(1)} %collective-permute-done.other_ref.refs_1_, f32[72,512]{1,0:T(8,128)S(1)} %collective-permute-done.1.refs_2_, f32[72,512]{1,0:T(8,128)S(1)} %collective-permute-done.2.refs_3_, ...), custom_call_target="tpu_custom_call" | custom-call | flops 6000000000 | bytes 100000 | tf_op jit(solution)/shard_map/gram_inverse/pallas_call | solution.py:268
  38.7 0.0 collective-permute-done.5.refs_1_
  38.8 0.0 collective-permute-done.6.refs_2_
  38.8 0.0 collective-permute-done.7.refs_3_
  38.8 0.0 copy-start.1
  38.8 2.7 %collective-permute-start.10 = (f32[128,128]{1,0:T(8,128)S(1)}, f32[128,128]{1,0:T(8,128)S(1)}, u32[]{:S(2)}, u32[]{:S(2)}) collective-permute-start(f32[128,128]{1,0:T(8,128)S(1)} %group_sum.1.refs_0_), channel_id=1, source_target_pairs={{0,6},{1,7},{2,4},{3,5},{4,2},{5,3},{6,0},{7,1},{8,14},{9,15},{10,... | collective-permute-start | bytes 196616 | tf_op jit(solution)/shard_map/ppermute | solution.py:264
  41.5 0.5 %collective-permute-start.9 = (f32[128,128]{1,0:T(8,128)S(1)}, f32[128,128]{1,0:T(8,128)S(1)}, u32[]{:S(2)}, u32[]{:S(2)}) collective-permute-start(f32[128,128]{1,0:T(8,128)S(1)} %group_sum.1.refs_0_), channel_id=1, source_target_pairs={{0,4},{1,5},{2,6},{3,7},{4,0},{5,1},{6,2},{7,3},{8,12},{9,13},{10,... | collective-permute-start | bytes 196616 | tf_op jit(solution)/shard_map/ppermute | solution.py:264
  42.1 0.3 collective-permute-start.8
  42.4 1.7 %collective-permute-done.10.refs_3_ = f32[128,128]{1,0:T(8,128)S(1)} collective-permute-done((f32[128,128]{1,0:T(8,128)S(1)}, f32[128,128]{1,0:T(8,128)S(1)}, u32[]{:S(2)}, u32[]{:S(2)}) %collective-permute-start.10) | collective-permute-done | bytes 65568 | tf_op jit(solution)/shard_map/ppermute | solution.py:264
  44.1 1.7 %collective-permute-done.9.refs_2_ = f32[128,128]{1,0:T(8,128)S(1)} collective-permute-done((f32[128,128]{1,0:T(8,128)S(1)}, f32[128,128]{1,0:T(8,128)S(1)}, u32[]{:S(2)}, u32[]{:S(2)}) %collective-permute-start.9) | collective-permute-done | bytes 65568 | tf_op jit(solution)/shard_map/ppermute | solution.py:264
  45.8 0.5 %collective-permute-done.8.refs_1_ = f32[128,128]{1,0:T(8,128)S(1)} collective-permute-done((f32[128,128]{1,0:T(8,128)S(1)}, f32[128,128]{1,0:T(8,128)S(1)}, u32[]{:S(2)}, u32[]{:S(2)}) %collective-permute-start.8) | collective-permute-done | bytes 65568 | tf_op jit(solution)/shard_map/ppermute | solution.py:264
  46.3 0.2 set_coeffs.1.mine_ref
  46.5 0.0 copy-start.6
  46.5 0.1 collective-permute-start.11
  46.6 0.6 %copy-done.6 = s32[256]{0:T(256)S(1)} copy-done((s32[256]{0:T(256)S(1)}, s32[256]{0:T(256)}, u32[]{:S(2)}) %copy-start.6) | copy-done | bytes 1048
  47.2 0.1 copy.11.limits_ref
  47.4 0.5 %collective-permute-done.11.other_ref = f32[128,128]{1,0:T(8,128)S(1)} collective-permute-done((f32[128,128]{1,0:T(8,128)S(1)}, f32[128,128]{1,0:T(8,128)S(1)}, u32[]{:S(2)}, u32[]{:S(2)}) %collective-permute-start.11) | collective-permute-done | bytes 65568 | tf_op jit(solution)/shard_map/ppermute | solution.py:264
  47.9 0.0 copy-done.1
  47.9 2.8 %set_exposure.1 = (f32[2,256,512]{2,1,0:T(8,128)}, f32[2,256]{1,0:T(2,128)}) custom-call(f32[128,128]{1,0:T(8,128)S(1)} %set_coeffs.1.mine_ref, f32[128,128]{1,0:T(8,128)S(1)} %collective-permute-done.11.other_ref, s32[256,1]{1,0:T(8,128)S(1)} %copy.11.limits_ref, f32[104,512]{1,0:T(8,128)S(1)} %copy-done.1, ...), custom_call_target="tpu_custom_call" | custom-call | flops 2000000000 | bytes 100000 | tf_op jit(solution)/shard_map/set_exposure/pallas_call | solution.py:268
  (2 shorter events, 0.0 us)
Async XLA Ops:
  0.6 6.2 %copy-start.2 = (f32[8192]{0:T(1024)S(1)}, f32[8192]{0:T(1024)}, u32[]{:S(2)}) copy-start(f32[8192]{0:T(1024)} %param.12) | copy-start | bytes 98308
  0.6 6.2 %copy-start.3 = (f32[8192]{0:T(1024)S(1)}, f32[8192]{0:T(1024)}, u32[]{:S(2)}) copy-start(f32[8192]{0:T(1024)} %param.13) | copy-start | bytes 98308
  0.7 6.2 %copy-start.4 = (s32[8192]{0:T(1024)S(1)}, s32[8192]{0:T(1024)}, u32[]{:S(2)}) copy-start(s32[8192]{0:T(1024)} %param.14) | copy-start | bytes 98308
  2.3 4.5 %collective-permute-start = (f32[104,512]{1,0:T(8,128)}, f32[104,512]{1,0:T(8,128)S(1)}, u32[]{:S(2)}, u32[]{:S(2)}) collective-permute-start(f32[104,512]{1,0:T(8,128)} %get-tuple-element.14.own_ref.refs_0_), channel_id=1, source_target_pairs={{0,1},{1,0},{2,3},{3,2},{4,5},{5,4},{6,7},{7,6},{8,9},{9,8},{10,11... | collective-permute-start | bytes 638984 | tf_op jit(solution)/shard_map/ppermute | solution.py:264
  2.8 24.3 %collective-permute-start.3 = (f32[72,512]{1,0:T(8,128)}, f32[72,512]{1,0:T(8,128)S(1)}, u32[]{:S(2)}, u32[]{:S(2)}) collective-permute-start(f32[72,512]{1,0:T(8,128)} %get-tuple-element.15), channel_id=1, source_target_pairs={{0,6},{1,7},{2,4},{3,5},{4,2},{5,3},{6,0},{7,1},{8,14},{9,15},{10,... | collective-permute-start | bytes 442376 | tf_op jit(solution)/shard_map/ppermute | solution.py:264
  6.2 20.9 %collective-permute-start.2 = (f32[72,512]{1,0:T(8,128)}, f32[72,512]{1,0:T(8,128)S(1)}, u32[]{:S(2)}, u32[]{:S(2)}) collective-permute-start(f32[72,512]{1,0:T(8,128)} %get-tuple-element.15), channel_id=1, source_target_pairs={{0,4},{1,5},{2,6},{3,7},{4,0},{5,1},{6,2},{7,3},{8,12},{9,13},{10,... | collective-permute-start | bytes 442376 | tf_op jit(solution)/shard_map/ppermute | solution.py:264
  6.7 20.4 %collective-permute-start.1 = (f32[72,512]{1,0:T(8,128)}, f32[72,512]{1,0:T(8,128)S(1)}, u32[]{:S(2)}, u32[]{:S(2)}) collective-permute-start(f32[72,512]{1,0:T(8,128)} %get-tuple-element.15), channel_id=1, source_target_pairs={{0,2},{1,3},{2,0},{3,1},{4,6},{5,7},{6,4},{7,5},{8,10},{9,11},{10,... | collective-permute-start | bytes 442376 | tf_op jit(solution)/shard_map/ppermute | solution.py:264
  6.9 0.7 %copy-start.5 = (s32[4]{0:T(128)S(1)}, s32[4]{0:T(128)}, u32[]{:S(2)}) copy-start(s32[4]{0:T(128)} %counts_ref.1) | copy-start | bytes 52
  7.5 0.9 %copy-start = (f32[104,512]{1,0:T(8,128)S(1)}, f32[104,512]{1,0:T(8,128)}, u32[]{:S(2)}) copy-start(f32[104,512]{1,0:T(8,128)} %get-tuple-element.14.own_ref.refs_0_) | copy-start | bytes 638980
  27.2 4.7 %collective-permute-start.4 = (f32[3,72,512]{2,1,0:T(8,128)S(1)}, f32[3,72,512]{2,1,0:T(8,128)S(1)}, u32[]{:S(2)}, u32[]{:S(2)}) collective-permute-start(f32[3,72,512]{2,1,0:T(8,128)S(1)} %pad_maximum_fusion), channel_id=1, source_target_pairs={{0,1},{1,0},{2,3},{3,2},{4,5},{5,4},{6,7},{7,6},{8,9},{9,8},{10,11... | collective-permute-start | bytes 1327112 | tf_op jit(solution)/shard_map/ppermute | solution.py:264
  27.2 11.5 %collective-permute-start.5 = (f32[128,128]{1,0:T(8,128)S(1)}, f32[128,128]{1,0:T(8,128)S(1)}, u32[]{:S(2)}, u32[]{:S(2)}) collective-permute-start(f32[128,128]{1,0:T(8,128)S(1)} %get-tuple-element.22), channel_id=1, source_target_pairs={{0,8},{8,0},{16,24},{24,16},{1,9},{9,1},{17,25},{25,17},{2,10},{10... | collective-permute-start | bytes 196616 | tf_op jit(solution)/shard_map/ppermute | solution.py:264
  29.3 9.5 %collective-permute-start.6 = (f32[128,128]{1,0:T(8,128)S(1)}, f32[128,128]{1,0:T(8,128)S(1)}, u32[]{:S(2)}, u32[]{:S(2)}) collective-permute-start(f32[128,128]{1,0:T(8,128)S(1)} %get-tuple-element.23), channel_id=1, source_target_pairs={{0,16},{8,24},{16,0},{24,8},{1,17},{9,25},{17,1},{25,9},{2,18},{10... | collective-permute-start | bytes 196616 | tf_op jit(solution)/shard_map/ppermute | solution.py:264
  31.9 6.9 %collective-permute-start.7 = (f32[128,128]{1,0:T(8,128)S(1)}, f32[128,128]{1,0:T(8,128)S(1)}, u32[]{:S(2)}, u32[]{:S(2)}) collective-permute-start(f32[128,128]{1,0:T(8,128)S(1)} %get-tuple-element.24), channel_id=1, source_target_pairs={{0,24},{8,16},{16,8},{24,0},{1,25},{9,17},{17,9},{25,1},{2,26},{10... | collective-permute-start | bytes 196616 | tf_op jit(solution)/shard_map/ppermute | solution.py:264
  38.8 9.1 %copy-start.1 = (f32[104,512]{1,0:T(8,128)S(1)}, f32[104,512]{1,0:T(8,128)}, u32[]{:S(2)}) copy-start(f32[104,512]{1,0:T(8,128)} %get-tuple-element.14.own_ref.refs_0_) | copy-start | bytes 638980
  38.8 5.3 %collective-permute-start.10 = (f32[128,128]{1,0:T(8,128)S(1)}, f32[128,128]{1,0:T(8,128)S(1)}, u32[]{:S(2)}, u32[]{:S(2)}) collective-permute-start(f32[128,128]{1,0:T(8,128)S(1)} %group_sum.1.refs_0_), channel_id=1, source_target_pairs={{0,6},{1,7},{2,4},{3,5},{4,2},{5,3},{6,0},{7,1},{8,14},{9,15},{10,... | collective-permute-start | bytes 196616 | tf_op jit(solution)/shard_map/ppermute | solution.py:264
  41.5 4.3 %collective-permute-start.9 = (f32[128,128]{1,0:T(8,128)S(1)}, f32[128,128]{1,0:T(8,128)S(1)}, u32[]{:S(2)}, u32[]{:S(2)}) collective-permute-start(f32[128,128]{1,0:T(8,128)S(1)} %group_sum.1.refs_0_), channel_id=1, source_target_pairs={{0,4},{1,5},{2,6},{3,7},{4,0},{5,1},{6,2},{7,3},{8,12},{9,13},{10,... | collective-permute-start | bytes 196616 | tf_op jit(solution)/shard_map/ppermute | solution.py:264
  42.1 4.3 %collective-permute-start.8 = (f32[128,128]{1,0:T(8,128)S(1)}, f32[128,128]{1,0:T(8,128)S(1)}, u32[]{:S(2)}, u32[]{:S(2)}) collective-permute-start(f32[128,128]{1,0:T(8,128)S(1)} %group_sum.1.refs_0_), channel_id=1, source_target_pairs={{0,2},{1,3},{2,0},{3,1},{4,6},{5,7},{6,4},{7,5},{8,10},{9,11},{10,... | collective-permute-start | bytes 196616 | tf_op jit(solution)/shard_map/ppermute | solution.py:264
  46.5 0.7 %copy-start.6 = (s32[256]{0:T(256)S(1)}, s32[256]{0:T(256)}, u32[]{:S(2)}) copy-start(s32[256]{0:T(256)} %param.17) | copy-start | bytes 3076
  46.5 1.3 %collective-permute-start.11 = (f32[128,128]{1,0:T(8,128)S(1)}, f32[128,128]{1,0:T(8,128)S(1)}, u32[]{:S(2)}, u32[]{:S(2)}) collective-permute-start(f32[128,128]{1,0:T(8,128)S(1)} %set_coeffs.1.mine_ref), channel_id=1, source_target_pairs={{0,1},{1,0},{2,3},{3,2},{4,5},{5,4},{6,7},{7,6},{8,9},{9,8},{10,11... | collective-permute-start | bytes 196616 | tf_op jit(solution)/shard_map/ppermute | solution.py:264

commit v3 on v2

--- a/solution.py
+++ b/solution.py
@@ -12,7 +12,7 @@
 F32 = jnp.float32
 BF16 = jnp.bfloat16
 TILE = 512
-CHUNK = 512
+CHUNK = 256
 SLOTS = 2
 DEPTH = 256
 PAD = 8
@@ -21,7 +21,7 @@
 NT = (((1,), (1,)), ((), ()))
 VMEM = pl.BlockSpec(memory_space=pltpu.VMEM)
 SMEM = pl.BlockSpec(memory_space=pltpu.SMEM)
-ANY = pl.BlockSpec(memory_space=pl.ANY)
+HBM = pl.BlockSpec(memory_space=pltpu.HBM)
 
 
 def mm(a, b, dims=NN):
@@ -66,30 +66,30 @@
     return ref[2 * factors : 2 * factors + 1, :]
 
 
-def pack_kernel(start_ref, shocks_ref, weights_ref, short_ref, whole_ref):
-    factors = start_ref.shape[0]
+def pack_kernel(counts_ref, start_ref, shocks_ref, weights_ref, short_ref, whole_ref):
+    factors, paths = start_ref.shape
+    filled = counts_ref[lax.axis_index("trade")].astype(F32)
+    spare = lax.broadcasted_iota(jnp.int32, (PAD, paths), 0) > 0
     for ref in (short_ref, whole_ref):
         ref[:factors, :] = start_ref[...]
         ref[factors : 2 * factors, :] = shocks_ref[0]
-        ref[2 * factors : 2 * factors + PAD, :] = jnp.broadcast_to(weights_ref[...].astype(F32), (PAD, ref.shape[1]))
+        ref[2 * factors : 2 * factors + PAD, :] = jnp.where(spare, filled, weights_ref[...].astype(F32))
     whole_ref[2 * factors + PAD :, :] = shocks_ref[1]
 
 
-def prepare(blocks, states_scr, wide_scr, load_scr, factors):
+def prepare(number, start, shocks, weight_row, states_scr, wide_scr):
     core = lax.axis_index("path") & 1
-    load_scr[...] = jnp.zeros_like(load_scr)
-    for number, block_ref in enumerate(blocks):
-        paths = block_ref.shape[1]
-        mine = pl.ds(number * paths, paths)
-        first, second = states_of(block_ref, factors)
-        third = 0.8 * second + 0.6 * block_ref[2 * factors + PAD :, :]
-        hi, lo = split2(basis_rows(pick(core, first, second)) * weights_of(block_ref, factors))
-        wide_scr[:, mine] = jnp.concatenate([hi, lo], axis=0)
-        hi, mid, low = split3(pick(core, second, third))
-        hi, mid, low = hi.astype(F32), mid.astype(F32), low.astype(F32)
-        ones = jnp.where(lax.broadcasted_iota(jnp.int32, (DEPTH - 6 * factors, paths), 0) < 3, 1.0, 0.0)
-        stacked = jnp.concatenate([hi, hi, mid, mid, hi, low, ones], axis=0)
-        states_scr[mine, :] = stacked.T.astype(BF16)
+    factors, paths = start.shape
+    mine = pl.ds(number * paths, paths)
+    second = 0.8 * start + 0.6 * shocks[0]
+    third = 0.8 * second + 0.6 * shocks[1]
+    hi, lo = split2(basis_rows(pick(core, start, second)) * weight_row)
+    wide_scr[:, mine] = jnp.concatenate([hi, lo], axis=0)
+    hi, mid, low = split3(pick(core, second, third))
+    hi, mid, low = hi.astype(F32), mid.astype(F32), low.astype(F32)
+    ones = jnp.where(lax.broadcasted_iota(jnp.int32, (DEPTH - 6 * factors, paths), 0) < 3, 1.0, 0.0)
+    stacked = jnp.concatenate([hi, hi, mid, mid, hi, low, ones], axis=0)
+    states_scr[mine, :] = stacked.T.astype(BF16)
 
 
 def load_rows(cols, load_ref, strike_ref, load_scr, slot):
@@ -120,26 +120,28 @@
 
 
 def moment_kernel(
-    groups, counts_ref, own_ref, other_ref, load_hbm, strike_hbm, notional_hbm, set_hbm, *refs
+    groups, own_ref, other_ref, load_hbm, strike_hbm, notional_hbm, set_hbm, *refs
 ):
     outs = refs[:groups]
-    load_ref, strike_ref, notional_ref, set_ref, sems, net_scr, *scratch = refs[groups:]
-    moves = copies(
-        (load_hbm, strike_hbm, notional_hbm, set_hbm), (load_ref, strike_ref, notional_ref, set_ref), sems
-    )
+    *staged, sems, net_scr, states_scr, wide_scr, load_scr = refs[groups:]
+    load_ref, strike_ref, notional_ref, set_ref = staged
+    moves = copies((load_hbm, strike_hbm, notional_hbm, set_hbm), staged, sems)
     for move in moves:
         move.start()
     group = lax.axis_index("trade")
-    filled = counts_ref[group]
+    factors = load_ref.shape[0]
+    filled = other_ref[2 * factors + 1 : 2 * factors + 2, :1].astype(jnp.int32)
     owned = net_scr.shape[0]
     bits = log2(owned)
     rows = 16
-    prepare((own_ref, other_ref), *scratch, load_ref.shape[0])
+    load_scr[...] = jnp.zeros_like(load_scr)
     net_scr[...] = jnp.zeros_like(net_scr)
+    for number, ref in enumerate((own_ref, other_ref)):
+        shocks = (ref[factors : 2 * factors, :], ref[2 * factors + PAD :, :])
+        prepare(number, ref[:factors, :], shocks, weights_of(ref, factors), states_scr, wide_scr)
     for move in moves:
         move.wait()
 
-    states_scr, wide_scr, load_scr = scratch
     chunks = [pl.ds(start, CHUNK) for start in range(0, states_scr.shape[0], CHUNK)]
 
     def add_tile(index, moment):
@@ -196,12 +198,17 @@
         basis = basis_rows(pick(core, *states_of(block, factors)))
         gram = gram + mm_full(basis * weights_of(block, factors), basis, NT)
     mat = gram
-    for k in range(wide):
-        row = mat[k : k + 1, :]
-        col = mat[:, k : k + 1]
-        pivot = 1.0 / mat[k : k + 1, k : k + 1]
-        row = jnp.where(lane[:1] == k, 1.0, row) * pivot
-        mat = jnp.where(sub == k, row, jnp.where(lane == k, 0.0, mat) - col * row)
+    for k in range(0, wide, 2):
+        top, low = mat[k : k + 1, :], mat[k + 1 : k + 2, :]
+        left, right = mat[:, k : k + 1], mat[:, k + 1 : k + 2]
+        a, b = left[k : k + 1], right[k : k + 1]
+        c, d = left[k + 1 : k + 2], right[k + 1 : k + 2]
+        scale = 1.0 / (a * d - b * c)
+        top = jnp.where(lane[:1] == k, 1.0, jnp.where(lane[:1] == k + 1, 0.0, top))
+        low = jnp.where(lane[:1] == k, 0.0, jnp.where(lane[:1] == k + 1, 1.0, low))
+        top, low = (d * top - b * low) * scale, (a * low - c * top) * scale
+        rest = jnp.where((lane >> 1) == k // 2, 0.0, mat) - left * top - right * low
+        mat = jnp.where(sub == k, top, jnp.where(sub == k + 1, low, rest))
     eye = jnp.where(sub == lane, 1.0, 0.0)
     mat = mat + mm_full(mat, eye - mm_full(gram, mat))
     zero = jnp.zeros_like(mat)
@@ -290,10 +297,11 @@
     assert dates == 2
 
     shape = jax.ShapeDtypeStruct
+    start_t, shocks_t, weights_row = start_state.T, jnp.swapaxes(shocks, 1, 2), weights[None, :]
     short, whole = run(
         pack_kernel, "pack_states",
         [shape(((dates - 1) * factors + factors + PAD, paths), F32), shape(((dates + 1) * factors + PAD, paths), F32)],
-        [VMEM] * 3, (start_state.T, jnp.swapaxes(shocks, 1, 2), weights[None, :]), 58,
+        [SMEM] + [VMEM] * 3, (live_counts, start_t, shocks_t, weights_row), 58,
     )
     other = swap(whole, "path", 1)
     across = [swap(short, "path", 2 * away) for away in range(1, ranks // 2)]
@@ -301,8 +309,8 @@
     strike_row, notional_row, set_row = strikes[None, :], notionals[None, :], trade_set[None, :]
     nets = run(
         functools.partial(moment_kernel, groups), "net_moments",
-        [shape((owned // 2, 2 * wide), F32)] * groups, [SMEM, VMEM, VMEM] + [ANY] * 4,
-        (live_counts, whole, other, loadings, strike_row, notional_row, set_row), 52.75,
+        [shape((owned // 2, 2 * wide), F32)] * groups, [VMEM] * 2 + [HBM] * 4,
+        (whole, other, loadings, strike_row, notional_row, set_row), 52.75,
         [
             pltpu.VMEM((factors, slots), F32),
             pltpu.VMEM((1, slots), F32),

time: 50.9 us -> 52.2 us (1.026)
  Pallas kernels: 30.2 us -> 32.2 us
  local copies, waits for them, and re-layouts: 2.32 us -> 1.67 us
    pallas_call x6, Pallas kernels: 30.2 us -> 32.2 us  [run(): pl.pallas_call(kernel, out_shape=out, in_specs=specs, out_specs=jax.tree....]
    unnamed x14 -> x12, local copies, waits for them, and re-layouts: 2.18 us -> 1.54 us
  transfers between devices with their start and end apart: 12 -> 12, of which waited for: 4 -> 4; matrix products, arithmetic and copies ran while one was open for 0% -> 0% of each run, Pallas kernels for 50% -> 53%
where the time goes in v3:
time: 52.2 us; the launch traced here: 52 us
  Pallas kernels  32.2 us (62%)
  starting transfers between devices  12.9 us (25%)
  waiting for transfers between devices  4.46 us (9%)
  local copies, waits for them, and re-layouts  1.67 us (3%)
  between operations  0.8 us (2%)
    pallas_call x6, Pallas kernels, run(): pl.pallas_call(kernel, out_shape=out, in_specs=specs, out_specs=jax.tree....  32.2 us
    ppermute x12, starting transfers between devices, swap(): lax.ppermute(x, axis, [(i, i ^ away) for i in range(lax.axis_size(axis))])  12.9 us
    ppermute x12, waiting for transfers between devices, swap(): lax.ppermute(x, axis, [(i, i ^ away) for i in range(lax.axis_size(axis))])  4.46 us
    unnamed x12, local copies, waits for them, and re-layouts  1.54 us
  transfers between devices with their start and end apart: 12, of which 4 were waited for; matrix products, arithmetic and copies ran while one was open for 0% of the time, Pallas kernels for 53%

profile of v3, /device:TPU:0, one launch (start us, length us, event | category | flops | bytes accessed | tf_op | source)
XLA Modules:
  0.0 52.0 jit_solution(10077266515721989576)
XLA Ops:
  0.6 0.0 copy-start.2
  0.6 0.0 copy-start.3
  0.7 0.0 copy-start.4
  0.7 1.7 %pack_states.1 = (f32[72,512]{1,0:T(8,128)}, f32[104,512]{1,0:T(8,128)}) custom-call(s32[4]{0:T(128)} %counts_ref.1, f32[32,512]{1,0:T(8,128)} %bitcast.17, f32[2,32,512]{2,1,0:T(8,128)} %bitcast.16, s32[1,512]{1,0:T(1,128)} %bitcast.18), custom_call_target="tpu_custom_call" | custom-call | bytes 100000 | tf_op jit(solution)/shard_map/pack_states/pallas_call | solution.py:275
  2.3 0.5 collective-permute-start
  2.8 3.4 %collective-permute-start.3 = (f32[72,512]{1,0:T(8,128)}, f32[72,512]{1,0:T(8,128)S(1)}, u32[]{:S(2)}, u32[]{:S(2)}) collective-permute-start(f32[72,512]{1,0:T(8,128)} %get-tuple-element.15), channel_id=1, source_target_pairs={{0,6},{1,7},{2,4},{3,5},{4,2},{5,3},{6,0},{7,1},{8,14},{9,15},{10,... | collective-permute-start | bytes 442376 | tf_op jit(solution)/shard_map/ppermute | solution.py:271
  6.2 0.5 collective-permute-start.2
  6.8 0.1 collective-permute-start.1
  6.9 0.0 collective-permute-done.other_ref.refs_1_
  6.9 0.0 copy-done.2
  6.9 0.0 copy-done.3
  6.9 0.0 copy-done.4
  6.9 0.0 copy-start
  6.9 0.9 %copy-done = f32[104,512]{1,0:T(8,128)S(1)} copy-done((f32[104,512]{1,0:T(8,128)S(1)}, f32[104,512]{1,0:T(8,128)}, u32[]{:S(2)}) %copy-start) | copy-done | bytes 213016
  7.8 18.9 %net_moments.1 = (f32[128,128]{1,0:T(8,128)S(1)}, f32[128,128]{1,0:T(8,128)S(1)}, f32[128,128]{1,0:T(8,128)S(1)}, f32[128,128]{1,0:T(8,128)S(1)}) custom-call(f32[104,512]{1,0:T(8,128)S(1)} %copy-done, f32[104,512]{1,0:T(8,128)S(1)} %collective-permute-done.other_ref.refs_1_, f32[32,8192]{1,0:T(8,128)} %load_hbm.1, f32[1,8192]{1,0:T(1,128)S(1)} %bitcast.13, ...), custom_call_target="tpu_custom_call" | custom-call | flops 20000000000 | bytes 100000 | tf_op jit(solution)/shard_map/net_moments/pallas_call | solution.py:275
  26.8 0.0 collective-permute-done.3.refs_4_
  26.8 0.0 collective-permute-done.2.refs_3_
  26.8 0.0 collective-permute-done.1.refs_2_
  26.8 0.1 collective-permute-start.4
  26.9 2.0 %collective-permute-start.5 = (f32[128,128]{1,0:T(8,128)S(1)}, f32[128,128]{1,0:T(8,128)S(1)}, u32[]{:S(2)}, u32[]{:S(2)}) collective-permute-start(f32[128,128]{1,0:T(8,128)S(1)} %get-tuple-element.22), channel_id=1, source_target_pairs={{0,8},{8,0},{16,24},{24,16},{1,9},{9,1},{17,25},{25,17},{2,10},{10... | collective-permute-start | bytes 196616 | tf_op jit(solution)/shard_map/ppermute | solution.py:271
  28.9 2.6 %collective-permute-start.6 = (f32[128,128]{1,0:T(8,128)S(1)}, f32[128,128]{1,0:T(8,128)S(1)}, u32[]{:S(2)}, u32[]{:S(2)}) collective-permute-start(f32[128,128]{1,0:T(8,128)S(1)} %get-tuple-element.23), channel_id=1, source_target_pairs={{0,16},{8,24},{16,0},{24,8},{1,17},{9,25},{17,1},{25,9},{2,18},{10... | collective-permute-start | bytes 196616 | tf_op jit(solution)/shard_map/ppermute | solution.py:271
  31.5 0.0 collective-permute-start.7
  31.5 0.0 collective-permute-done.4.refs_5_
  31.5 8.6 %gram_inverse.1.refs_4_ = f32[128,128]{1,0:T(8,128)S(1)} custom-call(f32[104,512]{1,0:T(8,128)S(1)} %copy-done, f32[104,512]{1,0:T(8,128)S(1)} %collective-permute-done.other_ref.refs_1_, f32[72,512]{1,0:T(8,128)S(1)} %collective-permute-done.1.refs_2_, f32[72,512]{1,0:T(8,128)S(1)} %collective-permute-done.2.refs_3_, ...), custom_call_target="tpu_custom_call" | custom-call | flops 6000000000 | bytes 100000 | tf_op jit(solution)/shard_map/gram_inverse/pallas_call | solution.py:275
  40.1 0.0 collective-permute-done.5.refs_1_
  40.2 0.0 collective-permute-done.6.refs_2_
  40.2 0.0 collective-permute-done.7.refs_3_
  40.2 0.0 copy-start.1
  40.2 2.7 %collective-permute-start.10 = (f32[128,128]{1,0:T(8,128)S(1)}, f32[128,128]{1,0:T(8,128)S(1)}, u32[]{:S(2)}, u32[]{:S(2)}) collective-permute-start(f32[128,128]{1,0:T(8,128)S(1)} %group_sum.1.refs_0_), channel_id=1, source_target_pairs={{0,6},{1,7},{2,4},{3,5},{4,2},{5,3},{6,0},{7,1},{8,14},{9,15},{10,... | collective-permute-start | bytes 196616 | tf_op jit(solution)/shard_map/ppermute | solution.py:271
  42.9 0.5 collective-permute-start.9
  43.4 0.3 collective-permute-start.8
  43.8 1.7 %collective-permute-done.10.refs_3_ = f32[128,128]{1,0:T(8,128)S(1)} collective-permute-done((f32[128,128]{1,0:T(8,128)S(1)}, f32[128,128]{1,0:T(8,128)S(1)}, u32[]{:S(2)}, u32[]{:S(2)}) %collective-permute-start.10) | collective-permute-done | bytes 65568 | tf_op jit(solution)/shard_map/ppermute | solution.py:271
  45.5 1.7 %collective-permute-done.9.refs_2_ = f32[128,128]{1,0:T(8,128)S(1)} collective-permute-done((f32[128,128]{1,0:T(8,128)S(1)}, f32[128,128]{1,0:T(8,128)S(1)}, u32[]{:S(2)}, u32[]{:S(2)}) %collective-permute-start.9) | collective-permute-done | bytes 65568 | tf_op jit(solution)/shard_map/ppermute | solution.py:271
  47.2 0.5 collective-permute-done.8.refs_1_
  47.7 0.2 set_coeffs.1.mine_ref
  47.9 0.0 copy-start.5
  47.9 0.1 collective-permute-start.11
  48.0 0.6 %copy-done.5 = s32[256]{0:T(256)S(1)} copy-done((s32[256]{0:T(256)S(1)}, s32[256]{0:T(256)}, u32[]{:S(2)}) %copy-start.5) | copy-done | bytes 1048
  48.6 0.1 copy.11.limits_ref
  48.7 0.5 collective-permute-done.11.other_ref
  49.2 0.0 copy-done.1
  49.2 2.8 %set_exposure.1 = (f32[2,256,512]{2,1,0:T(8,128)}, f32[2,256]{1,0:T(2,128)}) custom-call(f32[128,128]{1,0:T(8,128)S(1)} %set_coeffs.1.mine_ref, f32[128,128]{1,0:T(8,128)S(1)} %collective-permute-done.11.other_ref, s32[256,1]{1,0:T(8,128)S(1)} %copy.11.limits_ref, f32[104,512]{1,0:T(8,128)S(1)} %copy-done.1, ...), custom_call_target="tpu_custom_call" | custom-call | flops 2000000000 | bytes 100000 | tf_op jit(solution)/shard_map/set_exposure/pallas_call | solution.py:275
  (2 shorter events, 0.0 us)
Async XLA Ops:
  0.6 6.3 %copy-start.2 = (f32[8192]{0:T(1024)S(1)}, f32[8192]{0:T(1024)}, u32[]{:S(2)}) copy-start(f32[8192]{0:T(1024)} %param.12) | copy-start | bytes 98308
  0.6 6.2 %copy-start.3 = (f32[8192]{0:T(1024)S(1)}, f32[8192]{0:T(1024)}, u32[]{:S(2)}) copy-start(f32[8192]{0:T(1024)} %param.13) | copy-start | bytes 98308
  0.7 6.2 %copy-start.4 = (s32[8192]{0:T(1024)S(1)}, s32[8192]{0:T(1024)}, u32[]{:S(2)}) copy-start(s32[8192]{0:T(1024)} %param.14) | copy-start | bytes 98308
  2.3 4.5 %collective-permute-start = (f32[104,512]{1,0:T(8,128)}, f32[104,512]{1,0:T(8,128)S(1)}, u32[]{:S(2)}, u32[]{:S(2)}) collective-permute-start(f32[104,512]{1,0:T(8,128)} %get-tuple-element.14.own_ref.refs_0_), channel_id=1, source_target_pairs={{0,1},{1,0},{2,3},{3,2},{4,5},{5,4},{6,7},{7,6},{8,9},{9,8},{10,11... | collective-permute-start | bytes 638984 | tf_op jit(solution)/shard_map/ppermute | solution.py:271
  2.8 24.0 %collective-permute-start.3 = (f32[72,512]{1,0:T(8,128)}, f32[72,512]{1,0:T(8,128)S(1)}, u32[]{:S(2)}, u32[]{:S(2)}) collective-permute-start(f32[72,512]{1,0:T(8,128)} %get-tuple-element.15), channel_id=1, source_target_pairs={{0,6},{1,7},{2,4},{3,5},{4,2},{5,3},{6,0},{7,1},{8,14},{9,15},{10,... | collective-permute-start | bytes 442376 | tf_op jit(solution)/shard_map/ppermute | solution.py:271
  6.2 20.5 %collective-permute-start.2 = (f32[72,512]{1,0:T(8,128)}, f32[72,512]{1,0:T(8,128)S(1)}, u32[]{:S(2)}, u32[]{:S(2)}) collective-permute-start(f32[72,512]{1,0:T(8,128)} %get-tuple-element.15), channel_id=1, source_target_pairs={{0,4},{1,5},{2,6},{3,7},{4,0},{5,1},{6,2},{7,3},{8,12},{9,13},{10,... | collective-permute-start | bytes 442376 | tf_op jit(solution)/shard_map/ppermute | solution.py:271
  6.8 20.0 %collective-permute-start.1 = (f32[72,512]{1,0:T(8,128)}, f32[72,512]{1,0:T(8,128)S(1)}, u32[]{:S(2)}, u32[]{:S(2)}) collective-permute-start(f32[72,512]{1,0:T(8,128)} %get-tuple-element.15), channel_id=1, source_target_pairs={{0,2},{1,3},{2,0},{3,1},{4,6},{5,7},{6,4},{7,5},{8,10},{9,11},{10,... | collective-permute-start | bytes 442376 | tf_op jit(solution)/shard_map/ppermute | solution.py:271
  6.9 0.9 %copy-start = (f32[104,512]{1,0:T(8,128)S(1)}, f32[104,512]{1,0:T(8,128)}, u32[]{:S(2)}) copy-start(f32[104,512]{1,0:T(8,128)} %get-tuple-element.14.own_ref.refs_0_) | copy-start | bytes 638980
  26.8 4.7 %collective-permute-start.4 = (f32[3,72,512]{2,1,0:T(8,128)S(1)}, f32[3,72,512]{2,1,0:T(8,128)S(1)}, u32[]{:S(2)}, u32[]{:S(2)}) collective-permute-start(f32[3,72,512]{2,1,0:T(8,128)S(1)} %pad_maximum_fusion), channel_id=1, source_target_pairs={{0,1},{1,0},{2,3},{3,2},{4,5},{5,4},{6,7},{7,6},{8,9},{9,8},{10,11... | collective-permute-start | bytes 1327112 | tf_op jit(solution)/shard_map/ppermute | solution.py:271
  26.9 13.2 %collective-permute-start.5 = (f32[128,128]{1,0:T(8,128)S(1)}, f32[128,128]{1,0:T(8,128)S(1)}, u32[]{:S(2)}, u32[]{:S(2)}) collective-permute-start(f32[128,128]{1,0:T(8,128)S(1)} %get-tuple-element.22), channel_id=1, source_target_pairs={{0,8},{8,0},{16,24},{24,16},{1,9},{9,1},{17,25},{25,17},{2,10},{10... | collective-permute-start | bytes 196616 | tf_op jit(solution)/shard_map/ppermute | solution.py:271
  28.9 11.2 %collective-permute-start.6 = (f32[128,128]{1,0:T(8,128)S(1)}, f32[128,128]{1,0:T(8,128)S(1)}, u32[]{:S(2)}, u32[]{:S(2)}) collective-permute-start(f32[128,128]{1,0:T(8,128)S(1)} %get-tuple-element.23), channel_id=1, source_target_pairs={{0,16},{8,24},{16,0},{24,8},{1,17},{9,25},{17,1},{25,9},{2,18},{10... | collective-permute-start | bytes 196616 | tf_op jit(solution)/shard_map/ppermute | solution.py:271
  31.5 8.6 %collective-permute-start.7 = (f32[128,128]{1,0:T(8,128)S(1)}, f32[128,128]{1,0:T(8,128)S(1)}, u32[]{:S(2)}, u32[]{:S(2)}) collective-permute-start(f32[128,128]{1,0:T(8,128)S(1)} %get-tuple-element.24), channel_id=1, source_target_pairs={{0,24},{8,16},{16,8},{24,0},{1,25},{9,17},{17,9},{25,1},{2,26},{10... | collective-permute-start | bytes 196616 | tf_op jit(solution)/shard_map/ppermute | solution.py:271
  40.2 9.0 %copy-start.1 = (f32[104,512]{1,0:T(8,128)S(1)}, f32[104,512]{1,0:T(8,128)}, u32[]{:S(2)}) copy-start(f32[104,512]{1,0:T(8,128)} %get-tuple-element.14.own_ref.refs_0_) | copy-start | bytes 638980
  40.2 5.3 %collective-permute-start.10 = (f32[128,128]{1,0:T(8,128)S(1)}, f32[128,128]{1,0:T(8,128)S(1)}, u32[]{:S(2)}, u32[]{:S(2)}) collective-permute-start(f32[128,128]{1,0:T(8,128)S(1)} %group_sum.1.refs_0_), channel_id=1, source_target_pairs={{0,6},{1,7},{2,4},{3,5},{4,2},{5,3},{6,0},{7,1},{8,14},{9,15},{10,... | collective-permute-start | bytes 196616 | tf_op jit(solution)/shard_map/ppermute | solution.py:271
  42.9 4.3 %collective-permute-start.9 = (f32[128,128]{1,0:T(8,128)S(1)}, f32[128,128]{1,0:T(8,128)S(1)}, u32[]{:S(2)}, u32[]{:S(2)}) collective-permute-start(f32[128,128]{1,0:T(8,128)S(1)} %group_sum.1.refs_0_), channel_id=1, source_target_pairs={{0,4},{1,5},{2,6},{3,7},{4,0},{5,1},{6,2},{7,3},{8,12},{9,13},{10,... | collective-permute-start | bytes 196616 | tf_op jit(solution)/shard_map/ppermute | solution.py:271
  43.4 4.3 %collective-permute-start.8 = (f32[128,128]{1,0:T(8,128)S(1)}, f32[128,128]{1,0:T(8,128)S(1)}, u32[]{:S(2)}, u32[]{:S(2)}) collective-permute-start(f32[128,128]{1,0:T(8,128)S(1)} %group_sum.1.refs_0_), channel_id=1, source_target_pairs={{0,2},{1,3},{2,0},{3,1},{4,6},{5,7},{6,4},{7,5},{8,10},{9,11},{10,... | collective-permute-start | bytes 196616 | tf_op jit(solution)/shard_map/ppermute | solution.py:271
  47.9 0.7 %copy-start.5 = (s32[256]{0:T(256)S(1)}, s32[256]{0:T(256)}, u32[]{:S(2)}) copy-start(s32[256]{0:T(256)} %param.17) | copy-start | bytes 3076
  47.9 1.3 %collective-permute-start.11 = (f32[128,128]{1,0:T(8,128)S(1)}, f32[128,128]{1,0:T(8,128)S(1)}, u32[]{:S(2)}, u32[]{:S(2)}) collective-permute-start(f32[128,128]{1,0:T(8,128)S(1)} %set_coeffs.1.mine_ref), channel_id=1, source_target_pairs={{0,1},{1,0},{2,3},{3,2},{4,5},{5,4},{6,7},{7,6},{8,9},{9,8},{10,11... | collective-permute-start | bytes 196616 | tf_op jit(solution)/shard_map/ppermute | solution.py:271

commit v4 on v3

--- a/solution.py
+++ b/solution.py
@@ -12,8 +12,9 @@
 F32 = jnp.float32
 BF16 = jnp.bfloat16
 TILE = 512
-CHUNK = 256
-SLOTS = 2
+CHUNK = 512
+SLOTS = 4
+FIRST_PIVOTS = 36
 DEPTH = 256
 PAD = 8
 MIB = 1024 * 1024
@@ -187,30 +188,37 @@
         out[...] = jnp.concatenate([net[:half], net[half:]], axis=1)
 
 
-def inverse_kernel(factors, *refs):
-    blocks, inverse_ref = refs[:-1], refs[-1]
+def eliminate(mat, pivots):
+    sub = lax.broadcasted_iota(jnp.int32, mat.shape, 0)
+    lane = lax.broadcasted_iota(jnp.int32, mat.shape, 1)
+    for k in pivots:
+        row = mat[k : k + 1, :]
+        col = mat[:, k : k + 1]
+        pivot = 1.0 / mat[k : k + 1, k : k + 1]
+        row = jnp.where(lane[:1] == k, 1.0, row) * pivot
+        mat = jnp.where(sub == k, row, jnp.where(lane == k, 0.0, mat) - col * row)
+    return mat
+
+
+def gram_kernel(factors, *refs):
+    blocks, gram_ref, mat_ref = refs[:-2], refs[-2], refs[-1]
     core = lax.axis_index("path") & 1
     wide = 2 * factors
-    sub = lax.broadcasted_iota(jnp.int32, (wide, wide), 0)
-    lane = lax.broadcasted_iota(jnp.int32, (wide, wide), 1)
     gram = jnp.zeros((wide, wide), F32)
     for block in path_blocks(blocks):
         basis = basis_rows(pick(core, *states_of(block, factors)))
         gram = gram + mm_full(basis * weights_of(block, factors), basis, NT)
-    mat = gram
-    for k in range(0, wide, 2):
-        top, low = mat[k : k + 1, :], mat[k + 1 : k + 2, :]
-        left, right = mat[:, k : k + 1], mat[:, k + 1 : k + 2]
-        a, b = left[k : k + 1], right[k : k + 1]
-        c, d = left[k + 1 : k + 2], right[k + 1 : k + 2]
-        scale = 1.0 / (a * d - b * c)
-        top = jnp.where(lane[:1] == k, 1.0, jnp.where(lane[:1] == k + 1, 0.0, top))
-        low = jnp.where(lane[:1] == k, 0.0, jnp.where(lane[:1] == k + 1, 1.0, low))
-        top, low = (d * top - b * low) * scale, (a * low - c * top) * scale
-        rest = jnp.where((lane >> 1) == k // 2, 0.0, mat) - left * top - right * low
-        mat = jnp.where(sub == k, top, jnp.where(sub == k + 1, low, rest))
-    eye = jnp.where(sub == lane, 1.0, 0.0)
-    mat = mat + mm_full(mat, eye - mm_full(gram, mat))
+    gram_ref[...] = gram
+    mat_ref[...] = eliminate(gram, range(FIRST_PIVOTS))
+
+
+def inverse_kernel(gram_ref, mat_ref, inverse_ref):
+    gram = gram_ref[...]
+    wide = gram.shape[0]
+    mat = eliminate(mat_ref[...], range(FIRST_PIVOTS, wide))
+    sub = lax.broadcasted_iota(jnp.int32, (wide, wide), 0)
+    lane = lax.broadcasted_iota(jnp.int32, (wide, wide), 1)
+    mat = mat + mm_full(mat, jnp.where(sub == lane, 1.0, 0.0) - mm_full(gram, mat))
     zero = jnp.zeros_like(mat)
     upper = jnp.concatenate([mat, zero], axis=1)
     inverse_ref[...] = jnp.concatenate([upper, jnp.concatenate([zero, mat], axis=1)], axis=0)
@@ -328,11 +336,14 @@
     others = swap(jnp.stack(across), "path", 1)
     got = [swap(nets[away], "trade", away) for away in range(1, groups)]
     blocks = (whole, other, *across, others)
+    gram, mat = run(
+        functools.partial(gram_kernel, factors), "gram_first_pivots", [shape((wide, wide), F32)] * 2,
+        [VMEM] * len(blocks), blocks, 8, (), 5.0,
+    )
+    mat, net = lax.optimization_barrier((mat, net))
     inverse = run(
-        functools.partial(inverse_kernel, factors), "gram_inverse", shape((2 * wide, 2 * wide), F32),
-        [VMEM] * len(blocks), blocks, 8, (), 6.0,
-    )
-    inverse, net = lax.optimization_barrier((inverse, net))
+        inverse_kernel, "gram_inverse", shape((2 * wide, 2 * wide), F32), [VMEM] * 2, (gram, mat), 8, (), 3.0
+    )
     part = run(
         sum_kernel, "group_sum", shape((owned // 2, 2 * wide), F32), [VMEM] * groups, [net] + got, 4
     )

time: 52.2 us -> 48.3 us (0.925)
  Pallas kernels: 32.2 us -> 29.2 us
  waiting for transfers between devices: 4.46 us -> 3.54 us
    pallas_call x6 -> x7, Pallas kernels: 32.2 us -> 29.2 us  [run(): pl.pallas_call(kernel, out_shape=out, in_specs=specs, out_specs=jax.tree....]
    ppermute x12, waiting for transfers between devices: 4.46 us -> 3.54 us  [swap(): lax.ppermute(x, axis, [(i, i ^ away) for i in range(lax.axis_size(axis))])]
  transfers between devices with their start and end apart: 12 -> 12, of which waited for: 4 -> 5; matrix products, arithmetic and copies ran while one was open for 0% -> 0% of each run, Pallas kernels for 53% -> 51%
where the time goes in v4:
time: 48.3 us; the launch traced here: 48.1 us
  Pallas kernels  29.2 us (60%)
  starting transfers between devices  12.9 us (27%)
  waiting for transfers between devices  3.54 us (7%)
  local copies, waits for them, and re-layouts  1.68 us (3%)
  between operations  0.79 us (2%)
    pallas_call x7, Pallas kernels, run(): pl.pallas_call(kernel, out_shape=out, in_specs=specs, out_specs=jax.tree....  29.2 us
    ppermute x12, starting transfers between devices, swap(): lax.ppermute(x, axis, [(i, i ^ away) for i in range(lax.axis_size(axis))])  12.9 us
    ppermute x12, waiting for transfers between devices, swap(): lax.ppermute(x, axis, [(i, i ^ away) for i in range(lax.axis_size(axis))])  3.54 us
    unnamed x12, local copies, waits for them, and re-layouts  1.55 us
  transfers between devices with their start and end apart: 12, of which 5 were waited for; matrix products, arithmetic and copies ran while one was open for 0% of the time, Pallas kernels for 51%

profile of v4, /device:TPU:0, one launch (start us, length us, event | category | flops | bytes accessed | tf_op | source)
XLA Modules:
  0.0 48.1 jit_solution(17743229973620886200)
XLA Ops:
  0.6 0.0 copy-start.2
  0.6 0.0 copy-start.3
  0.7 0.0 copy-start.4
  0.7 1.7 %pack_states.1 = (f32[72,512]{1,0:T(8,128)}, f32[104,512]{1,0:T(8,128)}) custom-call(s32[4]{0:T(128)} %counts_ref.1, f32[32,512]{1,0:T(8,128)} %bitcast.17, f32[2,32,512]{2,1,0:T(8,128)} %bitcast.16, s32[1,512]{1,0:T(1,128)} %bitcast.18), custom_call_target="tpu_custom_call" | custom-call | bytes 100000 | tf_op jit(solution)/shard_map/pack_states/pallas_call | solution.py:283
  2.3 0.5 collective-permute-start
  2.8 3.4 %collective-permute-start.3 = (f32[72,512]{1,0:T(8,128)}, f32[72,512]{1,0:T(8,128)S(1)}, u32[]{:S(2)}, u32[]{:S(2)}) collective-permute-start(f32[72,512]{1,0:T(8,128)} %get-tuple-element.17), channel_id=1, source_target_pairs={{0,6},{1,7},{2,4},{3,5},{4,2},{5,3},{6,0},{7,1},{8,14},{9,15},{10,... | collective-permute-start | bytes 442376 | tf_op jit(solution)/shard_map/ppermute | solution.py:279
  6.2 0.5 %collective-permute-start.2 = (f32[72,512]{1,0:T(8,128)}, f32[72,512]{1,0:T(8,128)S(1)}, u32[]{:S(2)}, u32[]{:S(2)}) collective-permute-start(f32[72,512]{1,0:T(8,128)} %get-tuple-element.17), channel_id=1, source_target_pairs={{0,4},{1,5},{2,6},{3,7},{4,0},{5,1},{6,2},{7,3},{8,12},{9,13},{10,... | collective-permute-start | bytes 442376 | tf_op jit(solution)/shard_map/ppermute | solution.py:279
  6.8 0.1 collective-permute-start.1
  6.9 0.0 collective-permute-done.other_ref.refs_1_
  6.9 0.0 copy-done.2
  6.9 0.0 copy-done.3
  6.9 0.0 copy-done.4
  6.9 0.0 copy-start
  6.9 0.9 %copy-done = f32[104,512]{1,0:T(8,128)S(1)} copy-done((f32[104,512]{1,0:T(8,128)S(1)}, f32[104,512]{1,0:T(8,128)}, u32[]{:S(2)}) %copy-start) | copy-done | bytes 213016
  7.8 17.7 %net_moments.1 = (f32[128,128]{1,0:T(8,128)S(1)}, f32[128,128]{1,0:T(8,128)S(1)}, f32[128,128]{1,0:T(8,128)S(1)}, f32[128,128]{1,0:T(8,128)S(1)}) custom-call(f32[104,512]{1,0:T(8,128)S(1)} %copy-done, f32[104,512]{1,0:T(8,128)S(1)} %collective-permute-done.other_ref.refs_1_, f32[32,8192]{1,0:T(8,128)} %load_hbm.1, f32[1,8192]{1,0:T(1,128)S(1)} %bitcast.13, ...), custom_call_target="tpu_custom_call" | custom-call | flops 20000000000 | bytes 100000 | tf_op jit(solution)/shard_map/net_moments/pallas_call | solution.py:283
  25.6 0.0 collective-permute-done.3.refs_4_
  25.6 0.0 collective-permute-done.2.refs_3_
  25.6 0.0 collective-permute-done.1.refs_2_
  25.6 0.1 collective-permute-start.4
  25.7 2.1 %collective-permute-start.5 = (f32[128,128]{1,0:T(8,128)S(1)}, f32[128,128]{1,0:T(8,128)S(1)}, u32[]{:S(2)}, u32[]{:S(2)}) collective-permute-start(f32[128,128]{1,0:T(8,128)S(1)} %get-tuple-element.25), channel_id=1, source_target_pairs={{0,8},{8,0},{16,24},{24,16},{1,9},{9,1},{17,25},{25,17},{2,10},{10... | collective-permute-start | bytes 196616 | tf_op jit(solution)/shard_map/ppermute | solution.py:279
  27.8 2.6 %collective-permute-start.6 = (f32[128,128]{1,0:T(8,128)S(1)}, f32[128,128]{1,0:T(8,128)S(1)}, u32[]{:S(2)}, u32[]{:S(2)}) collective-permute-start(f32[128,128]{1,0:T(8,128)S(1)} %get-tuple-element.26), channel_id=1, source_target_pairs={{0,16},{8,24},{16,0},{24,8},{1,17},{9,25},{17,1},{25,9},{2,18},{10... | collective-permute-start | bytes 196616 | tf_op jit(solution)/shard_map/ppermute | solution.py:279
  30.4 0.0 collective-permute-start.7
  30.4 0.0 collective-permute-done.4.refs_5_
  30.4 4.1 %gram_first_pivots.1 = (f32[64,64]{1,0:T(8,128)S(1)}, f32[64,64]{1,0:T(8,128)S(1)}) custom-call(f32[104,512]{1,0:T(8,128)S(1)} %copy-done, f32[104,512]{1,0:T(8,128)S(1)} %collective-permute-done.other_ref.refs_1_, f32[72,512]{1,0:T(8,128)S(1)} %collective-permute-done.1.refs_2_, f32[72,512]{1,0:T(8,128)S(1)} %collective-permute-done.2.refs_3_, ...), custom_call_target="tpu_custom_call" | custom-call | flops 5000000000 | bytes 100000 | tf_op jit(solution)/shard_map/gram_first_pivots/pallas_call | solution.py:283
  34.4 0.0 collective-permute-done.5.refs_1_
  34.4 1.1 %collective-permute-done.6.refs_2_ = f32[128,128]{1,0:T(8,128)S(1)} collective-permute-done((f32[128,128]{1,0:T(8,128)S(1)}, f32[128,128]{1,0:T(8,128)S(1)}, u32[]{:S(2)}, u32[]{:S(2)}) %collective-permute-start.6) | collective-permute-done | bytes 65568 | tf_op jit(solution)/shard_map/ppermute | solution.py:279
  35.5 1.0 %collective-permute-done.7.refs_3_ = f32[128,128]{1,0:T(8,128)S(1)} collective-permute-done((f32[128,128]{1,0:T(8,128)S(1)}, f32[128,128]{1,0:T(8,128)S(1)}, u32[]{:S(2)}, u32[]{:S(2)}) %collective-permute-start.7) | collective-permute-done | bytes 65568 | tf_op jit(solution)/shard_map/ppermute | solution.py:279
  36.5 2.5 %collective-permute-start.10 = (f32[128,128]{1,0:T(8,128)S(1)}, f32[128,128]{1,0:T(8,128)S(1)}, u32[]{:S(2)}, u32[]{:S(2)}) collective-permute-start(f32[128,128]{1,0:T(8,128)S(1)} %group_sum.1.refs_0_), channel_id=1, source_target_pairs={{0,6},{1,7},{2,4},{3,5},{4,2},{5,3},{6,0},{7,1},{8,14},{9,15},{10,... | collective-permute-start | bytes 196616 | tf_op jit(solution)/shard_map/ppermute | solution.py:279
  39.0 0.5 %collective-permute-start.9 = (f32[128,128]{1,0:T(8,128)S(1)}, f32[128,128]{1,0:T(8,128)S(1)}, u32[]{:S(2)}, u32[]{:S(2)}) collective-permute-start(f32[128,128]{1,0:T(8,128)S(1)} %group_sum.1.refs_0_), channel_id=1, source_target_pairs={{0,4},{1,5},{2,6},{3,7},{4,0},{5,1},{6,2},{7,3},{8,12},{9,13},{10,... | collective-permute-start | bytes 196616 | tf_op jit(solution)/shard_map/ppermute | solution.py:279
  39.5 0.5 %collective-permute-start.8 = (f32[128,128]{1,0:T(8,128)S(1)}, f32[128,128]{1,0:T(8,128)S(1)}, u32[]{:S(2)}, u32[]{:S(2)}) collective-permute-start(f32[128,128]{1,0:T(8,128)S(1)} %group_sum.1.refs_0_), channel_id=1, source_target_pairs={{0,2},{1,3},{2,0},{3,1},{4,6},{5,7},{6,4},{7,5},{8,10},{9,11},{10,... | collective-permute-start | bytes 196616 | tf_op jit(solution)/shard_map/ppermute | solution.py:279
  40.1 2.8 %gram_inverse.1.refs_4_ = f32[128,128]{1,0:T(8,128)S(1)} custom-call(f32[64,64]{1,0:T(8,128)S(1)} %get-tuple-element.28.gram_ref, f32[64,64]{1,0:T(8,128)S(1)} %get-tuple-element.29.mat_ref), custom_call_target="tpu_custom_call" | custom-call | flops 3000000000 | bytes 100000 | tf_op jit(solution)/shard_map/gram_inverse/pallas_call | solution.py:283
  42.8 0.0 copy-start.1
  42.8 0.0 collective-permute-done.10.refs_3_
  42.8 0.5 collective-permute-done.9.refs_2_
  43.3 0.5 %collective-permute-done.8.refs_1_ = f32[128,128]{1,0:T(8,128)S(1)} collective-permute-done((f32[128,128]{1,0:T(8,128)S(1)}, f32[128,128]{1,0:T(8,128)S(1)}, u32[]{:S(2)}, u32[]{:S(2)}) %collective-permute-start.8) | collective-permute-done | bytes 65568 | tf_op jit(solution)/shard_map/ppermute | solution.py:279
  43.8 0.2 set_coeffs.1.mine_ref
  44.0 0.0 copy-start.5
  44.0 0.1 collective-permute-start.11
  44.1 0.6 %copy-done.5 = s32[256]{0:T(256)S(1)} copy-done((s32[256]{0:T(256)S(1)}, s32[256]{0:T(256)}, u32[]{:S(2)}) %copy-start.5) | copy-done | bytes 1048
  44.7 0.1 copy.11.limits_ref
  44.8 0.5 %collective-permute-done.11.other_ref = f32[128,128]{1,0:T(8,128)S(1)} collective-permute-done((f32[128,128]{1,0:T(8,128)S(1)}, f32[128,128]{1,0:T(8,128)S(1)}, u32[]{:S(2)}, u32[]{:S(2)}) %collective-permute-start.11) | collective-permute-done | bytes 65568 | tf_op jit(solution)/shard_map/ppermute | solution.py:279
  45.3 0.0 copy-done.1
  45.3 2.8 %set_exposure.1 = (f32[2,256,512]{2,1,0:T(8,128)}, f32[2,256]{1,0:T(2,128)}) custom-call(f32[128,128]{1,0:T(8,128)S(1)} %set_coeffs.1.mine_ref, f32[128,128]{1,0:T(8,128)S(1)} %collective-permute-done.11.other_ref, s32[256,1]{1,0:T(8,128)S(1)} %copy.11.limits_ref, f32[104,512]{1,0:T(8,128)S(1)} %copy-done.1, ...), custom_call_target="tpu_custom_call" | custom-call | flops 2000000000 | bytes 100000 | tf_op jit(solution)/shard_map/set_exposure/pallas_call | solution.py:283
  (2 shorter events, 0.0 us)
Async XLA Ops:
  0.6 6.3 %copy-start.2 = (f32[8192]{0:T(1024)S(1)}, f32[8192]{0:T(1024)}, u32[]{:S(2)}) copy-start(f32[8192]{0:T(1024)} %param.12) | copy-start | bytes 98308
  0.6 6.2 %copy-start.3 = (f32[8192]{0:T(1024)S(1)}, f32[8192]{0:T(1024)}, u32[]{:S(2)}) copy-start(f32[8192]{0:T(1024)} %param.13) | copy-start | bytes 98308
  0.7 6.2 %copy-start.4 = (s32[8192]{0:T(1024)S(1)}, s32[8192]{0:T(1024)}, u32[]{:S(2)}) copy-start(s32[8192]{0:T(1024)} %param.14) | copy-start | bytes 98308
  2.3 4.5 %collective-permute-start = (f32[104,512]{1,0:T(8,128)}, f32[104,512]{1,0:T(8,128)S(1)}, u32[]{:S(2)}, u32[]{:S(2)}) collective-permute-start(f32[104,512]{1,0:T(8,128)} %get-tuple-element.16.own_ref.refs_0_), channel_id=1, source_target_pairs={{0,1},{1,0},{2,3},{3,2},{4,5},{5,4},{6,7},{7,6},{8,9},{9,8},{10,11... | collective-permute-start | bytes 638984 | tf_op jit(solution)/shard_map/ppermute | solution.py:279
  2.8 22.8 %collective-permute-start.3 = (f32[72,512]{1,0:T(8,128)}, f32[72,512]{1,0:T(8,128)S(1)}, u32[]{:S(2)}, u32[]{:S(2)}) collective-permute-start(f32[72,512]{1,0:T(8,128)} %get-tuple-element.17), channel_id=1, source_target_pairs={{0,6},{1,7},{2,4},{3,5},{4,2},{5,3},{6,0},{7,1},{8,14},{9,15},{10,... | collective-permute-start | bytes 442376 | tf_op jit(solution)/shard_map/ppermute | solution.py:279
  6.2 19.3 %collective-permute-start.2 = (f32[72,512]{1,0:T(8,128)}, f32[72,512]{1,0:T(8,128)S(1)}, u32[]{:S(2)}, u32[]{:S(2)}) collective-permute-start(f32[72,512]{1,0:T(8,128)} %get-tuple-element.17), channel_id=1, source_target_pairs={{0,4},{1,5},{2,6},{3,7},{4,0},{5,1},{6,2},{7,3},{8,12},{9,13},{10,... | collective-permute-start | bytes 442376 | tf_op jit(solution)/shard_map/ppermute | solution.py:279
  6.8 18.9 %collective-permute-start.1 = (f32[72,512]{1,0:T(8,128)}, f32[72,512]{1,0:T(8,128)S(1)}, u32[]{:S(2)}, u32[]{:S(2)}) collective-permute-start(f32[72,512]{1,0:T(8,128)} %get-tuple-element.17), channel_id=1, source_target_pairs={{0,2},{1,3},{2,0},{3,1},{4,6},{5,7},{6,4},{7,5},{8,10},{9,11},{10,... | collective-permute-start | bytes 442376 | tf_op jit(solution)/shard_map/ppermute | solution.py:279
  6.9 0.9 %copy-start = (f32[104,512]{1,0:T(8,128)S(1)}, f32[104,512]{1,0:T(8,128)}, u32[]{:S(2)}) copy-start(f32[104,512]{1,0:T(8,128)} %get-tuple-element.16.own_ref.refs_0_) | copy-start | bytes 638980
  25.6 4.7 %collective-permute-start.4 = (f32[3,72,512]{2,1,0:T(8,128)S(1)}, f32[3,72,512]{2,1,0:T(8,128)S(1)}, u32[]{:S(2)}, u32[]{:S(2)}) collective-permute-start(f32[3,72,512]{2,1,0:T(8,128)S(1)} %pad_maximum_fusion), channel_id=1, source_target_pairs={{0,1},{1,0},{2,3},{3,2},{4,5},{5,4},{6,7},{7,6},{8,9},{9,8},{10,11... | collective-permute-start | bytes 1327112 | tf_op jit(solution)/shard_map/ppermute | solution.py:279
  25.7 8.7 %collective-permute-start.5 = (f32[128,128]{1,0:T(8,128)S(1)}, f32[128,128]{1,0:T(8,128)S(1)}, u32[]{:S(2)}, u32[]{:S(2)}) collective-permute-start(f32[128,128]{1,0:T(8,128)S(1)} %get-tuple-element.25), channel_id=1, source_target_pairs={{0,8},{8,0},{16,24},{24,16},{1,9},{9,1},{17,25},{25,17},{2,10},{10... | collective-permute-start | bytes 196616 | tf_op jit(solution)/shard_map/ppermute | solution.py:279
  27.8 7.7 %collective-permute-start.6 = (f32[128,128]{1,0:T(8,128)S(1)}, f32[128,128]{1,0:T(8,128)S(1)}, u32[]{:S(2)}, u32[]{:S(2)}) collective-permute-start(f32[128,128]{1,0:T(8,128)S(1)} %get-tuple-element.26), channel_id=1, source_target_pairs={{0,16},{8,24},{16,0},{24,8},{1,17},{9,25},{17,1},{25,9},{2,18},{10... | collective-permute-start | bytes 196616 | tf_op jit(solution)/shard_map/ppermute | solution.py:279
  30.4 6.1 %collective-permute-start.7 = (f32[128,128]{1,0:T(8,128)S(1)}, f32[128,128]{1,0:T(8,128)S(1)}, u32[]{:S(2)}, u32[]{:S(2)}) collective-permute-start(f32[128,128]{1,0:T(8,128)S(1)} %get-tuple-element.27), channel_id=1, source_target_pairs={{0,24},{8,16},{16,8},{24,0},{1,25},{9,17},{17,9},{25,1},{2,26},{10... | collective-permute-start | bytes 196616 | tf_op jit(solution)/shard_map/ppermute | solution.py:279
  36.5 6.3 %collective-permute-start.10 = (f32[128,128]{1,0:T(8,128)S(1)}, f32[128,128]{1,0:T(8,128)S(1)}, u32[]{:S(2)}, u32[]{:S(2)}) collective-permute-start(f32[128,128]{1,0:T(8,128)S(1)} %group_sum.1.refs_0_), channel_id=1, source_target_pairs={{0,6},{1,7},{2,4},{3,5},{4,2},{5,3},{6,0},{7,1},{8,14},{9,15},{10,... | collective-permute-start | bytes 196616 | tf_op jit(solution)/shard_map/ppermute | solution.py:279
  39.0 4.3 %collective-permute-start.9 = (f32[128,128]{1,0:T(8,128)S(1)}, f32[128,128]{1,0:T(8,128)S(1)}, u32[]{:S(2)}, u32[]{:S(2)}) collective-permute-start(f32[128,128]{1,0:T(8,128)S(1)} %group_sum.1.refs_0_), channel_id=1, source_target_pairs={{0,4},{1,5},{2,6},{3,7},{4,0},{5,1},{6,2},{7,3},{8,12},{9,13},{10,... | collective-permute-start | bytes 196616 | tf_op jit(solution)/shard_map/ppermute | solution.py:279
  39.5 4.3 %collective-permute-start.8 = (f32[128,128]{1,0:T(8,128)S(1)}, f32[128,128]{1,0:T(8,128)S(1)}, u32[]{:S(2)}, u32[]{:S(2)}) collective-permute-start(f32[128,128]{1,0:T(8,128)S(1)} %group_sum.1.refs_0_), channel_id=1, source_target_pairs={{0,2},{1,3},{2,0},{3,1},{4,6},{5,7},{6,4},{7,5},{8,10},{9,11},{10,... | collective-permute-start | bytes 196616 | tf_op jit(solution)/shard_map/ppermute | solution.py:279
  42.8 2.5 %copy-start.1 = (f32[104,512]{1,0:T(8,128)S(1)}, f32[104,512]{1,0:T(8,128)}, u32[]{:S(2)}) copy-start(f32[104,512]{1,0:T(8,128)} %get-tuple-element.16.own_ref.refs_0_) | copy-start | bytes 638980
  44.0 0.7 %copy-start.5 = (s32[256]{0:T(256)S(1)}, s32[256]{0:T(256)}, u32[]{:S(2)}) copy-start(s32[256]{0:T(256)} %param.17) | copy-start | bytes 3076
  44.0 1.3 %collective-permute-start.11 = (f32[128,128]{1,0:T(8,128)S(1)}, f32[128,128]{1,0:T(8,128)S(1)}, u32[]{:S(2)}, u32[]{:S(2)}) collective-permute-start(f32[128,128]{1,0:T(8,128)S(1)} %set_coeffs.1.mine_ref), channel_id=1, source_target_pairs={{0,1},{1,0},{2,3},{3,2},{4,5},{5,4},{6,7},{7,6},{8,9},{9,8},{10,11... | collective-permute-start | bytes 196616 | tf_op jit(solution)/shard_map/ppermute | solution.py:279

commit v5 on v4

--- a/solution.py
+++ b/solution.py
@@ -13,7 +13,7 @@
 BF16 = jnp.bfloat16
 TILE = 512
 CHUNK = 512
-SLOTS = 4
+SLOTS = 8
 FIRST_PIVOTS = 36
 DEPTH = 256
 PAD = 8
@@ -121,7 +121,7 @@
 
 
 def moment_kernel(
-    groups, own_ref, other_ref, load_hbm, strike_hbm, notional_hbm, set_hbm, *refs
+    groups, start_ref, shocks_ref, weights_ref, other_ref, load_hbm, strike_hbm, notional_hbm, set_hbm, *refs
 ):
     outs = refs[:groups]
     *staged, sems, net_scr, states_scr, wide_scr, load_scr = refs[groups:]
@@ -137,9 +137,9 @@
     rows = 16
     load_scr[...] = jnp.zeros_like(load_scr)
     net_scr[...] = jnp.zeros_like(net_scr)
-    for number, ref in enumerate((own_ref, other_ref)):
-        shocks = (ref[factors : 2 * factors, :], ref[2 * factors + PAD :, :])
-        prepare(number, ref[:factors, :], shocks, weights_of(ref, factors), states_scr, wide_scr)
+    prepare(0, start_ref[...], shocks_ref[...], weights_ref[...].astype(F32), states_scr, wide_scr)
+    shocks = (other_ref[factors : 2 * factors, :], other_ref[2 * factors + PAD :, :])
+    prepare(1, other_ref[:factors, :], shocks, weights_of(other_ref, factors), states_scr, wide_scr)
     for move in moves:
         move.wait()
 
@@ -201,7 +201,9 @@
 
 
 def gram_kernel(factors, *refs):
-    blocks, gram_ref, mat_ref = refs[:-2], refs[-2], refs[-1]
+    *blocks, thresholds_ref, gram_ref, mat_ref, limits_ref = refs
+    limits = 0.25 * thresholds_ref[...].astype(F32)
+    limits_ref[...] = jnp.broadcast_to(limits, (limits_ref.shape[1], limits.shape[1])).T
     core = lax.axis_index("path") & 1
     wide = 2 * factors
     gram = jnp.zeros((wide, wide), F32)
@@ -247,44 +249,51 @@
     refs[-1][...] = mm_full(total, refs[-2][...])
 
 
-def exposure_kernel(factors, mine_ref, other_ref, limits_ref, *refs):
-    blocks, (exposure_ref, expected_ref) = refs[:-2], refs[-2:]
-    core = lax.axis_index("path") & 1
+def exposure_kernel(factors, own, coeff_ref, limits_ref, *refs):
+    date = (lax.axis_index("path") & 1) ^ (0 if own else 1)
+    *blocks, exposure_hbm, expected_ref, value_scr, sem = refs
+    if not own:
+        *blocks, first_ref, _ = blocks
     wide = 2 * factors
     paths = blocks[0].shape[1]
-    limits = 0.25 * limits_ref[...].astype(F32)
-    mine, other = mine_ref[...], other_ref[...]
-    coeffs = []
-    for packed in (pick(core, mine, other), pick(core, other, mine)):
-        hi, lo = split2(jnp.concatenate([packed[:, :wide], packed[:, wide:]], axis=0))
-        coeffs.append(jnp.concatenate([hi, hi, lo], axis=1))
-    sums = [jnp.zeros((limits.shape[0], 128), F32) for _ in coeffs]
+    limits = limits_ref[:, :1]
+    packed = coeff_ref[...]
+    hi, lo = split2(jnp.concatenate([packed[:, :wide], packed[:, wide:]], axis=0))
+    coeffs = jnp.concatenate([hi, hi, lo], axis=1)
+    move = pltpu.make_async_copy(value_scr, exposure_hbm.at[date], sem)
+    sums = jnp.zeros((limits.shape[0], 128), F32)
     total = jnp.zeros((1, 1), F32)
     for number, block in enumerate(path_blocks(blocks)):
         weight_row = weights_of(block, factors)
         total = total + jnp.sum(weight_row, keepdims=True)
-        for date, state in enumerate(states_of(block, factors)):
-            hi, lo = split2(basis_rows(state))
-            value = jnp.maximum(mm(coeffs[date], jnp.concatenate([hi, lo, hi], axis=0)) - limits, 0.0)
-            if number == 0:
-                exposure_ref[date] = value
-            product = value * weight_row
-            for c in range(paths // 128):
-                sums[date] = sums[date] + product[:, c * 128 : (c + 1) * 128]
-    for date, partial in enumerate(sums):
-        expected_ref[date : date + 1, :] = jnp.sum(partial.T, axis=0, keepdims=True) / total
+        hi, lo = split2(basis_rows(pick(date, *states_of(block, factors))))
+        value = jnp.maximum(mm(coeffs, jnp.concatenate([hi, lo, hi], axis=0)) - limits, 0.0)
+        if number == 0:
+            value_scr[...] = value
+            move.start()
+        product = value * weight_row
+        for c in range(paths // 128):
+            sums = sums + product[:, c * 128 : (c + 1) * 128]
+    mine = jnp.sum(sums.T, axis=0, keepdims=True) / total
+    if own:
+        expected_ref[...] = mine
+    else:
+        other = first_ref[...]
+        expected_ref[...] = jnp.concatenate([pick(date, mine, other), pick(date, other, mine)], axis=0)
+    move.wait()
 
 
 def swap(x, axis, away):
     return lax.ppermute(x, axis, [(i, i ^ away) for i in range(lax.axis_size(axis))])
 
 
-def run(kernel, name, out, specs, args, mib, scratch=(), gflops=0.0):
+def run(kernel, name, out, specs, args, mib, scratch=(), gflops=0.0, out_specs=None, aliases=None):
     return pl.pallas_call(
         kernel,
         out_shape=out,
         in_specs=specs,
-        out_specs=jax.tree.map(lambda _: VMEM, out),
+        out_specs=out_specs or jax.tree.map(lambda _: VMEM, out),
+        input_output_aliases=aliases or {},
         scratch_shapes=list(scratch),
         compiler_params=pltpu.CompilerParams(vmem_limit_bytes=int(mib * MIB)),
         cost_estimate=pl.CostEstimate(flops=int(gflops * 1e9), bytes_accessed=10**5, transcendentals=0),
@@ -309,7 +318,7 @@
     short, whole = run(
         pack_kernel, "pack_states",
         [shape(((dates - 1) * factors + factors + PAD, paths), F32), shape(((dates + 1) * factors + PAD, paths), F32)],
-        [SMEM] + [VMEM] * 3, (live_counts, start_t, shocks_t, weights_row), 58,
+        [SMEM] + [VMEM] * 3, (live_counts, start_t, shocks_t, weights_row), 58, (), 20.0,
     )
     other = swap(whole, "path", 1)
     across = [swap(short, "path", 2 * away) for away in range(1, ranks // 2)]
@@ -317,8 +326,8 @@
     strike_row, notional_row, set_row = strikes[None, :], notionals[None, :], trade_set[None, :]
     nets = run(
         functools.partial(moment_kernel, groups), "net_moments",
-        [shape((owned // 2, 2 * wide), F32)] * groups, [VMEM] * 2 + [HBM] * 4,
-        (whole, other, loadings, strike_row, notional_row, set_row), 52.75,
+        [shape((owned // 2, 2 * wide), F32)] * groups, [VMEM] * 4 + [HBM] * 4,
+        (start_t, shocks_t, weights_row, other, loadings, strike_row, notional_row, set_row), 52.75,
         [
             pltpu.VMEM((factors, slots), F32),
             pltpu.VMEM((1, slots), F32),
@@ -335,10 +344,11 @@
     *across, net = lax.optimization_barrier((*across, nets[0]))
     others = swap(jnp.stack(across), "path", 1)
     got = [swap(nets[away], "trade", away) for away in range(1, groups)]
-    blocks = (whole, other, *across, others)
-    gram, mat = run(
-        functools.partial(gram_kernel, factors), "gram_first_pivots", [shape((wide, wide), F32)] * 2,
-        [VMEM] * len(blocks), blocks, 8, (), 5.0,
+    blocks = (short, other, *across, others)
+    gram, mat, limits = run(
+        functools.partial(gram_kernel, factors), "gram_first_pivots",
+        [shape((wide, wide), F32)] * 2 + [shape((owned, 128), F32)],
+        [VMEM] * (len(blocks) + 1), (*blocks, thresholds[None, :]), 8, (), 5.0,
     )
     mat, net = lax.optimization_barrier((mat, net))
     inverse = run(
@@ -353,10 +363,16 @@
         [part] + got + [inverse], 4,
     )
     partner = swap(mine, "path", 1)
+    scratch = [pltpu.VMEM((owned, paths), F32), pltpu.SemaphoreType.DMA]
+    exposure, first = run(
+        functools.partial(exposure_kernel, factors, True), "own_date_exposure",
+        (shape((dates, owned, paths), F32), shape((1, owned), F32)), [VMEM] * (2 + len(blocks)),
+        (mine, limits, *blocks), 16, scratch, 2.0, (HBM, VMEM),
+    )
     exposure, expected = run(
-        functools.partial(exposure_kernel, factors), "set_exposure",
-        (shape((dates, owned, paths), F32), shape((dates, owned), F32)), [VMEM] * (3 + len(blocks)),
-        (mine, partner, thresholds[:, None], *blocks), 16, (), 2.0,
+        functools.partial(exposure_kernel, factors, False), "other_date_exposure",
+        (shape((dates, owned, paths), F32), shape((dates, owned), F32)), [VMEM] * (3 + len(blocks)) + [HBM],
+        (partner, limits, *blocks, first, exposure), 16, scratch, 2.0, (HBM, VMEM), {3 + len(blocks): 0},
     )
     return (exposure, expected)
 

time: 48.3 us -> 48.2 us (level)
  Pallas kernels: 29.2 us -> 30.6 us
  waiting for transfers between devices: 3.54 us -> 2.28 us
    pallas_call x7 -> x8, Pallas kernels: 29.2 us -> 30.6 us  [run(): pl.pallas_call(kernel, out_shape=out, in_specs=specs, out_specs=out_specs...]
    ppermute x12, waiting for transfers between devices: 3.54 us -> 2.28 us  [swap(): lax.ppermute(x, axis, [(i, i ^ away) for i in range(lax.axis_size(axis))])]
    unnamed x12 -> x16, local copies, waits for them, and re-layouts: 1.55 us -> 1.33 us
  transfers between devices with their start and end apart: 12 -> 12, of which waited for: 5 -> 4; matrix products, arithmetic and copies ran while one was open for 0% -> 0% of each run, Pallas kernels for 51% -> 55%
where the time goes in v5:
time: 48.2 us; the launch traced here: 47.9 us
  Pallas kernels  30.6 us (63%)
  starting transfers between devices  12.9 us (27%)
  waiting for transfers between devices  2.28 us (5%)
  local copies, waits for them, and re-layouts  1.33 us (3%)
  between operations  0.83 us (2%)
    pallas_call x8, Pallas kernels, run(): pl.pallas_call(kernel, out_shape=out, in_specs=specs, out_specs=out_specs...  30.6 us
    ppermute x12, starting transfers between devices, swap(): lax.ppermute(x, axis, [(i, i ^ away) for i in range(lax.axis_size(axis))])  12.9 us
    ppermute x12, waiting for transfers between devices, swap(): lax.ppermute(x, axis, [(i, i ^ away) for i in range(lax.axis_size(axis))])  2.28 us
    unnamed x16, local copies, waits for them, and re-layouts  1.33 us
  transfers between devices with their start and end apart: 12, of which 4 were waited for; matrix products, arithmetic and copies ran while one was open for 0% of the time, Pallas kernels for 55%

profile of v5, /device:TPU:0, one launch (start us, length us, event | category | flops | bytes accessed | tf_op | source)
XLA Modules:
  0.0 47.9 jit_solution(12734514346356620859)
XLA Ops:
  0.6 0.0 copy-start.1
  0.6 0.0 copy-start.2
  0.7 0.0 copy-start.3
  0.7 0.0 copy-start.4
  0.7 0.0 copy-start.5
  0.7 1.7 %pack_states.1 = (f32[72,512]{1,0:T(8,128)}, f32[104,512]{1,0:T(8,128)}) custom-call(s32[4]{0:T(128)} %counts_ref.1, f32[32,512]{1,0:T(8,128)} %bitcast.15, f32[2,32,512]{2,1,0:T(8,128)} %bitcast.13, s32[1,512]{1,0:T(1,128)} %bitcast.20), custom_call_target="tpu_custom_call" | custom-call | flops 20000000000 | bytes 100000 | tf_op jit(solution)/shard_map/pack_states/pallas_call | solution.py:291
  2.4 0.5 collective-permute-start
  2.9 3.4 %collective-permute-start.3 = (f32[72,512]{1,0:T(8,128)}, f32[72,512]{1,0:T(8,128)S(1)}, u32[]{:S(2)}, u32[]{:S(2)}) collective-permute-start(f32[72,512]{1,0:T(8,128)} %get-tuple-element.19.refs_0_), channel_id=1, source_target_pairs={{0,6},{1,7},{2,4},{3,5},{4,2},{5,3},{6,0},{7,1},{8,14},{9,15},{10,... | collective-permute-start | bytes 442376 | tf_op jit(solution)/shard_map/ppermute | solution.py:287
  6.3 0.5 %collective-permute-start.2 = (f32[72,512]{1,0:T(8,128)}, f32[72,512]{1,0:T(8,128)S(1)}, u32[]{:S(2)}, u32[]{:S(2)}) collective-permute-start(f32[72,512]{1,0:T(8,128)} %get-tuple-element.19.refs_0_), channel_id=1, source_target_pairs={{0,4},{1,5},{2,6},{3,7},{4,0},{5,1},{6,2},{7,3},{8,12},{9,13},{10,... | collective-permute-start | bytes 442376 | tf_op jit(solution)/shard_map/ppermute | solution.py:287
  6.8 0.1 collective-permute-start.1
  7.0 0.0 collective-permute-done.other_ref.refs_1_
  7.0 0.0 copy-start.6
  7.0 0.0 copy-done.1
  7.0 0.0 copy-done.2
  7.0 0.0 copy-done.3
  7.0 0.0 copy-done.4
  7.0 0.0 copy-done.5
  7.0 0.6 %copy-done.6 = s32[512]{0:T(512)S(1)} copy-done((s32[512]{0:T(512)S(1)}, s32[512]{0:T(512)}, u32[]{:S(2)}) %copy-start.6) | copy-done | bytes 2072
  7.6 17.5 %net_moments.1 = (f32[128,128]{1,0:T(8,128)S(1)}, f32[128,128]{1,0:T(8,128)S(1)}, f32[128,128]{1,0:T(8,128)S(1)}, f32[128,128]{1,0:T(8,128)S(1)}) custom-call(f32[32,512]{1,0:T(8,128)S(1)} %bitcast.16, f32[2,32,512]{2,1,0:T(8,128)S(1)} %bitcast.14, s32[1,512]{1,0:T(1,128)S(1)} %bitcast.21, f32[104,512]{1,0:T(8,128)S(1)} %collective-permute-done.other_ref.refs_1_, ...), custom_call_target="tpu_custom_call" | custom-call | flops 20000000000 | bytes 100000 | tf_op jit(solution)/shard_map/net_moments/pallas_call | solution.py:291
  25.1 0.0 collective-permute-done.3.refs_4_
  25.2 0.0 collective-permute-done.2.refs_3_
  25.2 0.0 collective-permute-done.1.refs_2_
  25.2 0.0 copy-start
  25.2 0.1 collective-permute-start.4
  25.3 2.1 %collective-permute-start.5 = (f32[128,128]{1,0:T(8,128)S(1)}, f32[128,128]{1,0:T(8,128)S(1)}, u32[]{:S(2)}, u32[]{:S(2)}) collective-permute-start(f32[128,128]{1,0:T(8,128)S(1)} %get-tuple-element.28), channel_id=1, source_target_pairs={{0,8},{8,0},{16,24},{24,16},{1,9},{9,1},{17,25},{25,17},{2,10},{10... | collective-permute-start | bytes 196616 | tf_op jit(solution)/shard_map/ppermute | solution.py:287
  27.4 2.6 %collective-permute-start.6 = (f32[128,128]{1,0:T(8,128)S(1)}, f32[128,128]{1,0:T(8,128)S(1)}, u32[]{:S(2)}, u32[]{:S(2)}) collective-permute-start(f32[128,128]{1,0:T(8,128)S(1)} %get-tuple-element.29), channel_id=1, source_target_pairs={{0,16},{8,24},{16,0},{24,8},{1,17},{9,25},{17,1},{25,9},{2,18},{10... | collective-permute-start | bytes 196616 | tf_op jit(solution)/shard_map/ppermute | solution.py:287
  29.9 0.0 copy-start.7
  29.9 0.0 collective-permute-start.7
  29.9 0.0 collective-permute-done.4.refs_5_
  30.0 0.0 copy-done
  30.0 0.7 %copy-done.7 = s32[256]{0:T(256)S(1)} copy-done((s32[256]{0:T(256)S(1)}, s32[256]{0:T(256)}, u32[]{:S(2)}) %copy-start.7) | copy-done | bytes 1048
  30.6 4.1 %gram_first_pivots.1 = (f32[64,64]{1,0:T(8,128)S(1)}, f32[64,64]{1,0:T(8,128)S(1)}, f32[256,128]{1,0:T(8,128)S(1)}) custom-call(f32[72,512]{1,0:T(8,128)S(1)} %copy-done, f32[104,512]{1,0:T(8,128)S(1)} %collective-permute-done.other_ref.refs_1_, f32[72,512]{1,0:T(8,128)S(1)} %collective-permute-done.1.refs_2_, f32[72,512]{1,0:T(8,128)S(1)} %collective-permute-done.2.refs_3_, ...), custom_call_target="tpu_custom_call" | custom-call | flops 5000000000 | bytes 100000 | tf_op jit(solution)/shard_map/gram_first_pivots/pallas_call | solution.py:291
  34.8 0.0 collective-permute-done.5.refs_1_
  34.8 0.3 collective-permute-done.6.refs_2_
  35.1 1.0 %collective-permute-done.7.refs_3_ = f32[128,128]{1,0:T(8,128)S(1)} collective-permute-done((f32[128,128]{1,0:T(8,128)S(1)}, f32[128,128]{1,0:T(8,128)S(1)}, u32[]{:S(2)}, u32[]{:S(2)}) %collective-permute-start.7) | collective-permute-done | bytes 65568 | tf_op jit(solution)/shard_map/ppermute | solution.py:287
  36.1 2.5 %collective-permute-start.10 = (f32[128,128]{1,0:T(8,128)S(1)}, f32[128,128]{1,0:T(8,128)S(1)}, u32[]{:S(2)}, u32[]{:S(2)}) collective-permute-start(f32[128,128]{1,0:T(8,128)S(1)} %group_sum.1.refs_0_), channel_id=1, source_target_pairs={{0,6},{1,7},{2,4},{3,5},{4,2},{5,3},{6,0},{7,1},{8,14},{9,15},{10,... | collective-permute-start | bytes 196616 | tf_op jit(solution)/shard_map/ppermute | solution.py:287
  38.6 0.5 %collective-permute-start.9 = (f32[128,128]{1,0:T(8,128)S(1)}, f32[128,128]{1,0:T(8,128)S(1)}, u32[]{:S(2)}, u32[]{:S(2)}) collective-permute-start(f32[128,128]{1,0:T(8,128)S(1)} %group_sum.1.refs_0_), channel_id=1, source_target_pairs={{0,4},{1,5},{2,6},{3,7},{4,0},{5,1},{6,2},{7,3},{8,12},{9,13},{10,... | collective-permute-start | bytes 196616 | tf_op jit(solution)/shard_map/ppermute | solution.py:287
  39.1 0.5 %collective-permute-start.8 = (f32[128,128]{1,0:T(8,128)S(1)}, f32[128,128]{1,0:T(8,128)S(1)}, u32[]{:S(2)}, u32[]{:S(2)}) collective-permute-start(f32[128,128]{1,0:T(8,128)S(1)} %group_sum.1.refs_0_), channel_id=1, source_target_pairs={{0,2},{1,3},{2,0},{3,1},{4,6},{5,7},{6,4},{7,5},{8,10},{9,11},{10,... | collective-permute-start | bytes 196616 | tf_op jit(solution)/shard_map/ppermute | solution.py:287
  39.6 2.8 %gram_inverse.1.refs_4_ = f32[128,128]{1,0:T(8,128)S(1)} custom-call(f32[64,64]{1,0:T(8,128)S(1)} %get-tuple-element.31.gram_ref, f32[64,64]{1,0:T(8,128)S(1)} %get-tuple-element.32.mat_ref), custom_call_target="tpu_custom_call" | custom-call | flops 3000000000 | bytes 100000 | tf_op jit(solution)/shard_map/gram_inverse/pallas_call | solution.py:291
  42.4 0.0 collective-permute-done.10.refs_3_
  42.4 0.5 collective-permute-done.9.refs_2_
  42.9 0.5 %collective-permute-done.8.refs_1_ = f32[128,128]{1,0:T(8,128)S(1)} collective-permute-done((f32[128,128]{1,0:T(8,128)S(1)}, f32[128,128]{1,0:T(8,128)S(1)}, u32[]{:S(2)}, u32[]{:S(2)}) %collective-permute-start.8) | collective-permute-done | bytes 65568 | tf_op jit(solution)/shard_map/ppermute | solution.py:287
  43.4 0.2 set_coeffs.1.coeff_ref
  43.6 0.1 collective-permute-start.11
  43.7 1.8 %own_date_exposure.1 = (f32[2,256,512]{2,1,0:T(8,128)}, f32[1,256]{1,0:T(1,128)S(1)}) custom-call(f32[128,128]{1,0:T(8,128)S(1)} %set_coeffs.1.coeff_ref, f32[256,128]{1,0:T(8,128)S(1)} %get-tuple-element.33.limits_ref, f32[72,512]{1,0:T(8,128)S(1)} %copy-done, f32[104,512]{1,0:T(8,128)S(1)} %collective-permute-done.other_ref.refs_1_, ...), custom_call_target="tpu_custom_call" | custom-call | flops 2000000000 | bytes 100000 | tf_op jit(solution)/shard_map/own_date_exposure/pallas_call | solution.py:291
  45.5 0.0 collective-permute-done.11.coeff_ref
  45.5 2.4 %other_date_exposure.1 = (f32[2,256,512]{2,1,0:T(8,128)}, f32[2,256]{1,0:T(2,128)}) custom-call(f32[128,128]{1,0:T(8,128)S(1)} %collective-permute-done.11.coeff_ref, f32[256,128]{1,0:T(8,128)S(1)} %get-tuple-element.33.limits_ref, f32[72,512]{1,0:T(8,128)S(1)} %copy-done, ...), custom_call_target="tpu_custom_call", output_to_operand_aliasing={{0}: (9, {})} | custom-call | flops 2000000000 | bytes 100000 | tf_op jit(solution)/shard_map/other_date_exposure/pallas_call | solution.py:291
  (2 shorter events, 0.0 us)
Async XLA Ops:
  0.6 6.3 %copy-start.1 = (f32[2,512,32]{1,2,0:T(8,128)S(1)}, f32[2,512,32]{1,2,0:T(8,128)}, u32[]{:S(2)}) copy-start(f32[2,512,32]{1,2,0:T(8,128)} %param.10) | copy-start | bytes 393220
  0.6 6.3 %copy-start.2 = (f32[512,32]{0,1:T(8,128)S(1)}, f32[512,32]{0,1:T(8,128)}, u32[]{:S(2)}) copy-start(f32[512,32]{0,1:T(8,128)} %param.9) | copy-start | bytes 196612
  0.7 6.3 %copy-start.3 = (f32[8192]{0:T(1024)S(1)}, f32[8192]{0:T(1024)}, u32[]{:S(2)}) copy-start(f32[8192]{0:T(1024)} %param.12) | copy-start | bytes 98308
  0.7 6.3 %copy-start.4 = (f32[8192]{0:T(1024)S(1)}, f32[8192]{0:T(1024)}, u32[]{:S(2)}) copy-start(f32[8192]{0:T(1024)} %param.13) | copy-start | bytes 98308
  0.7 6.3 %copy-start.5 = (s32[8192]{0:T(1024)S(1)}, s32[8192]{0:T(1024)}, u32[]{:S(2)}) copy-start(s32[8192]{0:T(1024)} %param.14) | copy-start | bytes 98308
  2.4 4.5 %collective-permute-start = (f32[104,512]{1,0:T(8,128)}, f32[104,512]{1,0:T(8,128)S(1)}, u32[]{:S(2)}, u32[]{:S(2)}) collective-permute-start(f32[104,512]{1,0:T(8,128)} %get-tuple-element.20), channel_id=1, source_target_pairs={{0,1},{1,0},{2,3},{3,2},{4,5},{5,4},{6,7},{7,6},{8,9},{9,8},{10,11... | collective-permute-start | bytes 638984 | tf_op jit(solution)/shard_map/ppermute | solution.py:287
  2.9 22.3 %collective-permute-start.3 = (f32[72,512]{1,0:T(8,128)}, f32[72,512]{1,0:T(8,128)S(1)}, u32[]{:S(2)}, u32[]{:S(2)}) collective-permute-start(f32[72,512]{1,0:T(8,128)} %get-tuple-element.19.refs_0_), channel_id=1, source_target_pairs={{0,6},{1,7},{2,4},{3,5},{4,2},{5,3},{6,0},{7,1},{8,14},{9,15},{10,... | collective-permute-start | bytes 442376 | tf_op jit(solution)/shard_map/ppermute | solution.py:287
  6.3 18.8 %collective-permute-start.2 = (f32[72,512]{1,0:T(8,128)}, f32[72,512]{1,0:T(8,128)S(1)}, u32[]{:S(2)}, u32[]{:S(2)}) collective-permute-start(f32[72,512]{1,0:T(8,128)} %get-tuple-element.19.refs_0_), channel_id=1, source_target_pairs={{0,4},{1,5},{2,6},{3,7},{4,0},{5,1},{6,2},{7,3},{8,12},{9,13},{10,... | collective-permute-start | bytes 442376 | tf_op jit(solution)/shard_map/ppermute | solution.py:287
  6.8 18.3 %collective-permute-start.1 = (f32[72,512]{1,0:T(8,128)}, f32[72,512]{1,0:T(8,128)S(1)}, u32[]{:S(2)}, u32[]{:S(2)}) collective-permute-start(f32[72,512]{1,0:T(8,128)} %get-tuple-element.19.refs_0_), channel_id=1, source_target_pairs={{0,2},{1,3},{2,0},{3,1},{4,6},{5,7},{6,4},{7,5},{8,10},{9,11},{10,... | collective-permute-start | bytes 442376 | tf_op jit(solution)/shard_map/ppermute | solution.py:287
  7.0 0.7 %copy-start.6 = (s32[512]{0:T(512)S(1)}, s32[512]{0:T(512)}, u32[]{:S(2)}) copy-start(s32[512]{0:T(512)} %param.16) | copy-start | bytes 6148
  25.2 4.8 %copy-start = (f32[72,512]{1,0:T(8,128)S(1)}, f32[72,512]{1,0:T(8,128)}, u32[]{:S(2)}) copy-start(f32[72,512]{1,0:T(8,128)} %get-tuple-element.19.refs_0_) | copy-start | bytes 442372
  25.2 4.7 %collective-permute-start.4 = (f32[3,72,512]{2,1,0:T(8,128)S(1)}, f32[3,72,512]{2,1,0:T(8,128)S(1)}, u32[]{:S(2)}, u32[]{:S(2)}) collective-permute-start(f32[3,72,512]{2,1,0:T(8,128)S(1)} %pad_maximum_fusion), channel_id=1, source_target_pairs={{0,1},{1,0},{2,3},{3,2},{4,5},{5,4},{6,7},{7,6},{8,9},{9,8},{10,11... | collective-permute-start | bytes 1327112 | tf_op jit(solution)/shard_map/ppermute | solution.py:287
  25.3 9.5 %collective-permute-start.5 = (f32[128,128]{1,0:T(8,128)S(1)}, f32[128,128]{1,0:T(8,128)S(1)}, u32[]{:S(2)}, u32[]{:S(2)}) collective-permute-start(f32[128,128]{1,0:T(8,128)S(1)} %get-tuple-element.28), channel_id=1, source_target_pairs={{0,8},{8,0},{16,24},{24,16},{1,9},{9,1},{17,25},{25,17},{2,10},{10... | collective-permute-start | bytes 196616 | tf_op jit(solution)/shard_map/ppermute | solution.py:287
  27.4 7.7 %collective-permute-start.6 = (f32[128,128]{1,0:T(8,128)S(1)}, f32[128,128]{1,0:T(8,128)S(1)}, u32[]{:S(2)}, u32[]{:S(2)}) collective-permute-start(f32[128,128]{1,0:T(8,128)S(1)} %get-tuple-element.29), channel_id=1, source_target_pairs={{0,16},{8,24},{16,0},{24,8},{1,17},{9,25},{17,1},{25,9},{2,18},{10... | collective-permute-start | bytes 196616 | tf_op jit(solution)/shard_map/ppermute | solution.py:287
  29.9 0.7 %copy-start.7 = (s32[256]{0:T(256)S(1)}, s32[256]{0:T(256)}, u32[]{:S(2)}) copy-start(s32[256]{0:T(256)} %param.17) | copy-start | bytes 3076
  29.9 6.1 %collective-permute-start.7 = (f32[128,128]{1,0:T(8,128)S(1)}, f32[128,128]{1,0:T(8,128)S(1)}, u32[]{:S(2)}, u32[]{:S(2)}) collective-permute-start(f32[128,128]{1,0:T(8,128)S(1)} %get-tuple-element.30), channel_id=1, source_target_pairs={{0,24},{8,16},{16,8},{24,0},{1,25},{9,17},{17,9},{25,1},{2,26},{10... | collective-permute-start | bytes 196616 | tf_op jit(solution)/shard_map/ppermute | solution.py:287
  36.1 6.3 %collective-permute-start.10 = (f32[128,128]{1,0:T(8,128)S(1)}, f32[128,128]{1,0:T(8,128)S(1)}, u32[]{:S(2)}, u32[]{:S(2)}) collective-permute-start(f32[128,128]{1,0:T(8,128)S(1)} %group_sum.1.refs_0_), channel_id=1, source_target_pairs={{0,6},{1,7},{2,4},{3,5},{4,2},{5,3},{6,0},{7,1},{8,14},{9,15},{10,... | collective-permute-start | bytes 196616 | tf_op jit(solution)/shard_map/ppermute | solution.py:287
  38.6 4.3 %collective-permute-start.9 = (f32[128,128]{1,0:T(8,128)S(1)}, f32[128,128]{1,0:T(8,128)S(1)}, u32[]{:S(2)}, u32[]{:S(2)}) collective-permute-start(f32[128,128]{1,0:T(8,128)S(1)} %group_sum.1.refs_0_), channel_id=1, source_target_pairs={{0,4},{1,5},{2,6},{3,7},{4,0},{5,1},{6,2},{7,3},{8,12},{9,13},{10,... | collective-permute-start | bytes 196616 | tf_op jit(solution)/shard_map/ppermute | solution.py:287
  39.1 4.3 %collective-permute-start.8 = (f32[128,128]{1,0:T(8,128)S(1)}, f32[128,128]{1,0:T(8,128)S(1)}, u32[]{:S(2)}, u32[]{:S(2)}) collective-permute-start(f32[128,128]{1,0:T(8,128)S(1)} %group_sum.1.refs_0_), channel_id=1, source_target_pairs={{0,2},{1,3},{2,0},{3,1},{4,6},{5,7},{6,4},{7,5},{8,10},{9,11},{10,... | collective-permute-start | bytes 196616 | tf_op jit(solution)/shard_map/ppermute | solution.py:287
  43.6 1.9 %collective-permute-start.11 = (f32[128,128]{1,0:T(8,128)S(1)}, f32[128,128]{1,0:T(8,128)S(1)}, u32[]{:S(2)}, u32[]{:S(2)}) collective-permute-start(f32[128,128]{1,0:T(8,128)S(1)} %set_coeffs.1.coeff_ref), channel_id=1, source_target_pairs={{0,1},{1,0},{2,3},{3,2},{4,5},{5,4},{6,7},{7,6},{8,9},{9,8},{10,11... | collective-permute-start | bytes 196616 | tf_op jit(solution)/shard_map/ppermute | solution.py:287

commit v6 on v5

--- a/solution.py
+++ b/solution.py
@@ -13,7 +13,7 @@
 BF16 = jnp.bfloat16
 TILE = 512
 CHUNK = 512
-SLOTS = 8
+SLOTS = 4
 FIRST_PIVOTS = 36
 DEPTH = 256
 PAD = 8
@@ -179,7 +179,7 @@
                     moment = None
         return carry
 
-    lax.fori_loop(0, load_ref.shape[1] // (SLOTS * TILE), step, 0)
+    lax.fori_loop(0, (jnp.max(filled) + SLOTS * TILE - 1) // (SLOTS * TILE), step, 0)
     wide = net_scr.shape[1] // (2 * groups)
     half = owned // 2
     for away, out in enumerate(outs):
@@ -249,51 +249,49 @@
     refs[-1][...] = mm_full(total, refs[-2][...])
 
 
-def exposure_kernel(factors, own, coeff_ref, limits_ref, *refs):
-    date = (lax.axis_index("path") & 1) ^ (0 if own else 1)
-    *blocks, exposure_hbm, expected_ref, value_scr, sem = refs
-    if not own:
-        *blocks, first_ref, _ = blocks
+def exposure_kernel(factors, mine_ref, other_ref, limits_ref, *refs):
+    *blocks, exposure_hbm, expected_ref, value_scr, sems = refs
+    core = lax.axis_index("path") & 1
     wide = 2 * factors
     paths = blocks[0].shape[1]
     limits = limits_ref[:, :1]
-    packed = coeff_ref[...]
-    hi, lo = split2(jnp.concatenate([packed[:, :wide], packed[:, wide:]], axis=0))
-    coeffs = jnp.concatenate([hi, hi, lo], axis=1)
-    move = pltpu.make_async_copy(value_scr, exposure_hbm.at[date], sem)
-    sums = jnp.zeros((limits.shape[0], 128), F32)
+    results, moves = [], []
     total = jnp.zeros((1, 1), F32)
-    for number, block in enumerate(path_blocks(blocks)):
-        weight_row = weights_of(block, factors)
-        total = total + jnp.sum(weight_row, keepdims=True)
-        hi, lo = split2(basis_rows(pick(date, *states_of(block, factors))))
-        value = jnp.maximum(mm(coeffs, jnp.concatenate([hi, lo, hi], axis=0)) - limits, 0.0)
-        if number == 0:
-            value_scr[...] = value
-            move.start()
-        product = value * weight_row
-        for c in range(paths // 128):
-            sums = sums + product[:, c * 128 : (c + 1) * 128]
-    mine = jnp.sum(sums.T, axis=0, keepdims=True) / total
-    if own:
-        expected_ref[...] = mine
-    else:
-        other = first_ref[...]
-        expected_ref[...] = jnp.concatenate([pick(date, mine, other), pick(date, other, mine)], axis=0)
-    move.wait()
+    for block in path_blocks(blocks):
+        total = total + jnp.sum(weights_of(block, factors), keepdims=True)
+    for turn, ref in enumerate((mine_ref, other_ref)):
+        date = core ^ turn
+        packed = ref[...]
+        hi, lo = split2(jnp.concatenate([packed[:, :wide], packed[:, wide:]], axis=0))
+        coeffs = jnp.concatenate([hi, hi, lo], axis=1)
+        sums = jnp.zeros((limits.shape[0], 128), F32)
+        for number, block in enumerate(path_blocks(blocks)):
+            hi, lo = split2(basis_rows(pick(date, *states_of(block, factors))))
+            value = jnp.maximum(mm(coeffs, jnp.concatenate([hi, lo, hi], axis=0)) - limits, 0.0)
+            if number == 0:
+                value_scr[turn] = value
+                moves.append(pltpu.make_async_copy(value_scr.at[turn], exposure_hbm.at[date], sems.at[turn]))
+                moves[turn].start()
+            product = value * weights_of(block, factors)
+            for c in range(paths // 128):
+                sums = sums + product[:, c * 128 : (c + 1) * 128]
+        results.append(jnp.sum(sums.T, axis=0, keepdims=True) / total)
+    mine, other = results
+    expected_ref[...] = jnp.concatenate([pick(core, mine, other), pick(core, other, mine)], axis=0)
+    for move in moves:
+        move.wait()
 
 
 def swap(x, axis, away):
     return lax.ppermute(x, axis, [(i, i ^ away) for i in range(lax.axis_size(axis))])
 
 
-def run(kernel, name, out, specs, args, mib, scratch=(), gflops=0.0, out_specs=None, aliases=None):
+def run(kernel, name, out, specs, args, mib, scratch=(), gflops=0.0, out_specs=None):
     return pl.pallas_call(
         kernel,
         out_shape=out,
         in_specs=specs,
         out_specs=out_specs or jax.tree.map(lambda _: VMEM, out),
-        input_output_aliases=aliases or {},
         scratch_shapes=list(scratch),
         compiler_params=pltpu.CompilerParams(vmem_limit_bytes=int(mib * MIB)),
         cost_estimate=pl.CostEstimate(flops=int(gflops * 1e9), bytes_accessed=10**5, transcendentals=0),
@@ -363,16 +361,11 @@
         [part] + got + [inverse], 4,
     )
     partner = swap(mine, "path", 1)
-    scratch = [pltpu.VMEM((owned, paths), F32), pltpu.SemaphoreType.DMA]
-    exposure, first = run(
-        functools.partial(exposure_kernel, factors, True), "own_date_exposure",
-        (shape((dates, owned, paths), F32), shape((1, owned), F32)), [VMEM] * (2 + len(blocks)),
-        (mine, limits, *blocks), 16, scratch, 2.0, (HBM, VMEM),
-    )
     exposure, expected = run(
-        functools.partial(exposure_kernel, factors, False), "other_date_exposure",
-        (shape((dates, owned, paths), F32), shape((dates, owned), F32)), [VMEM] * (3 + len(blocks)) + [HBM],
-        (partner, limits, *blocks, first, exposure), 16, scratch, 2.0, (HBM, VMEM), {3 + len(blocks): 0},
+        functools.partial(exposure_kernel, factors), "set_exposure",
+        (shape((dates, owned, paths), F32), shape((dates, owned), F32)), [VMEM] * (3 + len(blocks)),
+        (mine, partner, limits, *blocks), 16,
+        [pltpu.VMEM((dates, owned, paths), F32), pltpu.SemaphoreType.DMA((dates,))], 2.0, (HBM, VMEM),
     )
     return (exposure, expected)
 

time: 48.2 us -> 48.7 us (1.010)
  Pallas kernels: 30.6 us -> 26.1 us
  starting transfers between devices: 12.9 us -> 16.8 us
  waiting for transfers between devices: 2.28 us -> 3.97 us
  local copies, waits for them, and re-layouts: 1.33 us -> 0.67 us
    pallas_call x8 -> x7, Pallas kernels: 30.6 us -> 26.1 us  [run(): pl.pallas_call(kernel, out_shape=out, in_specs=specs, out_specs=out_specs...]
    ppermute x12, starting transfers between devices: 12.9 us -> 16.8 us  [swap(): lax.ppermute(x, axis, [(i, i ^ away) for i in range(lax.axis_size(axis))])]
    ppermute x12, waiting for transfers between devices: 2.28 us -> 3.97 us  [swap(): lax.ppermute(x, axis, [(i, i ^ away) for i in range(lax.axis_size(axis))])]
    unnamed x16, local copies, waits for them, and re-layouts: 1.33 us -> 0.67 us
  transfers between devices with their start and end apart: 12 -> 12, of which waited for: 4 -> 4; matrix products, arithmetic and copies ran while one was open for 0% -> 0% of each run, Pallas kernels for 55% -> 43%
where the time goes in v6:
time: 48.7 us; the launch traced here: 48.4 us
  Pallas kernels  26.1 us (54%)
  starting transfers between devices  16.8 us (34%)
  waiting for transfers between devices  3.97 us (8%)
  between operations  0.81 us (2%)
  local copies, waits for them, and re-layouts  0.67 us (1%)
    pallas_call x7, Pallas kernels, run(): pl.pallas_call(kernel, out_shape=out, in_specs=specs, out_specs=out_specs...  26.1 us
    ppermute x12, starting transfers between devices, swap(): lax.ppermute(x, axis, [(i, i ^ away) for i in range(lax.axis_size(axis))])  16.8 us
    ppermute x12, waiting for transfers between devices, swap(): lax.ppermute(x, axis, [(i, i ^ away) for i in range(lax.axis_size(axis))])  3.97 us
  transfers between devices with their start and end apart: 12, of which 4 were waited for; matrix products, arithmetic and copies ran while one was open for 0% of the time, Pallas kernels for 43%

profile of v6, /device:TPU:0, one launch (start us, length us, event | category | flops | bytes accessed | tf_op | source)
XLA Modules:
  0.0 48.4 jit_solution(6404684705908662678)
XLA Ops:
  0.6 0.0 copy-start.1
  0.6 0.0 copy-start.2
  0.7 0.0 copy-start.3
  0.7 0.0 copy-start.4
  0.7 0.0 copy-start.5
  0.7 1.7 %pack_states.1 = (f32[72,512]{1,0:T(8,128)}, f32[104,512]{1,0:T(8,128)}) custom-call(s32[4]{0:T(128)} %counts_ref.1, f32[32,512]{1,0:T(8,128)} %bitcast.15, f32[2,32,512]{2,1,0:T(8,128)} %bitcast.13, s32[1,512]{1,0:T(1,128)} %bitcast.20), custom_call_target="tpu_custom_call" | custom-call | flops 20000000000 | bytes 100000 | tf_op jit(solution)/shard_map/pack_states/pallas_call | solution.py:290
  2.4 0.5 collective-permute-start
  2.9 3.4 %collective-permute-start.3 = (f32[72,512]{1,0:T(8,128)}, f32[72,512]{1,0:T(8,128)S(1)}, u32[]{:S(2)}, u32[]{:S(2)}) collective-permute-start(f32[72,512]{1,0:T(8,128)} %get-tuple-element.17.refs_0_), channel_id=1, source_target_pairs={{0,6},{1,7},{2,4},{3,5},{4,2},{5,3},{6,0},{7,1},{8,14},{9,15},{10,... | collective-permute-start | bytes 442376 | tf_op jit(solution)/shard_map/ppermute | solution.py:286
  6.3 0.5 %collective-permute-start.2 = (f32[72,512]{1,0:T(8,128)}, f32[72,512]{1,0:T(8,128)S(1)}, u32[]{:S(2)}, u32[]{:S(2)}) collective-permute-start(f32[72,512]{1,0:T(8,128)} %get-tuple-element.17.refs_0_), channel_id=1, source_target_pairs={{0,4},{1,5},{2,6},{3,7},{4,0},{5,1},{6,2},{7,3},{8,12},{9,13},{10,... | collective-permute-start | bytes 442376 | tf_op jit(solution)/shard_map/ppermute | solution.py:286
  6.8 0.1 collective-permute-start.1
  7.0 0.0 collective-permute-done.other_ref.refs_1_
  7.0 0.0 copy-start.6
  7.0 0.0 copy-done.1
  7.0 0.0 copy-done.2
  7.0 0.0 copy-done.3
  7.0 0.0 copy-done.4
  7.0 0.0 copy-done.5
  7.0 0.6 %copy-done.6 = s32[512]{0:T(512)S(1)} copy-done((s32[512]{0:T(512)S(1)}, s32[512]{0:T(512)}, u32[]{:S(2)}) %copy-start.6) | copy-done | bytes 2072
  7.6 13.8 %net_moments.1 = (f32[128,128]{1,0:T(8,128)S(1)}, f32[128,128]{1,0:T(8,128)S(1)}, f32[128,128]{1,0:T(8,128)S(1)}, f32[128,128]{1,0:T(8,128)S(1)}) custom-call(f32[32,512]{1,0:T(8,128)S(1)} %bitcast.16, f32[2,32,512]{2,1,0:T(8,128)S(1)} %bitcast.14, s32[1,512]{1,0:T(1,128)S(1)} %bitcast.21, f32[104,512]{1,0:T(8,128)S(1)} %collective-permute-done.other_ref.refs_1_, ...), custom_call_target="tpu_custom_call" | custom-call | flops 20000000000 | bytes 100000 | tf_op jit(solution)/shard_map/net_moments/pallas_call | solution.py:290
  21.4 0.0 collective-permute-done.3.refs_4_
  21.4 0.0 collective-permute-done.2.refs_3_
  21.5 0.0 collective-permute-done.1.refs_2_
  21.5 0.0 copy-start
  21.5 0.1 collective-permute-start.4
  21.6 6.1 %collective-permute-start.5 = (f32[128,128]{1,0:T(8,128)S(1)}, f32[128,128]{1,0:T(8,128)S(1)}, u32[]{:S(2)}, u32[]{:S(2)}) collective-permute-start(f32[128,128]{1,0:T(8,128)S(1)} %get-tuple-element.26), channel_id=1, source_target_pairs={{0,8},{8,0},{16,24},{24,16},{1,9},{9,1},{17,25},{25,17},{2,10},{10... | collective-permute-start | bytes 196616 | tf_op jit(solution)/shard_map/ppermute | solution.py:286
  27.7 1.1 %collective-permute-start.6 = (f32[128,128]{1,0:T(8,128)S(1)}, f32[128,128]{1,0:T(8,128)S(1)}, u32[]{:S(2)}, u32[]{:S(2)}) collective-permute-start(f32[128,128]{1,0:T(8,128)S(1)} %get-tuple-element.27), channel_id=1, source_target_pairs={{0,16},{8,24},{16,0},{24,8},{1,17},{9,25},{17,1},{25,9},{2,18},{10... | collective-permute-start | bytes 196616 | tf_op jit(solution)/shard_map/ppermute | solution.py:286
  28.8 0.0 copy-start.7
  28.8 1.4 %collective-permute-start.7 = (f32[128,128]{1,0:T(8,128)S(1)}, f32[128,128]{1,0:T(8,128)S(1)}, u32[]{:S(2)}, u32[]{:S(2)}) collective-permute-start(f32[128,128]{1,0:T(8,128)S(1)} %get-tuple-element.28), channel_id=1, source_target_pairs={{0,24},{8,16},{16,8},{24,0},{1,25},{9,17},{17,9},{25,1},{2,26},{10... | collective-permute-start | bytes 196616 | tf_op jit(solution)/shard_map/ppermute | solution.py:286
  30.1 0.0 collective-permute-done.4.refs_5_
  30.1 0.0 copy-done
  30.1 0.0 copy-done.7
  30.2 4.1 %gram_first_pivots.1 = (f32[64,64]{1,0:T(8,128)S(1)}, f32[64,64]{1,0:T(8,128)S(1)}, f32[256,128]{1,0:T(8,128)S(1)}) custom-call(f32[72,512]{1,0:T(8,128)S(1)} %copy-done, f32[104,512]{1,0:T(8,128)S(1)} %collective-permute-done.other_ref.refs_1_, f32[72,512]{1,0:T(8,128)S(1)} %collective-permute-done.1.refs_2_, f32[72,512]{1,0:T(8,128)S(1)} %collective-permute-done.2.refs_3_, ...), custom_call_target="tpu_custom_call" | custom-call | flops 5000000000 | bytes 100000 | tf_op jit(solution)/shard_map/gram_first_pivots/pallas_call | solution.py:290
  34.3 0.0 collective-permute-done.5.refs_1_
  34.3 1.8 %collective-permute-done.6.refs_2_ = f32[128,128]{1,0:T(8,128)S(1)} collective-permute-done((f32[128,128]{1,0:T(8,128)S(1)}, f32[128,128]{1,0:T(8,128)S(1)}, u32[]{:S(2)}, u32[]{:S(2)}) %collective-permute-start.6) | collective-permute-done | bytes 65568 | tf_op jit(solution)/shard_map/ppermute | solution.py:286
  36.1 0.0 collective-permute-done.7.refs_3_
  36.1 2.5 %collective-permute-start.10 = (f32[128,128]{1,0:T(8,128)S(1)}, f32[128,128]{1,0:T(8,128)S(1)}, u32[]{:S(2)}, u32[]{:S(2)}) collective-permute-start(f32[128,128]{1,0:T(8,128)S(1)} %group_sum.1.refs_0_), channel_id=1, source_target_pairs={{0,6},{1,7},{2,4},{3,5},{4,2},{5,3},{6,0},{7,1},{8,14},{9,15},{10,... | collective-permute-start | bytes 196616 | tf_op jit(solution)/shard_map/ppermute | solution.py:286
  38.6 0.5 %collective-permute-start.9 = (f32[128,128]{1,0:T(8,128)S(1)}, f32[128,128]{1,0:T(8,128)S(1)}, u32[]{:S(2)}, u32[]{:S(2)}) collective-permute-start(f32[128,128]{1,0:T(8,128)S(1)} %group_sum.1.refs_0_), channel_id=1, source_target_pairs={{0,4},{1,5},{2,6},{3,7},{4,0},{5,1},{6,2},{7,3},{8,12},{9,13},{10,... | collective-permute-start | bytes 196616 | tf_op jit(solution)/shard_map/ppermute | solution.py:286
  39.1 0.6 %collective-permute-start.8 = (f32[128,128]{1,0:T(8,128)S(1)}, f32[128,128]{1,0:T(8,128)S(1)}, u32[]{:S(2)}, u32[]{:S(2)}) collective-permute-start(f32[128,128]{1,0:T(8,128)S(1)} %group_sum.1.refs_0_), channel_id=1, source_target_pairs={{0,2},{1,3},{2,0},{3,1},{4,6},{5,7},{6,4},{7,5},{8,10},{9,11},{10,... | collective-permute-start | bytes 196616 | tf_op jit(solution)/shard_map/ppermute | solution.py:286
  39.7 2.8 %gram_inverse.1.refs_4_ = f32[128,128]{1,0:T(8,128)S(1)} custom-call(f32[64,64]{1,0:T(8,128)S(1)} %get-tuple-element.29.gram_ref, f32[64,64]{1,0:T(8,128)S(1)} %get-tuple-element.30.mat_ref), custom_call_target="tpu_custom_call" | custom-call | flops 3000000000 | bytes 100000 | tf_op jit(solution)/shard_map/gram_inverse/pallas_call | solution.py:290
  42.4 0.0 collective-permute-done.10.refs_3_
  42.4 0.4 collective-permute-done.9.refs_2_
  42.9 0.5 %collective-permute-done.8.refs_1_ = f32[128,128]{1,0:T(8,128)S(1)} collective-permute-done((f32[128,128]{1,0:T(8,128)S(1)}, f32[128,128]{1,0:T(8,128)S(1)}, u32[]{:S(2)}, u32[]{:S(2)}) %collective-permute-start.8) | collective-permute-done | bytes 65568 | tf_op jit(solution)/shard_map/ppermute | solution.py:286
  43.4 0.2 set_coeffs.1.mine_ref
  43.6 0.1 collective-permute-start.11
  43.7 1.2 %collective-permute-done.11.other_ref = f32[128,128]{1,0:T(8,128)S(1)} collective-permute-done((f32[128,128]{1,0:T(8,128)S(1)}, f32[128,128]{1,0:T(8,128)S(1)}, u32[]{:S(2)}, u32[]{:S(2)}) %collective-permute-start.11) | collective-permute-done | bytes 65568 | tf_op jit(solution)/shard_map/ppermute | solution.py:286
  44.9 3.5 %set_exposure.1 = (f32[2,256,512]{2,1,0:T(8,128)}, f32[2,256]{1,0:T(2,128)}) custom-call(f32[128,128]{1,0:T(8,128)S(1)} %set_coeffs.1.mine_ref, f32[128,128]{1,0:T(8,128)S(1)} %collective-permute-done.11.other_ref, f32[256,128]{1,0:T(8,128)S(1)} %get-tuple-element.31.limits_ref, f32[72,512]{1,0:T(8,128)S(1)} %copy-done, ...), custom_call_target="tpu_custom_call" | custom-call | flops 2000000000 | bytes 100000 | tf_op jit(solution)/shard_map/set_exposure/pallas_call | solution.py:290
  (2 shorter events, 0.0 us)
Async XLA Ops:
  0.6 6.3 %copy-start.1 = (f32[2,512,32]{1,2,0:T(8,128)S(1)}, f32[2,512,32]{1,2,0:T(8,128)}, u32[]{:S(2)}) copy-start(f32[2,512,32]{1,2,0:T(8,128)} %param.10) | copy-start | bytes 393220
  0.6 6.3 %copy-start.2 = (f32[512,32]{0,1:T(8,128)S(1)}, f32[512,32]{0,1:T(8,128)}, u32[]{:S(2)}) copy-start(f32[512,32]{0,1:T(8,128)} %param.9) | copy-start | bytes 196612
  0.7 6.3 %copy-start.3 = (f32[8192]{0:T(1024)S(1)}, f32[8192]{0:T(1024)}, u32[]{:S(2)}) copy-start(f32[8192]{0:T(1024)} %param.12) | copy-start | bytes 98308
  0.7 6.3 %copy-start.4 = (f32[8192]{0:T(1024)S(1)}, f32[8192]{0:T(1024)}, u32[]{:S(2)}) copy-start(f32[8192]{0:T(1024)} %param.13) | copy-start | bytes 98308
  0.7 6.3 %copy-start.5 = (s32[8192]{0:T(1024)S(1)}, s32[8192]{0:T(1024)}, u32[]{:S(2)}) copy-start(s32[8192]{0:T(1024)} %param.14) | copy-start | bytes 98308
  2.4 4.5 %collective-permute-start = (f32[104,512]{1,0:T(8,128)}, f32[104,512]{1,0:T(8,128)S(1)}, u32[]{:S(2)}, u32[]{:S(2)}) collective-permute-start(f32[104,512]{1,0:T(8,128)} %get-tuple-element.18), channel_id=1, source_target_pairs={{0,1},{1,0},{2,3},{3,2},{4,5},{5,4},{6,7},{7,6},{8,9},{9,8},{10,11... | collective-permute-start | bytes 638984 | tf_op jit(solution)/shard_map/ppermute | solution.py:286
  2.9 18.6 %collective-permute-start.3 = (f32[72,512]{1,0:T(8,128)}, f32[72,512]{1,0:T(8,128)S(1)}, u32[]{:S(2)}, u32[]{:S(2)}) collective-permute-start(f32[72,512]{1,0:T(8,128)} %get-tuple-element.17.refs_0_), channel_id=1, source_target_pairs={{0,6},{1,7},{2,4},{3,5},{4,2},{5,3},{6,0},{7,1},{8,14},{9,15},{10,... | collective-permute-start | bytes 442376 | tf_op jit(solution)/shard_map/ppermute | solution.py:286
  6.3 15.1 %collective-permute-start.2 = (f32[72,512]{1,0:T(8,128)}, f32[72,512]{1,0:T(8,128)S(1)}, u32[]{:S(2)}, u32[]{:S(2)}) collective-permute-start(f32[72,512]{1,0:T(8,128)} %get-tuple-element.17.refs_0_), channel_id=1, source_target_pairs={{0,4},{1,5},{2,6},{3,7},{4,0},{5,1},{6,2},{7,3},{8,12},{9,13},{10,... | collective-permute-start | bytes 442376 | tf_op jit(solution)/shard_map/ppermute | solution.py:286
  6.8 14.6 %collective-permute-start.1 = (f32[72,512]{1,0:T(8,128)}, f32[72,512]{1,0:T(8,128)S(1)}, u32[]{:S(2)}, u32[]{:S(2)}) collective-permute-start(f32[72,512]{1,0:T(8,128)} %get-tuple-element.17.refs_0_), channel_id=1, source_target_pairs={{0,2},{1,3},{2,0},{3,1},{4,6},{5,7},{6,4},{7,5},{8,10},{9,11},{10,... | collective-permute-start | bytes 442376 | tf_op jit(solution)/shard_map/ppermute | solution.py:286
  7.0 0.7 %copy-start.6 = (s32[512]{0:T(512)S(1)}, s32[512]{0:T(512)}, u32[]{:S(2)}) copy-start(s32[512]{0:T(512)} %param.16) | copy-start | bytes 6148
  21.5 8.7 %copy-start = (f32[72,512]{1,0:T(8,128)S(1)}, f32[72,512]{1,0:T(8,128)}, u32[]{:S(2)}) copy-start(f32[72,512]{1,0:T(8,128)} %get-tuple-element.17.refs_0_) | copy-start | bytes 442372
  21.5 8.6 %collective-permute-start.4 = (f32[3,72,512]{2,1,0:T(8,128)S(1)}, f32[3,72,512]{2,1,0:T(8,128)S(1)}, u32[]{:S(2)}, u32[]{:S(2)}) collective-permute-start(f32[3,72,512]{2,1,0:T(8,128)S(1)} %pad_maximum_fusion), channel_id=1, source_target_pairs={{0,1},{1,0},{2,3},{3,2},{4,5},{5,4},{6,7},{7,6},{8,9},{9,8},{10,11... | collective-permute-start | bytes 1327112 | tf_op jit(solution)/shard_map/ppermute | solution.py:286
  21.6 12.7 %collective-permute-start.5 = (f32[128,128]{1,0:T(8,128)S(1)}, f32[128,128]{1,0:T(8,128)S(1)}, u32[]{:S(2)}, u32[]{:S(2)}) collective-permute-start(f32[128,128]{1,0:T(8,128)S(1)} %get-tuple-element.26), channel_id=1, source_target_pairs={{0,8},{8,0},{16,24},{24,16},{1,9},{9,1},{17,25},{25,17},{2,10},{10... | collective-permute-start | bytes 196616 | tf_op jit(solution)/shard_map/ppermute | solution.py:286
  27.7 8.4 %collective-permute-start.6 = (f32[128,128]{1,0:T(8,128)S(1)}, f32[128,128]{1,0:T(8,128)S(1)}, u32[]{:S(2)}, u32[]{:S(2)}) collective-permute-start(f32[128,128]{1,0:T(8,128)S(1)} %get-tuple-element.27), channel_id=1, source_target_pairs={{0,16},{8,24},{16,0},{24,8},{1,17},{9,25},{17,1},{25,9},{2,18},{10... | collective-permute-start | bytes 196616 | tf_op jit(solution)/shard_map/ppermute | solution.py:286
  28.8 1.4 %copy-start.7 = (s32[256]{0:T(256)S(1)}, s32[256]{0:T(256)}, u32[]{:S(2)}) copy-start(s32[256]{0:T(256)} %param.17) | copy-start | bytes 3076
  28.8 7.3 %collective-permute-start.7 = (f32[128,128]{1,0:T(8,128)S(1)}, f32[128,128]{1,0:T(8,128)S(1)}, u32[]{:S(2)}, u32[]{:S(2)}) collective-permute-start(f32[128,128]{1,0:T(8,128)S(1)} %get-tuple-element.28), channel_id=1, source_target_pairs={{0,24},{8,16},{16,8},{24,0},{1,25},{9,17},{17,9},{25,1},{2,26},{10... | collective-permute-start | bytes 196616 | tf_op jit(solution)/shard_map/ppermute | solution.py:286
  36.1 6.3 %collective-permute-start.10 = (f32[128,128]{1,0:T(8,128)S(1)}, f32[128,128]{1,0:T(8,128)S(1)}, u32[]{:S(2)}, u32[]{:S(2)}) collective-permute-start(f32[128,128]{1,0:T(8,128)S(1)} %group_sum.1.refs_0_), channel_id=1, source_target_pairs={{0,6},{1,7},{2,4},{3,5},{4,2},{5,3},{6,0},{7,1},{8,14},{9,15},{10,... | collective-permute-start | bytes 196616 | tf_op jit(solution)/shard_map/ppermute | solution.py:286
  38.6 4.3 %collective-permute-start.9 = (f32[128,128]{1,0:T(8,128)S(1)}, f32[128,128]{1,0:T(8,128)S(1)}, u32[]{:S(2)}, u32[]{:S(2)}) collective-permute-start(f32[128,128]{1,0:T(8,128)S(1)} %group_sum.1.refs_0_), channel_id=1, source_target_pairs={{0,4},{1,5},{2,6},{3,7},{4,0},{5,1},{6,2},{7,3},{8,12},{9,13},{10,... | collective-permute-start | bytes 196616 | tf_op jit(solution)/shard_map/ppermute | solution.py:286
  39.1 4.3 %collective-permute-start.8 = (f32[128,128]{1,0:T(8,128)S(1)}, f32[128,128]{1,0:T(8,128)S(1)}, u32[]{:S(2)}, u32[]{:S(2)}) collective-permute-start(f32[128,128]{1,0:T(8,128)S(1)} %group_sum.1.refs_0_), channel_id=1, source_target_pairs={{0,2},{1,3},{2,0},{3,1},{4,6},{5,7},{6,4},{7,5},{8,10},{9,11},{10,... | collective-permute-start | bytes 196616 | tf_op jit(solution)/shard_map/ppermute | solution.py:286
  43.6 1.3 %collective-permute-start.11 = (f32[128,128]{1,0:T(8,128)S(1)}, f32[128,128]{1,0:T(8,128)S(1)}, u32[]{:S(2)}, u32[]{:S(2)}) collective-permute-start(f32[128,128]{1,0:T(8,128)S(1)} %set_coeffs.1.mine_ref), channel_id=1, source_target_pairs={{0,1},{1,0},{2,3},{3,2},{4,5},{5,4},{6,7},{7,6},{8,9},{9,8},{10,11... | collective-permute-start | bytes 196616 | tf_op jit(solution)/shard_map/ppermute | solution.py:286

commit v7 on v6

--- a/solution.py
+++ b/solution.py
@@ -12,7 +12,7 @@
 F32 = jnp.float32
 BF16 = jnp.bfloat16
 TILE = 512
-CHUNK = 512
+CHUNK = 1024
 SLOTS = 4
 FIRST_PIVOTS = 36
 DEPTH = 256
@@ -124,7 +124,7 @@
     groups, start_ref, shocks_ref, weights_ref, other_ref, load_hbm, strike_hbm, notional_hbm, set_hbm, *refs
 ):
     outs = refs[:groups]
-    *staged, sems, net_scr, states_scr, wide_scr, load_scr = refs[groups:]
+    *staged, sems, net_scr, states_scr, wide_scr, load_scr, part_scr, hot_scr = refs[groups:]
     load_ref, strike_ref, notional_ref, set_ref = staged
     moves = copies((load_hbm, strike_hbm, notional_hbm, set_hbm), staged, sems)
     for move in moves:
@@ -136,7 +136,8 @@
     bits = log2(owned)
     rows = 16
     load_scr[...] = jnp.zeros_like(load_scr)
-    net_scr[...] = jnp.zeros_like(net_scr)
+    for ref in (net_scr, part_scr, hot_scr):
+        ref[...] = jnp.zeros_like(ref)
     prepare(0, start_ref[...], shocks_ref[...], weights_ref[...].astype(F32), states_scr, wide_scr)
     shocks = (other_ref[factors : 2 * factors, :], other_ref[2 * factors + PAD :, :])
     prepare(1, other_ref[:factors, :], shocks, weights_of(other_ref, factors), states_scr, wide_scr)
@@ -145,7 +146,7 @@
 
     chunks = [pl.ds(start, CHUNK) for start in range(0, states_scr.shape[0], CHUNK)]
 
-    def add_tile(index, moment):
+    def keep_tile(index, slot, moment):
         cols = tile_at(index)
         slot_ids = index * TILE + lax.broadcasted_iota(jnp.int32, (1, TILE), 1)
         hi, lo = split2(moment * jnp.where(slot_ids < filled, notional_ref[:, cols], 0.0))
@@ -153,15 +154,19 @@
         both = both.reshape(both.shape[0] // rows, rows, TILE)
         sets = set_ref[:, cols]
         to_group = jnp.broadcast_to((sets >> bits) ^ group, (rows, TILE))
-        parts = []
+        place = slice(slot * TILE, (slot + 1) * TILE)
         for away in range(groups):
             mask = jnp.where(to_group == away, 1.0, 0.0).astype(BF16)
-            parts.append((both * mask[None]).reshape(-1, TILE))
+            size = both.shape[0] * rows
+            part_scr[away * size : (away + 1) * size, place] = (both * mask[None]).reshape(-1, TILE)
         one_hot = lax.broadcasted_iota(jnp.int32, (owned, TILE), 0) == (sets & (owned - 1))
-        one_hot = jnp.where(one_hot, 1.0, 0.0).astype(BF16)
-        net_scr[...] += mm(one_hot, jnp.concatenate(parts, axis=0), NT)
+        hot_scr[:, place] = jnp.where(one_hot, 1.0, 0.0).astype(BF16)
+
+    def add_tiles():
+        net_scr[...] += mm(hot_scr[...], part_scr[...], NT)
 
     def step(turn, carry):
+        add_tiles()
         stages = [(slot, chunk) for slot in range(SLOTS) for chunk in chunks]
         pays, moment = {}, None
         for number in range(len(stages) + 1):
@@ -175,11 +180,12 @@
                 part = chunk_moments(pays.pop(number - 1), chunk, wide_scr)
                 moment = part if moment is None else moment + part
                 if number % len(chunks) == 0:
-                    add_tile(SLOTS * turn + slot, moment)
+                    keep_tile(SLOTS * turn + slot, slot, moment)
                     moment = None
         return carry
 
     lax.fori_loop(0, (jnp.max(filled) + SLOTS * TILE - 1) // (SLOTS * TILE), step, 0)
+    add_tiles()
     wide = net_scr.shape[1] // (2 * groups)
     half = owned // 2
     for away, out in enumerate(outs):
@@ -255,29 +261,29 @@
     wide = 2 * factors
     paths = blocks[0].shape[1]
     limits = limits_ref[:, :1]
-    results, moves = [], []
+    mine, other = mine_ref[...], other_ref[...]
+    coeffs = []
+    for packed in (pick(core, mine, other), pick(core, other, mine)):
+        hi, lo = split2(jnp.concatenate([packed[:, :wide], packed[:, wide:]], axis=0))
+        coeffs.append(jnp.concatenate([hi, hi, lo], axis=1))
+    sums = [jnp.zeros((limits.shape[0], 128), F32) for _ in coeffs]
     total = jnp.zeros((1, 1), F32)
-    for block in path_blocks(blocks):
-        total = total + jnp.sum(weights_of(block, factors), keepdims=True)
-    for turn, ref in enumerate((mine_ref, other_ref)):
-        date = core ^ turn
-        packed = ref[...]
-        hi, lo = split2(jnp.concatenate([packed[:, :wide], packed[:, wide:]], axis=0))
-        coeffs = jnp.concatenate([hi, hi, lo], axis=1)
-        sums = jnp.zeros((limits.shape[0], 128), F32)
-        for number, block in enumerate(path_blocks(blocks)):
-            hi, lo = split2(basis_rows(pick(date, *states_of(block, factors))))
-            value = jnp.maximum(mm(coeffs, jnp.concatenate([hi, lo, hi], axis=0)) - limits, 0.0)
+    moves = []
+    for number, block in enumerate(path_blocks(blocks)):
+        weight_row = weights_of(block, factors)
+        total = total + jnp.sum(weight_row, keepdims=True)
+        for date, state in enumerate(states_of(block, factors)):
+            hi, lo = split2(basis_rows(state))
+            value = jnp.maximum(mm(coeffs[date], jnp.concatenate([hi, lo, hi], axis=0)) - limits, 0.0)
             if number == 0:
-                value_scr[turn] = value
-                moves.append(pltpu.make_async_copy(value_scr.at[turn], exposure_hbm.at[date], sems.at[turn]))
-                moves[turn].start()
-            product = value * weights_of(block, factors)
+                value_scr[date] = value
+                moves.append(pltpu.make_async_copy(value_scr.at[date], exposure_hbm.at[date], sems.at[date]))
+                moves[date].start()
+            product = value * weight_row
             for c in range(paths // 128):
-                sums = sums + product[:, c * 128 : (c + 1) * 128]
-        results.append(jnp.sum(sums.T, axis=0, keepdims=True) / total)
-    mine, other = results
-    expected_ref[...] = jnp.concatenate([pick(core, mine, other), pick(core, other, mine)], axis=0)
+                sums[date] = sums[date] + product[:, c * 128 : (c + 1) * 128]
+    for date, partial in enumerate(sums):
+        expected_ref[date : date + 1, :] = jnp.sum(partial.T, axis=0, keepdims=True) / total
     for move in moves:
         move.wait()
 
@@ -336,6 +342,8 @@
             pltpu.VMEM((2 * paths, DEPTH), BF16),
             pltpu.VMEM((2 * wide, 2 * paths), BF16),
             pltpu.VMEM((SLOTS, DEPTH, TILE), BF16),
+            pltpu.VMEM((2 * wide * groups, SLOTS * TILE), BF16),
+            pltpu.VMEM((owned, SLOTS * TILE), BF16),
         ],
         20.0,
     )

time: 48.7 us -> 46.1 us (0.947)
  starting transfers between devices: 16.8 us -> 12.7 us
  Pallas kernels: 26.1 us -> 27.8 us
  waiting for transfers between devices: 3.97 us -> 3.47 us
    ppermute x12, starting transfers between devices: 16.8 us -> 12.7 us  [swap(): lax.ppermute(x, axis, [(i, i ^ away) for i in range(lax.axis_size(axis))])]
    pallas_call x7, Pallas kernels: 26.1 us -> 27.8 us  [run(): pl.pallas_call(kernel, out_shape=out, in_specs=specs, out_specs=out_specs...]
    ppermute x12, waiting for transfers between devices: 3.97 us -> 3.47 us  [swap(): lax.ppermute(x, axis, [(i, i ^ away) for i in range(lax.axis_size(axis))])]
  transfers between devices with their start and end apart: 12 -> 12, of which waited for: 4 -> 4; matrix products, arithmetic and copies ran while one was open for 0% -> 0% of each run, Pallas kernels for 43% -> 51%
where the time goes in v7:
time: 46.1 us; the launch traced here: 45.5 us
  Pallas kernels  27.8 us (60%)
  starting transfers between devices  12.7 us (28%)
  waiting for transfers between devices  3.47 us (8%)
  between operations  0.81 us (2%)
  local copies, waits for them, and re-layouts  0.67 us (1%)
    pallas_call x7, Pallas kernels, run(): pl.pallas_call(kernel, out_shape=out, in_specs=specs, out_specs=out_specs...  27.8 us
    ppermute x12, starting transfers between devices, swap(): lax.ppermute(x, axis, [(i, i ^ away) for i in range(lax.axis_size(axis))])  12.7 us
    ppermute x12, waiting for transfers between devices, swap(): lax.ppermute(x, axis, [(i, i ^ away) for i in range(lax.axis_size(axis))])  3.47 us
  transfers between devices with their start and end apart: 12, of which 4 were waited for; matrix products, arithmetic and copies ran while one was open for 0% of the time, Pallas kernels for 51%

profile of v7, /device:TPU:0, one launch (start us, length us, event | category | flops | bytes accessed | tf_op | source)
XLA Modules:
  0.0 45.5 jit_solution(2511895926386780101)
XLA Ops:
  0.6 0.0 copy-start.1
  0.6 0.0 copy-start.2
  0.7 0.0 copy-start.3
  0.7 0.0 copy-start.4
  0.7 0.0 copy-start.5
  0.7 1.7 %pack_states.1 = (f32[72,512]{1,0:T(8,128)}, f32[104,512]{1,0:T(8,128)}) custom-call(s32[4]{0:T(128)} %counts_ref.1, f32[32,512]{1,0:T(8,128)} %bitcast.15, f32[2,32,512]{2,1,0:T(8,128)} %bitcast.13, s32[1,512]{1,0:T(1,128)} %bitcast.20), custom_call_target="tpu_custom_call" | custom-call | flops 20000000000 | bytes 100000 | tf_op jit(solution)/shard_map/pack_states/pallas_call | solution.py:296
  2.4 0.5 collective-permute-start
  2.9 3.4 %collective-permute-start.3 = (f32[72,512]{1,0:T(8,128)}, f32[72,512]{1,0:T(8,128)S(1)}, u32[]{:S(2)}, u32[]{:S(2)}) collective-permute-start(f32[72,512]{1,0:T(8,128)} %get-tuple-element.17.refs_0_), channel_id=1, source_target_pairs={{0,6},{1,7},{2,4},{3,5},{4,2},{5,3},{6,0},{7,1},{8,14},{9,15},{10,... | collective-permute-start | bytes 442376 | tf_op jit(solution)/shard_map/ppermute | solution.py:292
  6.3 0.5 %collective-permute-start.2 = (f32[72,512]{1,0:T(8,128)}, f32[72,512]{1,0:T(8,128)S(1)}, u32[]{:S(2)}, u32[]{:S(2)}) collective-permute-start(f32[72,512]{1,0:T(8,128)} %get-tuple-element.17.refs_0_), channel_id=1, source_target_pairs={{0,4},{1,5},{2,6},{3,7},{4,0},{5,1},{6,2},{7,3},{8,12},{9,13},{10,... | collective-permute-start | bytes 442376 | tf_op jit(solution)/shard_map/ppermute | solution.py:292
  6.8 0.1 collective-permute-start.1
  7.0 0.0 collective-permute-done.other_ref.refs_1_
  7.0 0.0 copy-start.6
  7.0 0.0 copy-done.1
  7.0 0.0 copy-done.2
  7.0 0.0 copy-done.3
  7.0 0.0 copy-done.4
  7.0 0.0 copy-done.5
  7.0 0.6 %copy-done.6 = s32[512]{0:T(512)S(1)} copy-done((s32[512]{0:T(512)S(1)}, s32[512]{0:T(512)}, u32[]{:S(2)}) %copy-start.6) | copy-done | bytes 2072
  7.6 16.2 %net_moments.1 = (f32[128,128]{1,0:T(8,128)S(1)}, f32[128,128]{1,0:T(8,128)S(1)}, f32[128,128]{1,0:T(8,128)S(1)}, f32[128,128]{1,0:T(8,128)S(1)}) custom-call(f32[32,512]{1,0:T(8,128)S(1)} %bitcast.16, f32[2,32,512]{2,1,0:T(8,128)S(1)} %bitcast.14, s32[1,512]{1,0:T(1,128)S(1)} %bitcast.21, f32[104,512]{1,0:T(8,128)S(1)} %collective-permute-done.other_ref.refs_1_, ...), custom_call_target="tpu_custom_call" | custom-call | flops 20000000000 | bytes 100000 | tf_op jit(solution)/shard_map/net_moments/pallas_call | solution.py:296
  23.9 0.0 collective-permute-done.3.refs_4_
  23.9 0.0 collective-permute-done.2.refs_3_
  23.9 0.0 collective-permute-done.1.refs_2_
  23.9 0.0 copy-start
  23.9 0.1 collective-permute-start.4
  24.0 2.1 %collective-permute-start.5 = (f32[128,128]{1,0:T(8,128)S(1)}, f32[128,128]{1,0:T(8,128)S(1)}, u32[]{:S(2)}, u32[]{:S(2)}) collective-permute-start(f32[128,128]{1,0:T(8,128)S(1)} %get-tuple-element.26), channel_id=1, source_target_pairs={{0,8},{8,0},{16,24},{24,16},{1,9},{9,1},{17,25},{25,17},{2,10},{10... | collective-permute-start | bytes 196616 | tf_op jit(solution)/shard_map/ppermute | solution.py:292
  26.1 0.0 collective-permute-start.6
  26.1 0.0 copy-start.7
  26.1 2.4 %collective-permute-start.7 = (f32[128,128]{1,0:T(8,128)S(1)}, f32[128,128]{1,0:T(8,128)S(1)}, u32[]{:S(2)}, u32[]{:S(2)}) collective-permute-start(f32[128,128]{1,0:T(8,128)S(1)} %get-tuple-element.28), channel_id=1, source_target_pairs={{0,24},{8,16},{16,8},{24,0},{1,25},{9,17},{17,9},{25,1},{2,26},{10... | collective-permute-start | bytes 196616 | tf_op jit(solution)/shard_map/ppermute | solution.py:292
  28.5 0.0 collective-permute-done.4.refs_5_
  28.5 0.0 copy-done
  28.5 0.0 copy-done.7
  28.5 4.1 %gram_first_pivots.1 = (f32[64,64]{1,0:T(8,128)S(1)}, f32[64,64]{1,0:T(8,128)S(1)}, f32[256,128]{1,0:T(8,128)S(1)}) custom-call(f32[72,512]{1,0:T(8,128)S(1)} %copy-done, f32[104,512]{1,0:T(8,128)S(1)} %collective-permute-done.other_ref.refs_1_, f32[72,512]{1,0:T(8,128)S(1)} %collective-permute-done.1.refs_2_, f32[72,512]{1,0:T(8,128)S(1)} %collective-permute-done.2.refs_3_, ...), custom_call_target="tpu_custom_call" | custom-call | flops 5000000000 | bytes 100000 | tf_op jit(solution)/shard_map/gram_first_pivots/pallas_call | solution.py:296
  32.7 0.0 collective-permute-done.5.refs_1_
  32.7 1.0 %collective-permute-done.6.refs_2_ = f32[128,128]{1,0:T(8,128)S(1)} collective-permute-done((f32[128,128]{1,0:T(8,128)S(1)}, f32[128,128]{1,0:T(8,128)S(1)}, u32[]{:S(2)}, u32[]{:S(2)}) %collective-permute-start.6) | collective-permute-done | bytes 65568 | tf_op jit(solution)/shard_map/ppermute | solution.py:292
  33.7 0.0 collective-permute-done.7.refs_3_
  33.8 2.7 %collective-permute-start.10 = (f32[128,128]{1,0:T(8,128)S(1)}, f32[128,128]{1,0:T(8,128)S(1)}, u32[]{:S(2)}, u32[]{:S(2)}) collective-permute-start(f32[128,128]{1,0:T(8,128)S(1)} %group_sum.1.refs_0_), channel_id=1, source_target_pairs={{0,6},{1,7},{2,4},{3,5},{4,2},{5,3},{6,0},{7,1},{8,14},{9,15},{10,... | collective-permute-start | bytes 196616 | tf_op jit(solution)/shard_map/ppermute | solution.py:292
  36.5 0.5 %collective-permute-start.9 = (f32[128,128]{1,0:T(8,128)S(1)}, f32[128,128]{1,0:T(8,128)S(1)}, u32[]{:S(2)}, u32[]{:S(2)}) collective-permute-start(f32[128,128]{1,0:T(8,128)S(1)} %group_sum.1.refs_0_), channel_id=1, source_target_pairs={{0,4},{1,5},{2,6},{3,7},{4,0},{5,1},{6,2},{7,3},{8,12},{9,13},{10,... | collective-permute-start | bytes 196616 | tf_op jit(solution)/shard_map/ppermute | solution.py:292
  37.0 0.3 collective-permute-start.8
  37.3 2.8 %gram_inverse.1.refs_4_ = f32[128,128]{1,0:T(8,128)S(1)} custom-call(f32[64,64]{1,0:T(8,128)S(1)} %get-tuple-element.29.gram_ref, f32[64,64]{1,0:T(8,128)S(1)} %get-tuple-element.30.mat_ref), custom_call_target="tpu_custom_call" | custom-call | flops 3000000000 | bytes 100000 | tf_op jit(solution)/shard_map/gram_inverse/pallas_call | solution.py:296
  40.1 0.0 collective-permute-done.10.refs_3_
  40.1 0.7 %collective-permute-done.9.refs_2_ = f32[128,128]{1,0:T(8,128)S(1)} collective-permute-done((f32[128,128]{1,0:T(8,128)S(1)}, f32[128,128]{1,0:T(8,128)S(1)}, u32[]{:S(2)}, u32[]{:S(2)}) %collective-permute-start.9) | collective-permute-done | bytes 65568 | tf_op jit(solution)/shard_map/ppermute | solution.py:292
  40.7 0.5 %collective-permute-done.8.refs_1_ = f32[128,128]{1,0:T(8,128)S(1)} collective-permute-done((f32[128,128]{1,0:T(8,128)S(1)}, f32[128,128]{1,0:T(8,128)S(1)}, u32[]{:S(2)}, u32[]{:S(2)}) %collective-permute-start.8) | collective-permute-done | bytes 65568 | tf_op jit(solution)/shard_map/ppermute | solution.py:292
  41.2 0.2 set_coeffs.1.mine_ref
  41.5 0.1 collective-permute-start.11
  41.5 1.2 %collective-permute-done.11.other_ref = f32[128,128]{1,0:T(8,128)S(1)} collective-permute-done((f32[128,128]{1,0:T(8,128)S(1)}, f32[128,128]{1,0:T(8,128)S(1)}, u32[]{:S(2)}, u32[]{:S(2)}) %collective-permute-start.11) | collective-permute-done | bytes 65568 | tf_op jit(solution)/shard_map/ppermute | solution.py:292
  42.8 2.7 %set_exposure.1 = (f32[2,256,512]{2,1,0:T(8,128)}, f32[2,256]{1,0:T(2,128)}) custom-call(f32[128,128]{1,0:T(8,128)S(1)} %set_coeffs.1.mine_ref, f32[128,128]{1,0:T(8,128)S(1)} %collective-permute-done.11.other_ref, f32[256,128]{1,0:T(8,128)S(1)} %get-tuple-element.31.limits_ref, f32[72,512]{1,0:T(8,128)S(1)} %copy-done, ...), custom_call_target="tpu_custom_call" | custom-call | flops 2000000000 | bytes 100000 | tf_op jit(solution)/shard_map/set_exposure/pallas_call | solution.py:296
  (2 shorter events, 0.0 us)
Async XLA Ops:
  0.6 6.3 %copy-start.1 = (f32[2,512,32]{1,2,0:T(8,128)S(1)}, f32[2,512,32]{1,2,0:T(8,128)}, u32[]{:S(2)}) copy-start(f32[2,512,32]{1,2,0:T(8,128)} %param.10) | copy-start | bytes 393220
  0.6 6.3 %copy-start.2 = (f32[512,32]{0,1:T(8,128)S(1)}, f32[512,32]{0,1:T(8,128)}, u32[]{:S(2)}) copy-start(f32[512,32]{0,1:T(8,128)} %param.9) | copy-start | bytes 196612
  0.7 6.3 %copy-start.3 = (f32[8192]{0:T(1024)S(1)}, f32[8192]{0:T(1024)}, u32[]{:S(2)}) copy-start(f32[8192]{0:T(1024)} %param.12) | copy-start | bytes 98308
  0.7 6.3 %copy-start.4 = (f32[8192]{0:T(1024)S(1)}, f32[8192]{0:T(1024)}, u32[]{:S(2)}) copy-start(f32[8192]{0:T(1024)} %param.13) | copy-start | bytes 98308
  0.7 6.3 %copy-start.5 = (s32[8192]{0:T(1024)S(1)}, s32[8192]{0:T(1024)}, u32[]{:S(2)}) copy-start(s32[8192]{0:T(1024)} %param.14) | copy-start | bytes 98308
  2.4 4.5 %collective-permute-start = (f32[104,512]{1,0:T(8,128)}, f32[104,512]{1,0:T(8,128)S(1)}, u32[]{:S(2)}, u32[]{:S(2)}) collective-permute-start(f32[104,512]{1,0:T(8,128)} %get-tuple-element.18), channel_id=1, source_target_pairs={{0,1},{1,0},{2,3},{3,2},{4,5},{5,4},{6,7},{7,6},{8,9},{9,8},{10,11... | collective-permute-start | bytes 638984 | tf_op jit(solution)/shard_map/ppermute | solution.py:292
  2.9 21.0 %collective-permute-start.3 = (f32[72,512]{1,0:T(8,128)}, f32[72,512]{1,0:T(8,128)S(1)}, u32[]{:S(2)}, u32[]{:S(2)}) collective-permute-start(f32[72,512]{1,0:T(8,128)} %get-tuple-element.17.refs_0_), channel_id=1, source_target_pairs={{0,6},{1,7},{2,4},{3,5},{4,2},{5,3},{6,0},{7,1},{8,14},{9,15},{10,... | collective-permute-start | bytes 442376 | tf_op jit(solution)/shard_map/ppermute | solution.py:292
  6.3 17.6 %collective-permute-start.2 = (f32[72,512]{1,0:T(8,128)}, f32[72,512]{1,0:T(8,128)S(1)}, u32[]{:S(2)}, u32[]{:S(2)}) collective-permute-start(f32[72,512]{1,0:T(8,128)} %get-tuple-element.17.refs_0_), channel_id=1, source_target_pairs={{0,4},{1,5},{2,6},{3,7},{4,0},{5,1},{6,2},{7,3},{8,12},{9,13},{10,... | collective-permute-start | bytes 442376 | tf_op jit(solution)/shard_map/ppermute | solution.py:292
  6.8 17.1 %collective-permute-start.1 = (f32[72,512]{1,0:T(8,128)}, f32[72,512]{1,0:T(8,128)S(1)}, u32[]{:S(2)}, u32[]{:S(2)}) collective-permute-start(f32[72,512]{1,0:T(8,128)} %get-tuple-element.17.refs_0_), channel_id=1, source_target_pairs={{0,2},{1,3},{2,0},{3,1},{4,6},{5,7},{6,4},{7,5},{8,10},{9,11},{10,... | collective-permute-start | bytes 442376 | tf_op jit(solution)/shard_map/ppermute | solution.py:292
  7.0 0.7 %copy-start.6 = (s32[512]{0:T(512)S(1)}, s32[512]{0:T(512)}, u32[]{:S(2)}) copy-start(s32[512]{0:T(512)} %param.16) | copy-start | bytes 6148
  23.9 4.6 %copy-start = (f32[72,512]{1,0:T(8,128)S(1)}, f32[72,512]{1,0:T(8,128)}, u32[]{:S(2)}) copy-start(f32[72,512]{1,0:T(8,128)} %get-tuple-element.17.refs_0_) | copy-start | bytes 442372
  23.9 4.6 %collective-permute-start.4 = (f32[3,72,512]{2,1,0:T(8,128)S(1)}, f32[3,72,512]{2,1,0:T(8,128)S(1)}, u32[]{:S(2)}, u32[]{:S(2)}) collective-permute-start(f32[3,72,512]{2,1,0:T(8,128)S(1)} %pad_maximum_fusion), channel_id=1, source_target_pairs={{0,1},{1,0},{2,3},{3,2},{4,5},{5,4},{6,7},{7,6},{8,9},{9,8},{10,11... | collective-permute-start | bytes 1327112 | tf_op jit(solution)/shard_map/ppermute | solution.py:292
  24.0 8.7 %collective-permute-start.5 = (f32[128,128]{1,0:T(8,128)S(1)}, f32[128,128]{1,0:T(8,128)S(1)}, u32[]{:S(2)}, u32[]{:S(2)}) collective-permute-start(f32[128,128]{1,0:T(8,128)S(1)} %get-tuple-element.26), channel_id=1, source_target_pairs={{0,8},{8,0},{16,24},{24,16},{1,9},{9,1},{17,25},{25,17},{2,10},{10... | collective-permute-start | bytes 196616 | tf_op jit(solution)/shard_map/ppermute | solution.py:292
  26.1 7.6 %collective-permute-start.6 = (f32[128,128]{1,0:T(8,128)S(1)}, f32[128,128]{1,0:T(8,128)S(1)}, u32[]{:S(2)}, u32[]{:S(2)}) collective-permute-start(f32[128,128]{1,0:T(8,128)S(1)} %get-tuple-element.27), channel_id=1, source_target_pairs={{0,16},{8,24},{16,0},{24,8},{1,17},{9,25},{17,1},{25,9},{2,18},{10... | collective-permute-start | bytes 196616 | tf_op jit(solution)/shard_map/ppermute | solution.py:292
  26.1 2.4 %copy-start.7 = (s32[256]{0:T(256)S(1)}, s32[256]{0:T(256)}, u32[]{:S(2)}) copy-start(s32[256]{0:T(256)} %param.17) | copy-start | bytes 3076
  26.1 7.6 %collective-permute-start.7 = (f32[128,128]{1,0:T(8,128)S(1)}, f32[128,128]{1,0:T(8,128)S(1)}, u32[]{:S(2)}, u32[]{:S(2)}) collective-permute-start(f32[128,128]{1,0:T(8,128)S(1)} %get-tuple-element.28), channel_id=1, source_target_pairs={{0,24},{8,16},{16,8},{24,0},{1,25},{9,17},{17,9},{25,1},{2,26},{10... | collective-permute-start | bytes 196616 | tf_op jit(solution)/shard_map/ppermute | solution.py:292
  33.8 6.3 %collective-permute-start.10 = (f32[128,128]{1,0:T(8,128)S(1)}, f32[128,128]{1,0:T(8,128)S(1)}, u32[]{:S(2)}, u32[]{:S(2)}) collective-permute-start(f32[128,128]{1,0:T(8,128)S(1)} %group_sum.1.refs_0_), channel_id=1, source_target_pairs={{0,6},{1,7},{2,4},{3,5},{4,2},{5,3},{6,0},{7,1},{8,14},{9,15},{10,... | collective-permute-start | bytes 196616 | tf_op jit(solution)/shard_map/ppermute | solution.py:292
  36.5 4.3 %collective-permute-start.9 = (f32[128,128]{1,0:T(8,128)S(1)}, f32[128,128]{1,0:T(8,128)S(1)}, u32[]{:S(2)}, u32[]{:S(2)}) collective-permute-start(f32[128,128]{1,0:T(8,128)S(1)} %group_sum.1.refs_0_), channel_id=1, source_target_pairs={{0,4},{1,5},{2,6},{3,7},{4,0},{5,1},{6,2},{7,3},{8,12},{9,13},{10,... | collective-permute-start | bytes 196616 | tf_op jit(solution)/shard_map/ppermute | solution.py:292
  37.0 4.3 %collective-permute-start.8 = (f32[128,128]{1,0:T(8,128)S(1)}, f32[128,128]{1,0:T(8,128)S(1)}, u32[]{:S(2)}, u32[]{:S(2)}) collective-permute-start(f32[128,128]{1,0:T(8,128)S(1)} %group_sum.1.refs_0_), channel_id=1, source_target_pairs={{0,2},{1,3},{2,0},{3,1},{4,6},{5,7},{6,4},{7,5},{8,10},{9,11},{10,... | collective-permute-start | bytes 196616 | tf_op jit(solution)/shard_map/ppermute | solution.py:292
  41.5 1.3 %collective-permute-start.11 = (f32[128,128]{1,0:T(8,128)S(1)}, f32[128,128]{1,0:T(8,128)S(1)}, u32[]{:S(2)}, u32[]{:S(2)}) collective-permute-start(f32[128,128]{1,0:T(8,128)S(1)} %set_coeffs.1.mine_ref), channel_id=1, source_target_pairs={{0,1},{1,0},{2,3},{3,2},{4,5},{5,4},{6,7},{7,6},{8,9},{9,8},{10,11... | collective-permute-start | bytes 196616 | tf_op jit(solution)/shard_map/ppermute | solution.py:292

commit v8 on v7

--- a/solution.py
+++ b/solution.py
@@ -132,7 +132,7 @@
     group = lax.axis_index("trade")
     factors = load_ref.shape[0]
     filled = other_ref[2 * factors + 1 : 2 * factors + 2, :1].astype(jnp.int32)
-    owned = net_scr.shape[0]
+    owned = net_scr.shape[1]
     bits = log2(owned)
     rows = 16
     load_scr[...] = jnp.zeros_like(load_scr)
@@ -163,7 +163,7 @@
         hot_scr[:, place] = jnp.where(one_hot, 1.0, 0.0).astype(BF16)
 
     def add_tiles():
-        net_scr[...] += mm(hot_scr[...], part_scr[...], NT)
+        net_scr[...] += mm(part_scr[...], hot_scr[...], NT)
 
     def step(turn, carry):
         add_tiles()
@@ -186,12 +186,12 @@
 
     lax.fori_loop(0, (jnp.max(filled) + SLOTS * TILE - 1) // (SLOTS * TILE), step, 0)
     add_tiles()
-    wide = net_scr.shape[1] // (2 * groups)
+    wide = net_scr.shape[0] // (2 * groups)
     half = owned // 2
     for away, out in enumerate(outs):
-        net = net_scr[:, 2 * wide * away : 2 * wide * (away + 1)]
-        net = net[:, :wide] + net[:, wide:]
-        out[...] = jnp.concatenate([net[:half], net[half:]], axis=1)
+        at = 2 * wide * away
+        net = net_scr[at : at + wide, :] + net_scr[at + wide : at + 2 * wide, :]
+        out[...] = jnp.concatenate([net[:, :half], net[:, half:]], axis=0).T
 
 
 def eliminate(mat, pivots):
@@ -338,7 +338,7 @@
             pltpu.VMEM((1, slots), F32),
             pltpu.VMEM((1, slots), jnp.int32),
             pltpu.SemaphoreType.DMA((4,)),
-            pltpu.VMEM((owned, 2 * wide * groups), F32),
+            pltpu.VMEM((2 * wide * groups, owned), F32),
             pltpu.VMEM((2 * paths, DEPTH), BF16),
             pltpu.VMEM((2 * wide, 2 * paths), BF16),
             pltpu.VMEM((SLOTS, DEPTH, TILE), BF16),

time: 46.1 us -> 45.6 us (0.989)
  Pallas kernels: 27.8 us -> 23.5 us
  starting transfers between devices: 12.7 us -> 16.1 us
  local copies, waits for them, and re-layouts: 0.67 us -> 1.33 us
    pallas_call x7, Pallas kernels: 27.8 us -> 23.5 us  [run(): pl.pallas_call(kernel, out_shape=out, in_specs=specs, out_specs=out_specs...]
    ppermute x12, starting transfers between devices: 12.7 us -> 16.1 us  [swap(): lax.ppermute(x, axis, [(i, i ^ away) for i in range(lax.axis_size(axis))])]
    unnamed x16, local copies, waits for them, and re-layouts: 0.67 us -> 1.33 us
  transfers between devices with their start and end apart: 12 -> 12, of which waited for: 4 -> 5; matrix products, arithmetic and copies ran while one was open for 0% -> 0% of each run, Pallas kernels for 51% -> 42%
where the time goes in v8:
time: 45.6 us; the launch traced here: 45.4 us
  Pallas kernels  23.5 us (52%)
  starting transfers between devices  16.1 us (35%)
  waiting for transfers between devices  3.52 us (8%)
  local copies, waits for them, and re-layouts  1.33 us (3%)
  between operations  0.82 us (2%)
    pallas_call x7, Pallas kernels, run(): pl.pallas_call(kernel, out_shape=out, in_specs=specs, out_specs=out_specs...  23.5 us
    ppermute x12, starting transfers between devices, swap(): lax.ppermute(x, axis, [(i, i ^ away) for i in range(lax.axis_size(axis))])  16.1 us
    ppermute x12, waiting for transfers between devices, swap(): lax.ppermute(x, axis, [(i, i ^ away) for i in range(lax.axis_size(axis))])  3.52 us
    unnamed x16, local copies, waits for them, and re-layouts  1.33 us
  transfers between devices with their start and end apart: 12, of which 5 were waited for; matrix products, arithmetic and copies ran while one was open for 0% of the time, Pallas kernels for 42%

profile of v8, /device:TPU:0, one launch (start us, length us, event | category | flops | bytes accessed | tf_op | source)
XLA Modules:
  0.0 45.4 jit_solution(12252190540052587755)
XLA Ops:
  0.6 0.0 copy-start.1
  0.6 0.0 copy-start.2
  0.7 0.0 copy-start.3
  0.7 0.0 copy-start.4
  0.7 0.0 copy-start.5
  0.7 1.7 %pack_states.1 = (f32[72,512]{1,0:T(8,128)}, f32[104,512]{1,0:T(8,128)}) custom-call(s32[4]{0:T(128)} %counts_ref.1, f32[32,512]{1,0:T(8,128)} %bitcast.15, f32[2,32,512]{2,1,0:T(8,128)} %bitcast.13, s32[1,512]{1,0:T(1,128)} %bitcast.20), custom_call_target="tpu_custom_call" | custom-call | flops 20000000000 | bytes 100000 | tf_op jit(solution)/shard_map/pack_states/pallas_call | solution.py:296
  2.4 0.5 collective-permute-start
  2.9 3.4 %collective-permute-start.3 = (f32[72,512]{1,0:T(8,128)}, f32[72,512]{1,0:T(8,128)S(1)}, u32[]{:S(2)}, u32[]{:S(2)}) collective-permute-start(f32[72,512]{1,0:T(8,128)} %get-tuple-element.17.refs_0_), channel_id=1, source_target_pairs={{0,6},{1,7},{2,4},{3,5},{4,2},{5,3},{6,0},{7,1},{8,14},{9,15},{10,... | collective-permute-start | bytes 442376 | tf_op jit(solution)/shard_map/ppermute | solution.py:292
  6.3 0.5 %collective-permute-start.2 = (f32[72,512]{1,0:T(8,128)}, f32[72,512]{1,0:T(8,128)S(1)}, u32[]{:S(2)}, u32[]{:S(2)}) collective-permute-start(f32[72,512]{1,0:T(8,128)} %get-tuple-element.17.refs_0_), channel_id=1, source_target_pairs={{0,4},{1,5},{2,6},{3,7},{4,0},{5,1},{6,2},{7,3},{8,12},{9,13},{10,... | collective-permute-start | bytes 442376 | tf_op jit(solution)/shard_map/ppermute | solution.py:292
  6.8 0.1 collective-permute-start.1
  7.0 0.0 collective-permute-done.other_ref.refs_1_
  7.0 0.0 copy-start.6
  7.0 0.0 copy-done.1
  7.0 0.0 copy-done.2
  7.0 0.0 copy-done.3
  7.0 0.0 copy-done.4
  7.0 0.0 copy-done.5
  7.0 0.6 %copy-done.6 = s32[512]{0:T(512)S(1)} copy-done((s32[512]{0:T(512)S(1)}, s32[512]{0:T(512)}, u32[]{:S(2)}) %copy-start.6) | copy-done | bytes 2072
  7.6 12.0 %net_moments.1 = (f32[128,128]{1,0:T(8,128)S(1)}, f32[128,128]{1,0:T(8,128)S(1)}, f32[128,128]{1,0:T(8,128)S(1)}, f32[128,128]{1,0:T(8,128)S(1)}) custom-call(f32[32,512]{1,0:T(8,128)S(1)} %bitcast.16, f32[2,32,512]{2,1,0:T(8,128)S(1)} %bitcast.14, s32[1,512]{1,0:T(1,128)S(1)} %bitcast.21, f32[104,512]{1,0:T(8,128)S(1)} %collective-permute-done.other_ref.refs_1_, ...), custom_call_target="tpu_custom_call" | custom-call | flops 20000000000 | bytes 100000 | tf_op jit(solution)/shard_map/net_moments/pallas_call | solution.py:296
  19.6 0.0 collective-permute-done.3.refs_4_
  19.6 0.0 collective-permute-done.2.refs_3_
  19.6 0.0 collective-permute-done.1.refs_2_
  19.6 0.0 copy-start
  19.7 0.1 collective-permute-start.4
  19.8 5.3 %collective-permute-start.5 = (f32[128,128]{1,0:T(8,128)S(1)}, f32[128,128]{1,0:T(8,128)S(1)}, u32[]{:S(2)}, u32[]{:S(2)}) collective-permute-start(f32[128,128]{1,0:T(8,128)S(1)} %get-tuple-element.26), channel_id=1, source_target_pairs={{0,8},{8,0},{16,24},{24,16},{1,9},{9,1},{17,25},{25,17},{2,10},{10... | collective-permute-start | bytes 196616 | tf_op jit(solution)/shard_map/ppermute | solution.py:292
  25.1 2.6 %collective-permute-start.6 = (f32[128,128]{1,0:T(8,128)S(1)}, f32[128,128]{1,0:T(8,128)S(1)}, u32[]{:S(2)}, u32[]{:S(2)}) collective-permute-start(f32[128,128]{1,0:T(8,128)S(1)} %get-tuple-element.27), channel_id=1, source_target_pairs={{0,16},{8,24},{16,0},{24,8},{1,17},{9,25},{17,1},{25,9},{2,18},{10... | collective-permute-start | bytes 196616 | tf_op jit(solution)/shard_map/ppermute | solution.py:292
  27.7 0.0 copy-start.7
  27.7 0.0 collective-permute-start.7
  27.7 0.0 collective-permute-done.4.refs_5_
  27.7 0.0 copy-done
  27.7 0.7 %copy-done.7 = s32[256]{0:T(256)S(1)} copy-done((s32[256]{0:T(256)S(1)}, s32[256]{0:T(256)}, u32[]{:S(2)}) %copy-start.7) | copy-done | bytes 1048
  28.4 4.1 %gram_first_pivots.1 = (f32[64,64]{1,0:T(8,128)S(1)}, f32[64,64]{1,0:T(8,128)S(1)}, f32[256,128]{1,0:T(8,128)S(1)}) custom-call(f32[72,512]{1,0:T(8,128)S(1)} %copy-done, f32[104,512]{1,0:T(8,128)S(1)} %collective-permute-done.other_ref.refs_1_, f32[72,512]{1,0:T(8,128)S(1)} %collective-permute-done.1.refs_2_, f32[72,512]{1,0:T(8,128)S(1)} %collective-permute-done.2.refs_3_, ...), custom_call_target="tpu_custom_call" | custom-call | flops 5000000000 | bytes 100000 | tf_op jit(solution)/shard_map/gram_first_pivots/pallas_call | solution.py:296
  32.5 0.0 collective-permute-done.5.refs_1_
  32.5 0.4 collective-permute-done.6.refs_2_
  32.9 0.9 %collective-permute-done.7.refs_3_ = f32[128,128]{1,0:T(8,128)S(1)} collective-permute-done((f32[128,128]{1,0:T(8,128)S(1)}, f32[128,128]{1,0:T(8,128)S(1)}, u32[]{:S(2)}, u32[]{:S(2)}) %collective-permute-start.7) | collective-permute-done | bytes 65568 | tf_op jit(solution)/shard_map/ppermute | solution.py:292
  33.8 2.5 %collective-permute-start.10 = (f32[128,128]{1,0:T(8,128)S(1)}, f32[128,128]{1,0:T(8,128)S(1)}, u32[]{:S(2)}, u32[]{:S(2)}) collective-permute-start(f32[128,128]{1,0:T(8,128)S(1)} %group_sum.1.refs_0_), channel_id=1, source_target_pairs={{0,6},{1,7},{2,4},{3,5},{4,2},{5,3},{6,0},{7,1},{8,14},{9,15},{10,... | collective-permute-start | bytes 196616 | tf_op jit(solution)/shard_map/ppermute | solution.py:292
  36.3 0.5 %collective-permute-start.9 = (f32[128,128]{1,0:T(8,128)S(1)}, f32[128,128]{1,0:T(8,128)S(1)}, u32[]{:S(2)}, u32[]{:S(2)}) collective-permute-start(f32[128,128]{1,0:T(8,128)S(1)} %group_sum.1.refs_0_), channel_id=1, source_target_pairs={{0,4},{1,5},{2,6},{3,7},{4,0},{5,1},{6,2},{7,3},{8,12},{9,13},{10,... | collective-permute-start | bytes 196616 | tf_op jit(solution)/shard_map/ppermute | solution.py:292
  36.8 0.5 %collective-permute-start.8 = (f32[128,128]{1,0:T(8,128)S(1)}, f32[128,128]{1,0:T(8,128)S(1)}, u32[]{:S(2)}, u32[]{:S(2)}) collective-permute-start(f32[128,128]{1,0:T(8,128)S(1)} %group_sum.1.refs_0_), channel_id=1, source_target_pairs={{0,2},{1,3},{2,0},{3,1},{4,6},{5,7},{6,4},{7,5},{8,10},{9,11},{10,... | collective-permute-start | bytes 196616 | tf_op jit(solution)/shard_map/ppermute | solution.py:292
  37.4 2.8 %gram_inverse.1.refs_4_ = f32[128,128]{1,0:T(8,128)S(1)} custom-call(f32[64,64]{1,0:T(8,128)S(1)} %get-tuple-element.29.gram_ref, f32[64,64]{1,0:T(8,128)S(1)} %get-tuple-element.30.mat_ref), custom_call_target="tpu_custom_call" | custom-call | flops 3000000000 | bytes 100000 | tf_op jit(solution)/shard_map/gram_inverse/pallas_call | solution.py:296
  40.1 0.0 collective-permute-done.10.refs_3_
  40.1 0.5 %collective-permute-done.9.refs_2_ = f32[128,128]{1,0:T(8,128)S(1)} collective-permute-done((f32[128,128]{1,0:T(8,128)S(1)}, f32[128,128]{1,0:T(8,128)S(1)}, u32[]{:S(2)}, u32[]{:S(2)}) %collective-permute-start.9) | collective-permute-done | bytes 65568 | tf_op jit(solution)/shard_map/ppermute | solution.py:292
  40.6 0.5 %collective-permute-done.8.refs_1_ = f32[128,128]{1,0:T(8,128)S(1)} collective-permute-done((f32[128,128]{1,0:T(8,128)S(1)}, f32[128,128]{1,0:T(8,128)S(1)}, u32[]{:S(2)}, u32[]{:S(2)}) %collective-permute-start.8) | collective-permute-done | bytes 65568 | tf_op jit(solution)/shard_map/ppermute | solution.py:292
  41.1 0.2 set_coeffs.1.mine_ref
  41.3 0.1 collective-permute-start.11
  41.4 1.2 %collective-permute-done.11.other_ref = f32[128,128]{1,0:T(8,128)S(1)} collective-permute-done((f32[128,128]{1,0:T(8,128)S(1)}, f32[128,128]{1,0:T(8,128)S(1)}, u32[]{:S(2)}, u32[]{:S(2)}) %collective-permute-start.11) | collective-permute-done | bytes 65568 | tf_op jit(solution)/shard_map/ppermute | solution.py:292
  42.6 2.7 %set_exposure.1 = (f32[2,256,512]{2,1,0:T(8,128)}, f32[2,256]{1,0:T(2,128)}) custom-call(f32[128,128]{1,0:T(8,128)S(1)} %set_coeffs.1.mine_ref, f32[128,128]{1,0:T(8,128)S(1)} %collective-permute-done.11.other_ref, f32[256,128]{1,0:T(8,128)S(1)} %get-tuple-element.31.limits_ref, f32[72,512]{1,0:T(8,128)S(1)} %copy-done, ...), custom_call_target="tpu_custom_call" | custom-call | flops 2000000000 | bytes 100000 | tf_op jit(solution)/shard_map/set_exposure/pallas_call | solution.py:296
  (2 shorter events, 0.0 us)
Async XLA Ops:
  0.6 6.3 %copy-start.1 = (f32[2,512,32]{1,2,0:T(8,128)S(1)}, f32[2,512,32]{1,2,0:T(8,128)}, u32[]{:S(2)}) copy-start(f32[2,512,32]{1,2,0:T(8,128)} %param.10) | copy-start | bytes 393220
  0.6 6.3 %copy-start.2 = (f32[512,32]{0,1:T(8,128)S(1)}, f32[512,32]{0,1:T(8,128)}, u32[]{:S(2)}) copy-start(f32[512,32]{0,1:T(8,128)} %param.9) | copy-start | bytes 196612
  0.7 6.3 %copy-start.3 = (f32[8192]{0:T(1024)S(1)}, f32[8192]{0:T(1024)}, u32[]{:S(2)}) copy-start(f32[8192]{0:T(1024)} %param.12) | copy-start | bytes 98308
  0.7 6.3 %copy-start.4 = (f32[8192]{0:T(1024)S(1)}, f32[8192]{0:T(1024)}, u32[]{:S(2)}) copy-start(f32[8192]{0:T(1024)} %param.13) | copy-start | bytes 98308
  0.7 6.3 %copy-start.5 = (s32[8192]{0:T(1024)S(1)}, s32[8192]{0:T(1024)}, u32[]{:S(2)}) copy-start(s32[8192]{0:T(1024)} %param.14) | copy-start | bytes 98308
  2.4 4.5 %collective-permute-start = (f32[104,512]{1,0:T(8,128)}, f32[104,512]{1,0:T(8,128)S(1)}, u32[]{:S(2)}, u32[]{:S(2)}) collective-permute-start(f32[104,512]{1,0:T(8,128)} %get-tuple-element.18), channel_id=1, source_target_pairs={{0,1},{1,0},{2,3},{3,2},{4,5},{5,4},{6,7},{7,6},{8,9},{9,8},{10,11... | collective-permute-start | bytes 638984 | tf_op jit(solution)/shard_map/ppermute | solution.py:292
  2.9 16.7 %collective-permute-start.3 = (f32[72,512]{1,0:T(8,128)}, f32[72,512]{1,0:T(8,128)S(1)}, u32[]{:S(2)}, u32[]{:S(2)}) collective-permute-start(f32[72,512]{1,0:T(8,128)} %get-tuple-element.17.refs_0_), channel_id=1, source_target_pairs={{0,6},{1,7},{2,4},{3,5},{4,2},{5,3},{6,0},{7,1},{8,14},{9,15},{10,... | collective-permute-start | bytes 442376 | tf_op jit(solution)/shard_map/ppermute | solution.py:292
  6.3 13.3 %collective-permute-start.2 = (f32[72,512]{1,0:T(8,128)}, f32[72,512]{1,0:T(8,128)S(1)}, u32[]{:S(2)}, u32[]{:S(2)}) collective-permute-start(f32[72,512]{1,0:T(8,128)} %get-tuple-element.17.refs_0_), channel_id=1, source_target_pairs={{0,4},{1,5},{2,6},{3,7},{4,0},{5,1},{6,2},{7,3},{8,12},{9,13},{10,... | collective-permute-start | bytes 442376 | tf_op jit(solution)/shard_map/ppermute | solution.py:292
  6.8 12.8 %collective-permute-start.1 = (f32[72,512]{1,0:T(8,128)}, f32[72,512]{1,0:T(8,128)S(1)}, u32[]{:S(2)}, u32[]{:S(2)}) collective-permute-start(f32[72,512]{1,0:T(8,128)} %get-tuple-element.17.refs_0_), channel_id=1, source_target_pairs={{0,2},{1,3},{2,0},{3,1},{4,6},{5,7},{6,4},{7,5},{8,10},{9,11},{10,... | collective-permute-start | bytes 442376 | tf_op jit(solution)/shard_map/ppermute | solution.py:292
  7.0 0.7 %copy-start.6 = (s32[512]{0:T(512)S(1)}, s32[512]{0:T(512)}, u32[]{:S(2)}) copy-start(s32[512]{0:T(512)} %param.16) | copy-start | bytes 6148
  19.6 8.1 %copy-start = (f32[72,512]{1,0:T(8,128)S(1)}, f32[72,512]{1,0:T(8,128)}, u32[]{:S(2)}) copy-start(f32[72,512]{1,0:T(8,128)} %get-tuple-element.17.refs_0_) | copy-start | bytes 442372
  19.7 8.0 %collective-permute-start.4 = (f32[3,72,512]{2,1,0:T(8,128)S(1)}, f32[3,72,512]{2,1,0:T(8,128)S(1)}, u32[]{:S(2)}, u32[]{:S(2)}) collective-permute-start(f32[3,72,512]{2,1,0:T(8,128)S(1)} %pad_maximum_fusion), channel_id=1, source_target_pairs={{0,1},{1,0},{2,3},{3,2},{4,5},{5,4},{6,7},{7,6},{8,9},{9,8},{10,11... | collective-permute-start | bytes 1327112 | tf_op jit(solution)/shard_map/ppermute | solution.py:292
  19.8 12.7 %collective-permute-start.5 = (f32[128,128]{1,0:T(8,128)S(1)}, f32[128,128]{1,0:T(8,128)S(1)}, u32[]{:S(2)}, u32[]{:S(2)}) collective-permute-start(f32[128,128]{1,0:T(8,128)S(1)} %get-tuple-element.26), channel_id=1, source_target_pairs={{0,8},{8,0},{16,24},{24,16},{1,9},{9,1},{17,25},{25,17},{2,10},{10... | collective-permute-start | bytes 196616 | tf_op jit(solution)/shard_map/ppermute | solution.py:292
  25.1 7.8 %collective-permute-start.6 = (f32[128,128]{1,0:T(8,128)S(1)}, f32[128,128]{1,0:T(8,128)S(1)}, u32[]{:S(2)}, u32[]{:S(2)}) collective-permute-start(f32[128,128]{1,0:T(8,128)S(1)} %get-tuple-element.27), channel_id=1, source_target_pairs={{0,16},{8,24},{16,0},{24,8},{1,17},{9,25},{17,1},{25,9},{2,18},{10... | collective-permute-start | bytes 196616 | tf_op jit(solution)/shard_map/ppermute | solution.py:292
  27.7 0.7 %copy-start.7 = (s32[256]{0:T(256)S(1)}, s32[256]{0:T(256)}, u32[]{:S(2)}) copy-start(s32[256]{0:T(256)} %param.17) | copy-start | bytes 3076
  27.7 6.1 %collective-permute-start.7 = (f32[128,128]{1,0:T(8,128)S(1)}, f32[128,128]{1,0:T(8,128)S(1)}, u32[]{:S(2)}, u32[]{:S(2)}) collective-permute-start(f32[128,128]{1,0:T(8,128)S(1)} %get-tuple-element.28), channel_id=1, source_target_pairs={{0,24},{8,16},{16,8},{24,0},{1,25},{9,17},{17,9},{25,1},{2,26},{10... | collective-permute-start | bytes 196616 | tf_op jit(solution)/shard_map/ppermute | solution.py:292
  33.8 6.3 %collective-permute-start.10 = (f32[128,128]{1,0:T(8,128)S(1)}, f32[128,128]{1,0:T(8,128)S(1)}, u32[]{:S(2)}, u32[]{:S(2)}) collective-permute-start(f32[128,128]{1,0:T(8,128)S(1)} %group_sum.1.refs_0_), channel_id=1, source_target_pairs={{0,6},{1,7},{2,4},{3,5},{4,2},{5,3},{6,0},{7,1},{8,14},{9,15},{10,... | collective-permute-start | bytes 196616 | tf_op jit(solution)/shard_map/ppermute | solution.py:292
  36.3 4.3 %collective-permute-start.9 = (f32[128,128]{1,0:T(8,128)S(1)}, f32[128,128]{1,0:T(8,128)S(1)}, u32[]{:S(2)}, u32[]{:S(2)}) collective-permute-start(f32[128,128]{1,0:T(8,128)S(1)} %group_sum.1.refs_0_), channel_id=1, source_target_pairs={{0,4},{1,5},{2,6},{3,7},{4,0},{5,1},{6,2},{7,3},{8,12},{9,13},{10,... | collective-permute-start | bytes 196616 | tf_op jit(solution)/shard_map/ppermute | solution.py:292
  36.8 4.3 %collective-permute-start.8 = (f32[128,128]{1,0:T(8,128)S(1)}, f32[128,128]{1,0:T(8,128)S(1)}, u32[]{:S(2)}, u32[]{:S(2)}) collective-permute-start(f32[128,128]{1,0:T(8,128)S(1)} %group_sum.1.refs_0_), channel_id=1, source_target_pairs={{0,2},{1,3},{2,0},{3,1},{4,6},{5,7},{6,4},{7,5},{8,10},{9,11},{10,... | collective-permute-start | bytes 196616 | tf_op jit(solution)/shard_map/ppermute | solution.py:292
  41.3 1.3 %collective-permute-start.11 = (f32[128,128]{1,0:T(8,128)S(1)}, f32[128,128]{1,0:T(8,128)S(1)}, u32[]{:S(2)}, u32[]{:S(2)}) collective-permute-start(f32[128,128]{1,0:T(8,128)S(1)} %set_coeffs.1.mine_ref), channel_id=1, source_target_pairs={{0,1},{1,0},{2,3},{3,2},{4,5},{5,4},{6,7},{7,6},{8,9},{9,8},{10,11... | collective-permute-start | bytes 196616 | tf_op jit(solution)/shard_map/ppermute | solution.py:292

commit v9 on v8

--- a/solution.py
+++ b/solution.py
@@ -11,6 +11,8 @@
 ROOT_HALF = 0.7071067811865476
 F32 = jnp.float32
 BF16 = jnp.bfloat16
+F8 = jnp.float8_e5m2
+SCALE = 256.0
 TILE = 512
 CHUNK = 1024
 SLOTS = 4
@@ -78,15 +80,17 @@
     whole_ref[2 * factors + PAD :, :] = shocks_ref[1]
 
 
-def prepare(number, start, shocks, weight_row, states_scr, wide_scr):
+def prepare(number, start, shocks, weight_row, states_scr, wide_scr, few_scr):
     core = lax.axis_index("path") & 1
     factors, paths = start.shape
     mine = pl.ds(number * paths, paths)
     second = 0.8 * start + 0.6 * shocks[0]
     third = 0.8 * second + 0.6 * shocks[1]
-    hi, lo = split2(basis_rows(pick(core, start, second)) * weight_row)
+    weighted = basis_rows(pick(core, start, second)) * weight_row
+    few_scr[:, mine] = weighted.astype(F8)
+    hi, lo = split2(weighted)
     wide_scr[:, mine] = jnp.concatenate([hi, lo], axis=0)
-    hi, mid, low = split3(pick(core, second, third))
+    hi, mid, low = split3(SCALE * pick(core, second, third))
     hi, mid, low = hi.astype(F32), mid.astype(F32), low.astype(F32)
     ones = jnp.where(lax.broadcasted_iota(jnp.int32, (DEPTH - 6 * factors, paths), 0) < 3, 1.0, 0.0)
     stacked = jnp.concatenate([hi, hi, mid, mid, hi, low, ones], axis=0)
@@ -98,18 +102,20 @@
     hi, mid, low = split3(load_ref[:, cols])
     for part, piece in enumerate((hi, mid, hi, mid, low, hi)):
         load_scr[slot, pl.ds(part * factors, factors), :] = piece
-    s_hi, s_mid, s_low = split3(-strike_ref[:, cols])
+    s_hi, s_mid, s_low = split3(-SCALE * strike_ref[:, cols])
     rows = lax.broadcasted_iota(jnp.int32, (16, TILE), 0)
     strike_rows = jnp.where(rows == 1, s_mid.astype(F32), jnp.where(rows == 2, s_low.astype(F32), 0.0))
     strike_rows = jnp.where(rows == 0, s_hi.astype(F32), strike_rows)
     load_scr[slot, pl.ds(6 * factors, 16), :] = strike_rows.astype(BF16)
 
 
-def chunk_moments(pay, rows, wide_scr):
+def chunk_moments(pay, rows, wide_scr, few_scr):
     wide = wide_scr.shape[0] // 2
-    hi, lo = split2(jnp.maximum(pay, 0.0))
+    cash = jnp.maximum(pay, 0.0)
+    hi = cash.astype(BF16)
+    lo = (cash - hi.astype(F32)).astype(F8)
     both = mm(wide_scr[:, rows], hi)
-    return both[:wide] + (both[wide:] + mm(wide_scr[:wide, rows], lo))
+    return both[:wide] + (both[wide:] + mm(few_scr[:, rows], lo))
 
 
 def tile_at(index):
@@ -124,7 +130,7 @@
     groups, start_ref, shocks_ref, weights_ref, other_ref, load_hbm, strike_hbm, notional_hbm, set_hbm, *refs
 ):
     outs = refs[:groups]
-    *staged, sems, net_scr, states_scr, wide_scr, load_scr, part_scr, hot_scr = refs[groups:]
+    *staged, sems, net_scr, states_scr, wide_scr, few_scr, load_scr, part_scr, hot_scr = refs[groups:]
     load_ref, strike_ref, notional_ref, set_ref = staged
     moves = copies((load_hbm, strike_hbm, notional_hbm, set_hbm), staged, sems)
     for move in moves:
@@ -138,9 +144,9 @@
     load_scr[...] = jnp.zeros_like(load_scr)
     for ref in (net_scr, part_scr, hot_scr):
         ref[...] = jnp.zeros_like(ref)
-    prepare(0, start_ref[...], shocks_ref[...], weights_ref[...].astype(F32), states_scr, wide_scr)
+    prepare(0, start_ref[...], shocks_ref[...], weights_ref[...].astype(F32), states_scr, wide_scr, few_scr)
     shocks = (other_ref[factors : 2 * factors, :], other_ref[2 * factors + PAD :, :])
-    prepare(1, other_ref[:factors, :], shocks, weights_of(other_ref, factors), states_scr, wide_scr)
+    prepare(1, other_ref[:factors, :], shocks, weights_of(other_ref, factors), states_scr, wide_scr, few_scr)
     for move in moves:
         move.wait()
 
@@ -149,7 +155,7 @@
     def keep_tile(index, slot, moment):
         cols = tile_at(index)
         slot_ids = index * TILE + lax.broadcasted_iota(jnp.int32, (1, TILE), 1)
-        hi, lo = split2(moment * jnp.where(slot_ids < filled, notional_ref[:, cols], 0.0))
+        hi, lo = split2(moment * jnp.where(slot_ids < filled, notional_ref[:, cols] * (1.0 / SCALE), 0.0))
         both = jnp.concatenate([hi, lo], axis=0)
         both = both.reshape(both.shape[0] // rows, rows, TILE)
         sets = set_ref[:, cols]
@@ -177,7 +183,7 @@
                 pays[number] = mm(states_scr[chunk, :], load_scr[slot])
             if number > 0:
                 slot, chunk = stages[number - 1]
-                part = chunk_moments(pays.pop(number - 1), chunk, wide_scr)
+                part = chunk_moments(pays.pop(number - 1), chunk, wide_scr, few_scr)
                 moment = part if moment is None else moment + part
                 if number % len(chunks) == 0:
                     keep_tile(SLOTS * turn + slot, slot, moment)
@@ -341,6 +347,7 @@
             pltpu.VMEM((2 * wide * groups, owned), F32),
             pltpu.VMEM((2 * paths, DEPTH), BF16),
             pltpu.VMEM((2 * wide, 2 * paths), BF16),
+            pltpu.VMEM((wide, 2 * paths), F8),
             pltpu.VMEM((SLOTS, DEPTH, TILE), BF16),
             pltpu.VMEM((2 * wide * groups, SLOTS * TILE), BF16),
             pltpu.VMEM((owned, SLOTS * TILE), BF16),

time: 45.6 us -> 44.9 us (0.985)
  starting transfers between devices: 16.1 us -> 12.9 us
  Pallas kernels: 23.5 us -> 26.1 us
    ppermute x12, starting transfers between devices: 16.1 us -> 12.9 us  [swap(): lax.ppermute(x, axis, [(i, i ^ away) for i in range(lax.axis_size(axis))])]
    pallas_call x7, Pallas kernels: 23.5 us -> 26.1 us  [run(): pl.pallas_call(kernel, out_shape=out, in_specs=specs, out_specs=out_specs...]
  transfers between devices with their start and end apart: 12 -> 12, of which waited for: 5 -> 5; matrix products, arithmetic and copies ran while one was open for 0% -> 0% of each run, Pallas kernels for 42% -> 48%
where the time goes in v9:
time: 44.9 us; the launch traced here: 44.6 us
  Pallas kernels  26.1 us (58%)
  starting transfers between devices  12.9 us (29%)
  waiting for transfers between devices  3.51 us (8%)
  local copies, waits for them, and re-layouts  1.33 us (3%)
  between operations  0.82 us (2%)
    pallas_call x7, Pallas kernels, run(): pl.pallas_call(kernel, out_shape=out, in_specs=specs, out_specs=out_specs...  26.1 us
    ppermute x12, starting transfers between devices, swap(): lax.ppermute(x, axis, [(i, i ^ away) for i in range(lax.axis_size(axis))])  12.9 us
    ppermute x12, waiting for transfers between devices, swap(): lax.ppermute(x, axis, [(i, i ^ away) for i in range(lax.axis_size(axis))])  3.51 us
    unnamed x16, local copies, waits for them, and re-layouts  1.33 us
  transfers between devices with their start and end apart: 12, of which 5 were waited for; matrix products, arithmetic and copies ran while one was open for 0% of the time, Pallas kernels for 48%

profile of v9, /device:TPU:0, one launch (start us, length us, event | category | flops | bytes accessed | tf_op | source)
XLA Modules:
  0.0 44.6 jit_solution(16288617760188942783)
XLA Ops:
  0.6 0.0 copy-start.1
  0.6 0.0 copy-start.2
  0.7 0.0 copy-start.3
  0.7 0.0 copy-start.4
  0.7 0.0 copy-start.5
  0.7 1.7 %pack_states.1 = (f32[72,512]{1,0:T(8,128)}, f32[104,512]{1,0:T(8,128)}) custom-call(s32[4]{0:T(128)} %counts_ref.1, f32[32,512]{1,0:T(8,128)} %bitcast.15, f32[2,32,512]{2,1,0:T(8,128)} %bitcast.13, s32[1,512]{1,0:T(1,128)} %bitcast.20), custom_call_target="tpu_custom_call" | custom-call | flops 20000000000 | bytes 100000 | tf_op jit(solution)/shard_map/pack_states/pallas_call | solution.py:302
  2.4 0.5 %collective-permute-start = (f32[104,512]{1,0:T(8,128)}, f32[104,512]{1,0:T(8,128)S(1)}, u32[]{:S(2)}, u32[]{:S(2)}) collective-permute-start(f32[104,512]{1,0:T(8,128)} %get-tuple-element.18), channel_id=1, source_target_pairs={{0,1},{1,0},{2,3},{3,2},{4,5},{5,4},{6,7},{7,6},{8,9},{9,8},{10,11... | collective-permute-start | bytes 638984 | tf_op jit(solution)/shard_map/ppermute | solution.py:298
  2.9 3.4 %collective-permute-start.3 = (f32[72,512]{1,0:T(8,128)}, f32[72,512]{1,0:T(8,128)S(1)}, u32[]{:S(2)}, u32[]{:S(2)}) collective-permute-start(f32[72,512]{1,0:T(8,128)} %get-tuple-element.17.refs_0_), channel_id=1, source_target_pairs={{0,6},{1,7},{2,4},{3,5},{4,2},{5,3},{6,0},{7,1},{8,14},{9,15},{10,... | collective-permute-start | bytes 442376 | tf_op jit(solution)/shard_map/ppermute | solution.py:298
  6.3 0.5 %collective-permute-start.2 = (f32[72,512]{1,0:T(8,128)}, f32[72,512]{1,0:T(8,128)S(1)}, u32[]{:S(2)}, u32[]{:S(2)}) collective-permute-start(f32[72,512]{1,0:T(8,128)} %get-tuple-element.17.refs_0_), channel_id=1, source_target_pairs={{0,4},{1,5},{2,6},{3,7},{4,0},{5,1},{6,2},{7,3},{8,12},{9,13},{10,... | collective-permute-start | bytes 442376 | tf_op jit(solution)/shard_map/ppermute | solution.py:298
  6.8 0.1 collective-permute-start.1
  7.0 0.0 collective-permute-done.other_ref.refs_1_
  7.0 0.0 copy-start.6
  7.0 0.0 copy-done.1
  7.0 0.0 copy-done.2
  7.0 0.0 copy-done.3
  7.0 0.0 copy-done.4
  7.0 0.0 copy-done.5
  7.0 0.6 %copy-done.6 = s32[512]{0:T(512)S(1)} copy-done((s32[512]{0:T(512)S(1)}, s32[512]{0:T(512)}, u32[]{:S(2)}) %copy-start.6) | copy-done | bytes 2072
  7.6 14.5 %net_moments.1 = (f32[128,128]{1,0:T(8,128)S(1)}, f32[128,128]{1,0:T(8,128)S(1)}, f32[128,128]{1,0:T(8,128)S(1)}, f32[128,128]{1,0:T(8,128)S(1)}) custom-call(f32[32,512]{1,0:T(8,128)S(1)} %bitcast.16, f32[2,32,512]{2,1,0:T(8,128)S(1)} %bitcast.14, s32[1,512]{1,0:T(1,128)S(1)} %bitcast.21, f32[104,512]{1,0:T(8,128)S(1)} %collective-permute-done.other_ref.refs_1_, ...), custom_call_target="tpu_custom_call" | custom-call | flops 20000000000 | bytes 100000 | tf_op jit(solution)/shard_map/net_moments/pallas_call | solution.py:302
  22.2 0.0 collective-permute-done.3.refs_4_
  22.2 0.0 collective-permute-done.2.refs_3_
  22.2 0.0 collective-permute-done.1.refs_2_
  22.2 0.0 copy-start
  22.3 0.1 collective-permute-start.4
  22.3 2.1 %collective-permute-start.5 = (f32[128,128]{1,0:T(8,128)S(1)}, f32[128,128]{1,0:T(8,128)S(1)}, u32[]{:S(2)}, u32[]{:S(2)}) collective-permute-start(f32[128,128]{1,0:T(8,128)S(1)} %get-tuple-element.26), channel_id=1, source_target_pairs={{0,8},{8,0},{16,24},{24,16},{1,9},{9,1},{17,25},{25,17},{2,10},{10... | collective-permute-start | bytes 196616 | tf_op jit(solution)/shard_map/ppermute | solution.py:298
  24.4 2.6 %collective-permute-start.6 = (f32[128,128]{1,0:T(8,128)S(1)}, f32[128,128]{1,0:T(8,128)S(1)}, u32[]{:S(2)}, u32[]{:S(2)}) collective-permute-start(f32[128,128]{1,0:T(8,128)S(1)} %get-tuple-element.27), channel_id=1, source_target_pairs={{0,16},{8,24},{16,0},{24,8},{1,17},{9,25},{17,1},{25,9},{2,18},{10... | collective-permute-start | bytes 196616 | tf_op jit(solution)/shard_map/ppermute | solution.py:298
  27.0 0.0 copy-start.7
  27.0 0.0 collective-permute-start.7
  27.0 0.0 collective-permute-done.4.refs_5_
  27.0 0.0 copy-done
  27.0 0.7 %copy-done.7 = s32[256]{0:T(256)S(1)} copy-done((s32[256]{0:T(256)S(1)}, s32[256]{0:T(256)}, u32[]{:S(2)}) %copy-start.7) | copy-done | bytes 1048
  27.6 4.1 %gram_first_pivots.1 = (f32[64,64]{1,0:T(8,128)S(1)}, f32[64,64]{1,0:T(8,128)S(1)}, f32[256,128]{1,0:T(8,128)S(1)}) custom-call(f32[72,512]{1,0:T(8,128)S(1)} %copy-done, f32[104,512]{1,0:T(8,128)S(1)} %collective-permute-done.other_ref.refs_1_, f32[72,512]{1,0:T(8,128)S(1)} %collective-permute-done.1.refs_2_, f32[72,512]{1,0:T(8,128)S(1)} %collective-permute-done.2.refs_3_, ...), custom_call_target="tpu_custom_call" | custom-call | flops 5000000000 | bytes 100000 | tf_op jit(solution)/shard_map/gram_first_pivots/pallas_call | solution.py:302
  31.8 0.0 collective-permute-done.5.refs_1_
  31.8 0.4 collective-permute-done.6.refs_2_
  32.2 0.9 %collective-permute-done.7.refs_3_ = f32[128,128]{1,0:T(8,128)S(1)} collective-permute-done((f32[128,128]{1,0:T(8,128)S(1)}, f32[128,128]{1,0:T(8,128)S(1)}, u32[]{:S(2)}, u32[]{:S(2)}) %collective-permute-start.7) | collective-permute-done | bytes 65568 | tf_op jit(solution)/shard_map/ppermute | solution.py:298
  33.1 2.5 %collective-permute-start.10 = (f32[128,128]{1,0:T(8,128)S(1)}, f32[128,128]{1,0:T(8,128)S(1)}, u32[]{:S(2)}, u32[]{:S(2)}) collective-permute-start(f32[128,128]{1,0:T(8,128)S(1)} %group_sum.1.refs_0_), channel_id=1, source_target_pairs={{0,6},{1,7},{2,4},{3,5},{4,2},{5,3},{6,0},{7,1},{8,14},{9,15},{10,... | collective-permute-start | bytes 196616 | tf_op jit(solution)/shard_map/ppermute | solution.py:298
  35.6 0.5 %collective-permute-start.9 = (f32[128,128]{1,0:T(8,128)S(1)}, f32[128,128]{1,0:T(8,128)S(1)}, u32[]{:S(2)}, u32[]{:S(2)}) collective-permute-start(f32[128,128]{1,0:T(8,128)S(1)} %group_sum.1.refs_0_), channel_id=1, source_target_pairs={{0,4},{1,5},{2,6},{3,7},{4,0},{5,1},{6,2},{7,3},{8,12},{9,13},{10,... | collective-permute-start | bytes 196616 | tf_op jit(solution)/shard_map/ppermute | solution.py:298
  36.1 0.5 %collective-permute-start.8 = (f32[128,128]{1,0:T(8,128)S(1)}, f32[128,128]{1,0:T(8,128)S(1)}, u32[]{:S(2)}, u32[]{:S(2)}) collective-permute-start(f32[128,128]{1,0:T(8,128)S(1)} %group_sum.1.refs_0_), channel_id=1, source_target_pairs={{0,2},{1,3},{2,0},{3,1},{4,6},{5,7},{6,4},{7,5},{8,10},{9,11},{10,... | collective-permute-start | bytes 196616 | tf_op jit(solution)/shard_map/ppermute | solution.py:298
  36.7 2.8 %gram_inverse.1.refs_4_ = f32[128,128]{1,0:T(8,128)S(1)} custom-call(f32[64,64]{1,0:T(8,128)S(1)} %get-tuple-element.29.gram_ref, f32[64,64]{1,0:T(8,128)S(1)} %get-tuple-element.30.mat_ref), custom_call_target="tpu_custom_call" | custom-call | flops 3000000000 | bytes 100000 | tf_op jit(solution)/shard_map/gram_inverse/pallas_call | solution.py:302
  39.4 0.0 collective-permute-done.10.refs_3_
  39.4 0.5 %collective-permute-done.9.refs_2_ = f32[128,128]{1,0:T(8,128)S(1)} collective-permute-done((f32[128,128]{1,0:T(8,128)S(1)}, f32[128,128]{1,0:T(8,128)S(1)}, u32[]{:S(2)}, u32[]{:S(2)}) %collective-permute-start.9) | collective-permute-done | bytes 65568 | tf_op jit(solution)/shard_map/ppermute | solution.py:298
  39.9 0.5 %collective-permute-done.8.refs_1_ = f32[128,128]{1,0:T(8,128)S(1)} collective-permute-done((f32[128,128]{1,0:T(8,128)S(1)}, f32[128,128]{1,0:T(8,128)S(1)}, u32[]{:S(2)}, u32[]{:S(2)}) %collective-permute-start.8) | collective-permute-done | bytes 65568 | tf_op jit(solution)/shard_map/ppermute | solution.py:298
  40.4 0.2 set_coeffs.1.mine_ref
  40.6 0.1 collective-permute-start.11
  40.7 1.2 %collective-permute-done.11.other_ref = f32[128,128]{1,0:T(8,128)S(1)} collective-permute-done((f32[128,128]{1,0:T(8,128)S(1)}, f32[128,128]{1,0:T(8,128)S(1)}, u32[]{:S(2)}, u32[]{:S(2)}) %collective-permute-start.11) | collective-permute-done | bytes 65568 | tf_op jit(solution)/shard_map/ppermute | solution.py:298
  41.9 2.7 %set_exposure.1 = (f32[2,256,512]{2,1,0:T(8,128)}, f32[2,256]{1,0:T(2,128)}) custom-call(f32[128,128]{1,0:T(8,128)S(1)} %set_coeffs.1.mine_ref, f32[128,128]{1,0:T(8,128)S(1)} %collective-permute-done.11.other_ref, f32[256,128]{1,0:T(8,128)S(1)} %get-tuple-element.31.limits_ref, f32[72,512]{1,0:T(8,128)S(1)} %copy-done, ...), custom_call_target="tpu_custom_call" | custom-call | flops 2000000000 | bytes 100000 | tf_op jit(solution)/shard_map/set_exposure/pallas_call | solution.py:302
  (2 shorter events, 0.0 us)
Async XLA Ops:
  0.6 6.3 %copy-start.1 = (f32[2,512,32]{1,2,0:T(8,128)S(1)}, f32[2,512,32]{1,2,0:T(8,128)}, u32[]{:S(2)}) copy-start(f32[2,512,32]{1,2,0:T(8,128)} %param.10) | copy-start | bytes 393220
  0.6 6.3 %copy-start.2 = (f32[512,32]{0,1:T(8,128)S(1)}, f32[512,32]{0,1:T(8,128)}, u32[]{:S(2)}) copy-start(f32[512,32]{0,1:T(8,128)} %param.9) | copy-start | bytes 196612
  0.7 6.3 %copy-start.3 = (f32[8192]{0:T(1024)S(1)}, f32[8192]{0:T(1024)}, u32[]{:S(2)}) copy-start(f32[8192]{0:T(1024)} %param.12) | copy-start | bytes 98308
  0.7 6.3 %copy-start.4 = (f32[8192]{0:T(1024)S(1)}, f32[8192]{0:T(1024)}, u32[]{:S(2)}) copy-start(f32[8192]{0:T(1024)} %param.13) | copy-start | bytes 98308
  0.7 6.3 %copy-start.5 = (s32[8192]{0:T(1024)S(1)}, s32[8192]{0:T(1024)}, u32[]{:S(2)}) copy-start(s32[8192]{0:T(1024)} %param.14) | copy-start | bytes 98308
  2.4 4.5 %collective-permute-start = (f32[104,512]{1,0:T(8,128)}, f32[104,512]{1,0:T(8,128)S(1)}, u32[]{:S(2)}, u32[]{:S(2)}) collective-permute-start(f32[104,512]{1,0:T(8,128)} %get-tuple-element.18), channel_id=1, source_target_pairs={{0,1},{1,0},{2,3},{3,2},{4,5},{5,4},{6,7},{7,6},{8,9},{9,8},{10,11... | collective-permute-start | bytes 638984 | tf_op jit(solution)/shard_map/ppermute | solution.py:298
  2.9 19.3 %collective-permute-start.3 = (f32[72,512]{1,0:T(8,128)}, f32[72,512]{1,0:T(8,128)S(1)}, u32[]{:S(2)}, u32[]{:S(2)}) collective-permute-start(f32[72,512]{1,0:T(8,128)} %get-tuple-element.17.refs_0_), channel_id=1, source_target_pairs={{0,6},{1,7},{2,4},{3,5},{4,2},{5,3},{6,0},{7,1},{8,14},{9,15},{10,... | collective-permute-start | bytes 442376 | tf_op jit(solution)/shard_map/ppermute | solution.py:298
  6.3 15.9 %collective-permute-start.2 = (f32[72,512]{1,0:T(8,128)}, f32[72,512]{1,0:T(8,128)S(1)}, u32[]{:S(2)}, u32[]{:S(2)}) collective-permute-start(f32[72,512]{1,0:T(8,128)} %get-tuple-element.17.refs_0_), channel_id=1, source_target_pairs={{0,4},{1,5},{2,6},{3,7},{4,0},{5,1},{6,2},{7,3},{8,12},{9,13},{10,... | collective-permute-start | bytes 442376 | tf_op jit(solution)/shard_map/ppermute | solution.py:298
  6.8 15.4 %collective-permute-start.1 = (f32[72,512]{1,0:T(8,128)}, f32[72,512]{1,0:T(8,128)S(1)}, u32[]{:S(2)}, u32[]{:S(2)}) collective-permute-start(f32[72,512]{1,0:T(8,128)} %get-tuple-element.17.refs_0_), channel_id=1, source_target_pairs={{0,2},{1,3},{2,0},{3,1},{4,6},{5,7},{6,4},{7,5},{8,10},{9,11},{10,... | collective-permute-start | bytes 442376 | tf_op jit(solution)/shard_map/ppermute | solution.py:298
  7.0 0.7 %copy-start.6 = (s32[512]{0:T(512)S(1)}, s32[512]{0:T(512)}, u32[]{:S(2)}) copy-start(s32[512]{0:T(512)} %param.16) | copy-start | bytes 6148
  22.2 4.8 %copy-start = (f32[72,512]{1,0:T(8,128)S(1)}, f32[72,512]{1,0:T(8,128)}, u32[]{:S(2)}) copy-start(f32[72,512]{1,0:T(8,128)} %get-tuple-element.17.refs_0_) | copy-start | bytes 442372
  22.3 4.7 %collective-permute-start.4 = (f32[3,72,512]{2,1,0:T(8,128)S(1)}, f32[3,72,512]{2,1,0:T(8,128)S(1)}, u32[]{:S(2)}, u32[]{:S(2)}) collective-permute-start(f32[3,72,512]{2,1,0:T(8,128)S(1)} %pad_maximum_fusion), channel_id=1, source_target_pairs={{0,1},{1,0},{2,3},{3,2},{4,5},{5,4},{6,7},{7,6},{8,9},{9,8},{10,11... | collective-permute-start | bytes 1327112 | tf_op jit(solution)/shard_map/ppermute | solution.py:298
  22.3 9.5 %collective-permute-start.5 = (f32[128,128]{1,0:T(8,128)S(1)}, f32[128,128]{1,0:T(8,128)S(1)}, u32[]{:S(2)}, u32[]{:S(2)}) collective-permute-start(f32[128,128]{1,0:T(8,128)S(1)} %get-tuple-element.26), channel_id=1, source_target_pairs={{0,8},{8,0},{16,24},{24,16},{1,9},{9,1},{17,25},{25,17},{2,10},{10... | collective-permute-start | bytes 196616 | tf_op jit(solution)/shard_map/ppermute | solution.py:298
  24.4 7.8 %collective-permute-start.6 = (f32[128,128]{1,0:T(8,128)S(1)}, f32[128,128]{1,0:T(8,128)S(1)}, u32[]{:S(2)}, u32[]{:S(2)}) collective-permute-start(f32[128,128]{1,0:T(8,128)S(1)} %get-tuple-element.27), channel_id=1, source_target_pairs={{0,16},{8,24},{16,0},{24,8},{1,17},{9,25},{17,1},{25,9},{2,18},{10... | collective-permute-start | bytes 196616 | tf_op jit(solution)/shard_map/ppermute | solution.py:298
  27.0 0.7 %copy-start.7 = (s32[256]{0:T(256)S(1)}, s32[256]{0:T(256)}, u32[]{:S(2)}) copy-start(s32[256]{0:T(256)} %param.17) | copy-start | bytes 3076
  27.0 6.1 %collective-permute-start.7 = (f32[128,128]{1,0:T(8,128)S(1)}, f32[128,128]{1,0:T(8,128)S(1)}, u32[]{:S(2)}, u32[]{:S(2)}) collective-permute-start(f32[128,128]{1,0:T(8,128)S(1)} %get-tuple-element.28), channel_id=1, source_target_pairs={{0,24},{8,16},{16,8},{24,0},{1,25},{9,17},{17,9},{25,1},{2,26},{10... | collective-permute-start | bytes 196616 | tf_op jit(solution)/shard_map/ppermute | solution.py:298
  33.1 6.3 %collective-permute-start.10 = (f32[128,128]{1,0:T(8,128)S(1)}, f32[128,128]{1,0:T(8,128)S(1)}, u32[]{:S(2)}, u32[]{:S(2)}) collective-permute-start(f32[128,128]{1,0:T(8,128)S(1)} %group_sum.1.refs_0_), channel_id=1, source_target_pairs={{0,6},{1,7},{2,4},{3,5},{4,2},{5,3},{6,0},{7,1},{8,14},{9,15},{10,... | collective-permute-start | bytes 196616 | tf_op jit(solution)/shard_map/ppermute | solution.py:298
  35.6 4.3 %collective-permute-start.9 = (f32[128,128]{1,0:T(8,128)S(1)}, f32[128,128]{1,0:T(8,128)S(1)}, u32[]{:S(2)}, u32[]{:S(2)}) collective-permute-start(f32[128,128]{1,0:T(8,128)S(1)} %group_sum.1.refs_0_), channel_id=1, source_target_pairs={{0,4},{1,5},{2,6},{3,7},{4,0},{5,1},{6,2},{7,3},{8,12},{9,13},{10,... | collective-permute-start | bytes 196616 | tf_op jit(solution)/shard_map/ppermute | solution.py:298
  36.1 4.3 %collective-permute-start.8 = (f32[128,128]{1,0:T(8,128)S(1)}, f32[128,128]{1,0:T(8,128)S(1)}, u32[]{:S(2)}, u32[]{:S(2)}) collective-permute-start(f32[128,128]{1,0:T(8,128)S(1)} %group_sum.1.refs_0_), channel_id=1, source_target_pairs={{0,2},{1,3},{2,0},{3,1},{4,6},{5,7},{6,4},{7,5},{8,10},{9,11},{10,... | collective-permute-start | bytes 196616 | tf_op jit(solution)/shard_map/ppermute | solution.py:298
  40.6 1.3 %collective-permute-start.11 = (f32[128,128]{1,0:T(8,128)S(1)}, f32[128,128]{1,0:T(8,128)S(1)}, u32[]{:S(2)}, u32[]{:S(2)}) collective-permute-start(f32[128,128]{1,0:T(8,128)S(1)} %set_coeffs.1.mine_ref), channel_id=1, source_target_pairs={{0,1},{1,0},{2,3},{3,2},{4,5},{5,4},{6,7},{7,6},{8,9},{9,8},{10,11... | collective-permute-start | bytes 196616 | tf_op jit(solution)/shard_map/ppermute | solution.py:298

commit v10 on v9

--- a/solution.py
+++ b/solution.py
@@ -91,10 +91,9 @@
     hi, lo = split2(weighted)
     wide_scr[:, mine] = jnp.concatenate([hi, lo], axis=0)
     hi, mid, low = split3(SCALE * pick(core, second, third))
-    hi, mid, low = hi.astype(F32), mid.astype(F32), low.astype(F32)
     ones = jnp.where(lax.broadcasted_iota(jnp.int32, (DEPTH - 6 * factors, paths), 0) < 3, 1.0, 0.0)
-    stacked = jnp.concatenate([hi, hi, mid, mid, hi, low, ones], axis=0)
-    states_scr[mine, :] = stacked.T.astype(BF16)
+    stacked = jnp.concatenate([hi, hi, mid, mid, hi, low, ones.astype(BF16)], axis=0)
+    states_scr[mine, :] = stacked.T
 
 
 def load_rows(cols, load_ref, strike_ref, load_scr, slot):
@@ -142,8 +141,7 @@
     bits = log2(owned)
     rows = 16
     load_scr[...] = jnp.zeros_like(load_scr)
-    for ref in (net_scr, part_scr, hot_scr):
-        ref[...] = jnp.zeros_like(ref)
+    net_scr[...] = jnp.zeros_like(net_scr)
     prepare(0, start_ref[...], shocks_ref[...], weights_ref[...].astype(F32), states_scr, wide_scr, few_scr)
     shocks = (other_ref[factors : 2 * factors, :], other_ref[2 * factors + PAD :, :])
     prepare(1, other_ref[:factors, :], shocks, weights_of(other_ref, factors), states_scr, wide_scr, few_scr)
@@ -172,7 +170,8 @@
         net_scr[...] += mm(part_scr[...], hot_scr[...], NT)
 
     def step(turn, carry):
-        add_tiles()
+        if carry is not None:
+            add_tiles()
         stages = [(slot, chunk) for slot in range(SLOTS) for chunk in chunks]
         pays, moment = {}, None
         for number in range(len(stages) + 1):
@@ -190,7 +189,8 @@
                     moment = None
         return carry
 
-    lax.fori_loop(0, (jnp.max(filled) + SLOTS * TILE - 1) // (SLOTS * TILE), step, 0)
+    step(0, None)
+    lax.fori_loop(1, (jnp.max(filled) + SLOTS * TILE - 1) // (SLOTS * TILE), step, 0)
     add_tiles()
     wide = net_scr.shape[0] // (2 * groups)
     half = owned // 2

time: 44.9 us -> 44.2 us (0.984)
  local copies, waits for them, and re-layouts: 1.33 us -> 0.67 us
    unnamed x16, local copies, waits for them, and re-layouts: 1.33 us -> 0.67 us
  transfers between devices with their start and end apart: 12 -> 12, of which waited for: 5 -> 4; matrix products, arithmetic and copies ran while one was open for 0% -> 0% of each run, Pallas kernels for 48% -> 49%
where the time goes in v10:
time: 44.2 us; the launch traced here: 44 us
  Pallas kernels  26.1 us (59%)
  starting transfers between devices  12.7 us (29%)
  waiting for transfers between devices  3.48 us (8%)
  between operations  0.97 us (2%)
  local copies, waits for them, and re-layouts  0.67 us (2%)
    pallas_call x7, Pallas kernels, run(): pl.pallas_call(kernel, out_shape=out, in_specs=specs, out_specs=out_specs...  26.1 us
    ppermute x12, starting transfers between devices, swap(): lax.ppermute(x, axis, [(i, i ^ away) for i in range(lax.axis_size(axis))])  12.7 us
    ppermute x12, waiting for transfers between devices, swap(): lax.ppermute(x, axis, [(i, i ^ away) for i in range(lax.axis_size(axis))])  3.48 us
  transfers between devices with their start and end apart: 12, of which 4 were waited for; matrix products, arithmetic and copies ran while one was open for 0% of the time, Pallas kernels for 49%

profile of v10, /device:TPU:0, one launch (start us, length us, event | category | flops | bytes accessed | tf_op | source)
XLA Modules:
  0.0 44.0 jit_solution(2298703305828299225)
XLA Ops:
  0.6 0.0 copy-start.1
  0.6 0.0 copy-start.2
  0.7 0.0 copy-start.3
  0.7 0.0 copy-start.4
  0.7 0.0 copy-start.5
  0.7 1.7 %pack_states.1 = (f32[72,512]{1,0:T(8,128)}, f32[104,512]{1,0:T(8,128)}) custom-call(s32[4]{0:T(128)} %counts_ref.1, f32[32,512]{1,0:T(8,128)} %bitcast.15, f32[2,32,512]{2,1,0:T(8,128)} %bitcast.13, s32[1,512]{1,0:T(1,128)} %bitcast.20), custom_call_target="tpu_custom_call" | custom-call | flops 20000000000 | bytes 100000 | tf_op jit(solution)/shard_map/pack_states/pallas_call | solution.py:302
  2.4 0.5 %collective-permute-start = (f32[104,512]{1,0:T(8,128)}, f32[104,512]{1,0:T(8,128)S(1)}, u32[]{:S(2)}, u32[]{:S(2)}) collective-permute-start(f32[104,512]{1,0:T(8,128)} %get-tuple-element.18), channel_id=1, source_target_pairs={{0,1},{1,0},{2,3},{3,2},{4,5},{5,4},{6,7},{7,6},{8,9},{9,8},{10,11... | collective-permute-start | bytes 638984 | tf_op jit(solution)/shard_map/ppermute | solution.py:298
  2.9 3.4 %collective-permute-start.3 = (f32[72,512]{1,0:T(8,128)}, f32[72,512]{1,0:T(8,128)S(1)}, u32[]{:S(2)}, u32[]{:S(2)}) collective-permute-start(f32[72,512]{1,0:T(8,128)} %get-tuple-element.17.refs_0_), channel_id=1, source_target_pairs={{0,6},{1,7},{2,4},{3,5},{4,2},{5,3},{6,0},{7,1},{8,14},{9,15},{10,... | collective-permute-start | bytes 442376 | tf_op jit(solution)/shard_map/ppermute | solution.py:298
  6.3 0.5 %collective-permute-start.2 = (f32[72,512]{1,0:T(8,128)}, f32[72,512]{1,0:T(8,128)S(1)}, u32[]{:S(2)}, u32[]{:S(2)}) collective-permute-start(f32[72,512]{1,0:T(8,128)} %get-tuple-element.17.refs_0_), channel_id=1, source_target_pairs={{0,4},{1,5},{2,6},{3,7},{4,0},{5,1},{6,2},{7,3},{8,12},{9,13},{10,... | collective-permute-start | bytes 442376 | tf_op jit(solution)/shard_map/ppermute | solution.py:298
  6.8 0.1 collective-permute-start.1
  7.0 0.0 collective-permute-done.other_ref.refs_1_
  7.0 0.0 copy-start.6
  7.0 0.0 copy-done.1
  7.0 0.0 copy-done.2
  7.0 0.0 copy-done.3
  7.0 0.0 copy-done.4
  7.0 0.0 copy-done.5
  7.0 0.6 %copy-done.6 = s32[512]{0:T(512)S(1)} copy-done((s32[512]{0:T(512)S(1)}, s32[512]{0:T(512)}, u32[]{:S(2)}) %copy-start.6) | copy-done | bytes 2072
  7.6 14.6 %net_moments.1 = (f32[128,128]{1,0:T(8,128)S(1)}, f32[128,128]{1,0:T(8,128)S(1)}, f32[128,128]{1,0:T(8,128)S(1)}, f32[128,128]{1,0:T(8,128)S(1)}) custom-call(f32[32,512]{1,0:T(8,128)S(1)} %bitcast.16, f32[2,32,512]{2,1,0:T(8,128)S(1)} %bitcast.14, s32[1,512]{1,0:T(1,128)S(1)} %bitcast.21, f32[104,512]{1,0:T(8,128)S(1)} %collective-permute-done.other_ref.refs_1_, ...), custom_call_target="tpu_custom_call" | custom-call | flops 20000000000 | bytes 100000 | tf_op jit(solution)/shard_map/net_moments/pallas_call | solution.py:302
  22.2 0.0 collective-permute-done.3.refs_4_
  22.2 0.0 collective-permute-done.2.refs_3_
  22.3 0.0 collective-permute-done.1.refs_2_
  22.3 0.0 copy-start
  22.3 0.1 collective-permute-start.4
  22.4 2.0 %collective-permute-start.5 = (f32[128,128]{1,0:T(8,128)S(1)}, f32[128,128]{1,0:T(8,128)S(1)}, u32[]{:S(2)}, u32[]{:S(2)}) collective-permute-start(f32[128,128]{1,0:T(8,128)S(1)} %get-tuple-element.26), channel_id=1, source_target_pairs={{0,8},{8,0},{16,24},{24,16},{1,9},{9,1},{17,25},{25,17},{2,10},{10... | collective-permute-start | bytes 196616 | tf_op jit(solution)/shard_map/ppermute | solution.py:298
  24.4 0.0 collective-permute-start.6
  24.4 0.0 copy-start.7
  24.4 2.4 %collective-permute-start.7 = (f32[128,128]{1,0:T(8,128)S(1)}, f32[128,128]{1,0:T(8,128)S(1)}, u32[]{:S(2)}, u32[]{:S(2)}) collective-permute-start(f32[128,128]{1,0:T(8,128)S(1)} %get-tuple-element.28), channel_id=1, source_target_pairs={{0,24},{8,16},{16,8},{24,0},{1,25},{9,17},{17,9},{25,1},{2,26},{10... | collective-permute-start | bytes 196616 | tf_op jit(solution)/shard_map/ppermute | solution.py:298
  26.9 0.0 collective-permute-done.4.refs_5_
  26.9 0.0 copy-done
  26.9 0.0 copy-done.7
  26.9 4.1 %gram_first_pivots.1 = (f32[64,64]{1,0:T(8,128)S(1)}, f32[64,64]{1,0:T(8,128)S(1)}, f32[256,128]{1,0:T(8,128)S(1)}) custom-call(f32[72,512]{1,0:T(8,128)S(1)} %copy-done, f32[104,512]{1,0:T(8,128)S(1)} %collective-permute-done.other_ref.refs_1_, f32[72,512]{1,0:T(8,128)S(1)} %collective-permute-done.1.refs_2_, f32[72,512]{1,0:T(8,128)S(1)} %collective-permute-done.2.refs_3_, ...), custom_call_target="tpu_custom_call" | custom-call | flops 5000000000 | bytes 100000 | tf_op jit(solution)/shard_map/gram_first_pivots/pallas_call | solution.py:302
  31.0 0.0 collective-permute-done.5.refs_1_
  31.1 1.0 %collective-permute-done.6.refs_2_ = f32[128,128]{1,0:T(8,128)S(1)} collective-permute-done((f32[128,128]{1,0:T(8,128)S(1)}, f32[128,128]{1,0:T(8,128)S(1)}, u32[]{:S(2)}, u32[]{:S(2)}) %collective-permute-start.6) | collective-permute-done | bytes 65568 | tf_op jit(solution)/shard_map/ppermute | solution.py:298
  32.1 0.0 collective-permute-done.7.refs_3_
  32.1 2.7 %collective-permute-start.10 = (f32[128,128]{1,0:T(8,128)S(1)}, f32[128,128]{1,0:T(8,128)S(1)}, u32[]{:S(2)}, u32[]{:S(2)}) collective-permute-start(f32[128,128]{1,0:T(8,128)S(1)} %group_sum.1.refs_0_), channel_id=1, source_target_pairs={{0,6},{1,7},{2,4},{3,5},{4,2},{5,3},{6,0},{7,1},{8,14},{9,15},{10,... | collective-permute-start | bytes 196616 | tf_op jit(solution)/shard_map/ppermute | solution.py:298
  34.8 0.5 %collective-permute-start.9 = (f32[128,128]{1,0:T(8,128)S(1)}, f32[128,128]{1,0:T(8,128)S(1)}, u32[]{:S(2)}, u32[]{:S(2)}) collective-permute-start(f32[128,128]{1,0:T(8,128)S(1)} %group_sum.1.refs_0_), channel_id=1, source_target_pairs={{0,4},{1,5},{2,6},{3,7},{4,0},{5,1},{6,2},{7,3},{8,12},{9,13},{10,... | collective-permute-start | bytes 196616 | tf_op jit(solution)/shard_map/ppermute | solution.py:298
  35.3 0.3 collective-permute-start.8
  35.7 2.8 %gram_inverse.1.refs_4_ = f32[128,128]{1,0:T(8,128)S(1)} custom-call(f32[64,64]{1,0:T(8,128)S(1)} %get-tuple-element.29.gram_ref, f32[64,64]{1,0:T(8,128)S(1)} %get-tuple-element.30.mat_ref), custom_call_target="tpu_custom_call" | custom-call | flops 3000000000 | bytes 100000 | tf_op jit(solution)/shard_map/gram_inverse/pallas_call | solution.py:302
  38.4 0.0 collective-permute-done.10.refs_3_
  38.4 0.7 %collective-permute-done.9.refs_2_ = f32[128,128]{1,0:T(8,128)S(1)} collective-permute-done((f32[128,128]{1,0:T(8,128)S(1)}, f32[128,128]{1,0:T(8,128)S(1)}, u32[]{:S(2)}, u32[]{:S(2)}) %collective-permute-start.9) | collective-permute-done | bytes 65568 | tf_op jit(solution)/shard_map/ppermute | solution.py:298
  39.1 0.5 %collective-permute-done.8.refs_1_ = f32[128,128]{1,0:T(8,128)S(1)} collective-permute-done((f32[128,128]{1,0:T(8,128)S(1)}, f32[128,128]{1,0:T(8,128)S(1)}, u32[]{:S(2)}, u32[]{:S(2)}) %collective-permute-start.8) | collective-permute-done | bytes 65568 | tf_op jit(solution)/shard_map/ppermute | solution.py:298
  39.6 0.2 set_coeffs.1.mine_ref
  39.8 0.1 collective-permute-start.11
  39.9 1.2 %collective-permute-done.11.other_ref = f32[128,128]{1,0:T(8,128)S(1)} collective-permute-done((f32[128,128]{1,0:T(8,128)S(1)}, f32[128,128]{1,0:T(8,128)S(1)}, u32[]{:S(2)}, u32[]{:S(2)}) %collective-permute-start.11) | collective-permute-done | bytes 65568 | tf_op jit(solution)/shard_map/ppermute | solution.py:298
  41.1 2.7 %set_exposure.1 = (f32[2,256,512]{2,1,0:T(8,128)}, f32[2,256]{1,0:T(2,128)}) custom-call(f32[128,128]{1,0:T(8,128)S(1)} %set_coeffs.1.mine_ref, f32[128,128]{1,0:T(8,128)S(1)} %collective-permute-done.11.other_ref, f32[256,128]{1,0:T(8,128)S(1)} %get-tuple-element.31.limits_ref, f32[72,512]{1,0:T(8,128)S(1)} %copy-done, ...), custom_call_target="tpu_custom_call" | custom-call | flops 2000000000 | bytes 100000 | tf_op jit(solution)/shard_map/set_exposure/pallas_call | solution.py:302
  (2 shorter events, 0.0 us)
Async XLA Ops:
  0.6 6.3 %copy-start.1 = (f32[2,512,32]{1,2,0:T(8,128)S(1)}, f32[2,512,32]{1,2,0:T(8,128)}, u32[]{:S(2)}) copy-start(f32[2,512,32]{1,2,0:T(8,128)} %param.10) | copy-start | bytes 393220
  0.6 6.3 %copy-start.2 = (f32[512,32]{0,1:T(8,128)S(1)}, f32[512,32]{0,1:T(8,128)}, u32[]{:S(2)}) copy-start(f32[512,32]{0,1:T(8,128)} %param.9) | copy-start | bytes 196612
  0.7 6.3 %copy-start.3 = (f32[8192]{0:T(1024)S(1)}, f32[8192]{0:T(1024)}, u32[]{:S(2)}) copy-start(f32[8192]{0:T(1024)} %param.12) | copy-start | bytes 98308
  0.7 6.3 %copy-start.4 = (f32[8192]{0:T(1024)S(1)}, f32[8192]{0:T(1024)}, u32[]{:S(2)}) copy-start(f32[8192]{0:T(1024)} %param.13) | copy-start | bytes 98308
  0.7 6.3 %copy-start.5 = (s32[8192]{0:T(1024)S(1)}, s32[8192]{0:T(1024)}, u32[]{:S(2)}) copy-start(s32[8192]{0:T(1024)} %param.14) | copy-start | bytes 98308
  2.4 4.5 %collective-permute-start = (f32[104,512]{1,0:T(8,128)}, f32[104,512]{1,0:T(8,128)S(1)}, u32[]{:S(2)}, u32[]{:S(2)}) collective-permute-start(f32[104,512]{1,0:T(8,128)} %get-tuple-element.18), channel_id=1, source_target_pairs={{0,1},{1,0},{2,3},{3,2},{4,5},{5,4},{6,7},{7,6},{8,9},{9,8},{10,11... | collective-permute-start | bytes 638984 | tf_op jit(solution)/shard_map/ppermute | solution.py:298
  2.9 19.4 %collective-permute-start.3 = (f32[72,512]{1,0:T(8,128)}, f32[72,512]{1,0:T(8,128)S(1)}, u32[]{:S(2)}, u32[]{:S(2)}) collective-permute-start(f32[72,512]{1,0:T(8,128)} %get-tuple-element.17.refs_0_), channel_id=1, source_target_pairs={{0,6},{1,7},{2,4},{3,5},{4,2},{5,3},{6,0},{7,1},{8,14},{9,15},{10,... | collective-permute-start | bytes 442376 | tf_op jit(solution)/shard_map/ppermute | solution.py:298
  6.3 15.9 %collective-permute-start.2 = (f32[72,512]{1,0:T(8,128)}, f32[72,512]{1,0:T(8,128)S(1)}, u32[]{:S(2)}, u32[]{:S(2)}) collective-permute-start(f32[72,512]{1,0:T(8,128)} %get-tuple-element.17.refs_0_), channel_id=1, source_target_pairs={{0,4},{1,5},{2,6},{3,7},{4,0},{5,1},{6,2},{7,3},{8,12},{9,13},{10,... | collective-permute-start | bytes 442376 | tf_op jit(solution)/shard_map/ppermute | solution.py:298
  6.8 15.4 %collective-permute-start.1 = (f32[72,512]{1,0:T(8,128)}, f32[72,512]{1,0:T(8,128)S(1)}, u32[]{:S(2)}, u32[]{:S(2)}) collective-permute-start(f32[72,512]{1,0:T(8,128)} %get-tuple-element.17.refs_0_), channel_id=1, source_target_pairs={{0,2},{1,3},{2,0},{3,1},{4,6},{5,7},{6,4},{7,5},{8,10},{9,11},{10,... | collective-permute-start | bytes 442376 | tf_op jit(solution)/shard_map/ppermute | solution.py:298
  7.0 0.7 %copy-start.6 = (s32[512]{0:T(512)S(1)}, s32[512]{0:T(512)}, u32[]{:S(2)}) copy-start(s32[512]{0:T(512)} %param.16) | copy-start | bytes 6148
  22.3 4.6 %copy-start = (f32[72,512]{1,0:T(8,128)S(1)}, f32[72,512]{1,0:T(8,128)}, u32[]{:S(2)}) copy-start(f32[72,512]{1,0:T(8,128)} %get-tuple-element.17.refs_0_) | copy-start | bytes 442372
  22.3 4.6 %collective-permute-start.4 = (f32[3,72,512]{2,1,0:T(8,128)S(1)}, f32[3,72,512]{2,1,0:T(8,128)S(1)}, u32[]{:S(2)}, u32[]{:S(2)}) collective-permute-start(f32[3,72,512]{2,1,0:T(8,128)S(1)} %pad_maximum_fusion), channel_id=1, source_target_pairs={{0,1},{1,0},{2,3},{3,2},{4,5},{5,4},{6,7},{7,6},{8,9},{9,8},{10,11... | collective-permute-start | bytes 1327112 | tf_op jit(solution)/shard_map/ppermute | solution.py:298
  22.4 8.7 %collective-permute-start.5 = (f32[128,128]{1,0:T(8,128)S(1)}, f32[128,128]{1,0:T(8,128)S(1)}, u32[]{:S(2)}, u32[]{:S(2)}) collective-permute-start(f32[128,128]{1,0:T(8,128)S(1)} %get-tuple-element.26), channel_id=1, source_target_pairs={{0,8},{8,0},{16,24},{24,16},{1,9},{9,1},{17,25},{25,17},{2,10},{10... | collective-permute-start | bytes 196616 | tf_op jit(solution)/shard_map/ppermute | solution.py:298
  24.4 7.6 %collective-permute-start.6 = (f32[128,128]{1,0:T(8,128)S(1)}, f32[128,128]{1,0:T(8,128)S(1)}, u32[]{:S(2)}, u32[]{:S(2)}) collective-permute-start(f32[128,128]{1,0:T(8,128)S(1)} %get-tuple-element.27), channel_id=1, source_target_pairs={{0,16},{8,24},{16,0},{24,8},{1,17},{9,25},{17,1},{25,9},{2,18},{10... | collective-permute-start | bytes 196616 | tf_op jit(solution)/shard_map/ppermute | solution.py:298
  24.4 2.4 %copy-start.7 = (s32[256]{0:T(256)S(1)}, s32[256]{0:T(256)}, u32[]{:S(2)}) copy-start(s32[256]{0:T(256)} %param.17) | copy-start | bytes 3076
  24.4 7.6 %collective-permute-start.7 = (f32[128,128]{1,0:T(8,128)S(1)}, f32[128,128]{1,0:T(8,128)S(1)}, u32[]{:S(2)}, u32[]{:S(2)}) collective-permute-start(f32[128,128]{1,0:T(8,128)S(1)} %get-tuple-element.28), channel_id=1, source_target_pairs={{0,24},{8,16},{16,8},{24,0},{1,25},{9,17},{17,9},{25,1},{2,26},{10... | collective-permute-start | bytes 196616 | tf_op jit(solution)/shard_map/ppermute | solution.py:298
  32.1 6.3 %collective-permute-start.10 = (f32[128,128]{1,0:T(8,128)S(1)}, f32[128,128]{1,0:T(8,128)S(1)}, u32[]{:S(2)}, u32[]{:S(2)}) collective-permute-start(f32[128,128]{1,0:T(8,128)S(1)} %group_sum.1.refs_0_), channel_id=1, source_target_pairs={{0,6},{1,7},{2,4},{3,5},{4,2},{5,3},{6,0},{7,1},{8,14},{9,15},{10,... | collective-permute-start | bytes 196616 | tf_op jit(solution)/shard_map/ppermute | solution.py:298
  34.8 4.3 %collective-permute-start.9 = (f32[128,128]{1,0:T(8,128)S(1)}, f32[128,128]{1,0:T(8,128)S(1)}, u32[]{:S(2)}, u32[]{:S(2)}) collective-permute-start(f32[128,128]{1,0:T(8,128)S(1)} %group_sum.1.refs_0_), channel_id=1, source_target_pairs={{0,4},{1,5},{2,6},{3,7},{4,0},{5,1},{6,2},{7,3},{8,12},{9,13},{10,... | collective-permute-start | bytes 196616 | tf_op jit(solution)/shard_map/ppermute | solution.py:298
  35.3 4.3 %collective-permute-start.8 = (f32[128,128]{1,0:T(8,128)S(1)}, f32[128,128]{1,0:T(8,128)S(1)}, u32[]{:S(2)}, u32[]{:S(2)}) collective-permute-start(f32[128,128]{1,0:T(8,128)S(1)} %group_sum.1.refs_0_), channel_id=1, source_target_pairs={{0,2},{1,3},{2,0},{3,1},{4,6},{5,7},{6,4},{7,5},{8,10},{9,11},{10,... | collective-permute-start | bytes 196616 | tf_op jit(solution)/shard_map/ppermute | solution.py:298
  39.8 1.3 %collective-permute-start.11 = (f32[128,128]{1,0:T(8,128)S(1)}, f32[128,128]{1,0:T(8,128)S(1)}, u32[]{:S(2)}, u32[]{:S(2)}) collective-permute-start(f32[128,128]{1,0:T(8,128)S(1)} %set_coeffs.1.mine_ref), channel_id=1, source_target_pairs={{0,1},{1,0},{2,3},{3,2},{4,5},{5,4},{6,7},{7,6},{8,9},{9,8},{10,11... | collective-permute-start | bytes 196616 | tf_op jit(solution)/shard_map/ppermute | solution.py:298

commit v11 on v9

--- a/solution.py
+++ b/solution.py
@@ -15,7 +15,7 @@
 SCALE = 256.0
 TILE = 512
 CHUNK = 1024
-SLOTS = 4
+SLOTS = 8
 FIRST_PIVOTS = 36
 DEPTH = 256
 PAD = 8

time: 44.9 us -> 45.2 us (level)
  local copies, waits for them, and re-layouts: 1.33 us -> 0.67 us
  waiting for transfers between devices: 3.51 us -> 3.99 us
    unnamed x16, local copies, waits for them, and re-layouts: 1.33 us -> 0.67 us
    ppermute x12, waiting for transfers between devices: 3.51 us -> 3.99 us  [swap(): lax.ppermute(x, axis, [(i, i ^ away) for i in range(lax.axis_size(axis))])]
  transfers between devices with their start and end apart: 12 -> 12, of which waited for: 5 -> 4; matrix products, arithmetic and copies ran while one was open for 0% -> 0% of each run, Pallas kernels for 48% -> 49%
where the time goes in v11:
time: 45.2 us; the launch traced here: 44.9 us
  Pallas kernels  26.4 us (58%)
  starting transfers between devices  12.8 us (28%)
  waiting for transfers between devices  3.99 us (9%)
  between operations  0.97 us (2%)
  local copies, waits for them, and re-layouts  0.67 us (1%)
    pallas_call x7, Pallas kernels, run(): pl.pallas_call(kernel, out_shape=out, in_specs=specs, out_specs=out_specs...  26.4 us
    ppermute x12, starting transfers between devices, swap(): lax.ppermute(x, axis, [(i, i ^ away) for i in range(lax.axis_size(axis))])  12.8 us
    ppermute x12, waiting for transfers between devices, swap(): lax.ppermute(x, axis, [(i, i ^ away) for i in range(lax.axis_size(axis))])  3.99 us
  transfers between devices with their start and end apart: 12, of which 4 were waited for; matrix products, arithmetic and copies ran while one was open for 0% of the time, Pallas kernels for 49%

profile of v11, /device:TPU:0, one launch (start us, length us, event | category | flops | bytes accessed | tf_op | source)
XLA Modules:
  0.0 44.9 jit_solution(11813089240456879779)
XLA Ops:
  0.6 0.0 copy-start.1
  0.6 0.0 copy-start.2
  0.7 0.0 copy-start.3
  0.7 0.0 copy-start.4
  0.7 0.0 copy-start.5
  0.7 1.7 %pack_states.1 = (f32[72,512]{1,0:T(8,128)}, f32[104,512]{1,0:T(8,128)}) custom-call(s32[4]{0:T(128)} %counts_ref.1, f32[32,512]{1,0:T(8,128)} %bitcast.15, f32[2,32,512]{2,1,0:T(8,128)} %bitcast.13, s32[1,512]{1,0:T(1,128)} %bitcast.20), custom_call_target="tpu_custom_call" | custom-call | flops 20000000000 | bytes 100000 | tf_op jit(solution)/shard_map/pack_states/pallas_call | solution.py:302
  2.4 0.5 %collective-permute-start = (f32[104,512]{1,0:T(8,128)}, f32[104,512]{1,0:T(8,128)S(1)}, u32[]{:S(2)}, u32[]{:S(2)}) collective-permute-start(f32[104,512]{1,0:T(8,128)} %get-tuple-element.18), channel_id=1, source_target_pairs={{0,1},{1,0},{2,3},{3,2},{4,5},{5,4},{6,7},{7,6},{8,9},{9,8},{10,11... | collective-permute-start | bytes 638984 | tf_op jit(solution)/shard_map/ppermute | solution.py:298
  2.9 3.4 %collective-permute-start.3 = (f32[72,512]{1,0:T(8,128)}, f32[72,512]{1,0:T(8,128)S(1)}, u32[]{:S(2)}, u32[]{:S(2)}) collective-permute-start(f32[72,512]{1,0:T(8,128)} %get-tuple-element.17.refs_0_), channel_id=1, source_target_pairs={{0,6},{1,7},{2,4},{3,5},{4,2},{5,3},{6,0},{7,1},{8,14},{9,15},{10,... | collective-permute-start | bytes 442376 | tf_op jit(solution)/shard_map/ppermute | solution.py:298
  6.3 0.5 %collective-permute-start.2 = (f32[72,512]{1,0:T(8,128)}, f32[72,512]{1,0:T(8,128)S(1)}, u32[]{:S(2)}, u32[]{:S(2)}) collective-permute-start(f32[72,512]{1,0:T(8,128)} %get-tuple-element.17.refs_0_), channel_id=1, source_target_pairs={{0,4},{1,5},{2,6},{3,7},{4,0},{5,1},{6,2},{7,3},{8,12},{9,13},{10,... | collective-permute-start | bytes 442376 | tf_op jit(solution)/shard_map/ppermute | solution.py:298
  6.8 0.1 collective-permute-start.1
  7.0 0.0 collective-permute-done.other_ref.refs_1_
  7.0 0.0 copy-start.6
  7.0 0.0 copy-done.1
  7.0 0.0 copy-done.2
  7.0 0.0 copy-done.3
  7.0 0.0 copy-done.4
  7.0 0.0 copy-done.5
  7.0 0.6 %copy-done.6 = s32[512]{0:T(512)S(1)} copy-done((s32[512]{0:T(512)S(1)}, s32[512]{0:T(512)}, u32[]{:S(2)}) %copy-start.6) | copy-done | bytes 2072
  7.6 14.9 %net_moments.1 = (f32[128,128]{1,0:T(8,128)S(1)}, f32[128,128]{1,0:T(8,128)S(1)}, f32[128,128]{1,0:T(8,128)S(1)}, f32[128,128]{1,0:T(8,128)S(1)}) custom-call(f32[32,512]{1,0:T(8,128)S(1)} %bitcast.16, f32[2,32,512]{2,1,0:T(8,128)S(1)} %bitcast.14, s32[1,512]{1,0:T(1,128)S(1)} %bitcast.21, f32[104,512]{1,0:T(8,128)S(1)} %collective-permute-done.other_ref.refs_1_, ...), custom_call_target="tpu_custom_call" | custom-call | flops 20000000000 | bytes 100000 | tf_op jit(solution)/shard_map/net_moments/pallas_call | solution.py:302
  22.5 0.0 collective-permute-done.3.refs_4_
  22.5 0.0 collective-permute-done.2.refs_3_
  22.6 0.0 collective-permute-done.1.refs_2_
  22.6 0.0 copy-start
  22.6 0.1 collective-permute-start.4
  22.7 2.0 %collective-permute-start.5 = (f32[128,128]{1,0:T(8,128)S(1)}, f32[128,128]{1,0:T(8,128)S(1)}, u32[]{:S(2)}, u32[]{:S(2)}) collective-permute-start(f32[128,128]{1,0:T(8,128)S(1)} %get-tuple-element.26), channel_id=1, source_target_pairs={{0,8},{8,0},{16,24},{24,16},{1,9},{9,1},{17,25},{25,17},{2,10},{10... | collective-permute-start | bytes 196616 | tf_op jit(solution)/shard_map/ppermute | solution.py:298
  24.7 1.1 %collective-permute-start.6 = (f32[128,128]{1,0:T(8,128)S(1)}, f32[128,128]{1,0:T(8,128)S(1)}, u32[]{:S(2)}, u32[]{:S(2)}) collective-permute-start(f32[128,128]{1,0:T(8,128)S(1)} %get-tuple-element.27), channel_id=1, source_target_pairs={{0,16},{8,24},{16,0},{24,8},{1,17},{9,25},{17,1},{25,9},{2,18},{10... | collective-permute-start | bytes 196616 | tf_op jit(solution)/shard_map/ppermute | solution.py:298
  25.8 0.0 copy-start.7
  25.8 1.4 %collective-permute-start.7 = (f32[128,128]{1,0:T(8,128)S(1)}, f32[128,128]{1,0:T(8,128)S(1)}, u32[]{:S(2)}, u32[]{:S(2)}) collective-permute-start(f32[128,128]{1,0:T(8,128)S(1)} %get-tuple-element.28), channel_id=1, source_target_pairs={{0,24},{8,16},{16,8},{24,0},{1,25},{9,17},{17,9},{25,1},{2,26},{10... | collective-permute-start | bytes 196616 | tf_op jit(solution)/shard_map/ppermute | solution.py:298
  27.2 0.0 collective-permute-done.4.refs_5_
  27.2 0.0 copy-done
  27.2 0.0 copy-done.7
  27.2 4.1 %gram_first_pivots.1 = (f32[64,64]{1,0:T(8,128)S(1)}, f32[64,64]{1,0:T(8,128)S(1)}, f32[256,128]{1,0:T(8,128)S(1)}) custom-call(f32[72,512]{1,0:T(8,128)S(1)} %copy-done, f32[104,512]{1,0:T(8,128)S(1)} %collective-permute-done.other_ref.refs_1_, f32[72,512]{1,0:T(8,128)S(1)} %collective-permute-done.1.refs_2_, f32[72,512]{1,0:T(8,128)S(1)} %collective-permute-done.2.refs_3_, ...), custom_call_target="tpu_custom_call" | custom-call | flops 5000000000 | bytes 100000 | tf_op jit(solution)/shard_map/gram_first_pivots/pallas_call | solution.py:302
  31.4 0.0 collective-permute-done.5.refs_1_
  31.4 1.8 %collective-permute-done.6.refs_2_ = f32[128,128]{1,0:T(8,128)S(1)} collective-permute-done((f32[128,128]{1,0:T(8,128)S(1)}, f32[128,128]{1,0:T(8,128)S(1)}, u32[]{:S(2)}, u32[]{:S(2)}) %collective-permute-start.6) | collective-permute-done | bytes 65568 | tf_op jit(solution)/shard_map/ppermute | solution.py:298
  33.2 0.0 collective-permute-done.7.refs_3_
  33.2 2.5 %collective-permute-start.10 = (f32[128,128]{1,0:T(8,128)S(1)}, f32[128,128]{1,0:T(8,128)S(1)}, u32[]{:S(2)}, u32[]{:S(2)}) collective-permute-start(f32[128,128]{1,0:T(8,128)S(1)} %group_sum.1.refs_0_), channel_id=1, source_target_pairs={{0,6},{1,7},{2,4},{3,5},{4,2},{5,3},{6,0},{7,1},{8,14},{9,15},{10,... | collective-permute-start | bytes 196616 | tf_op jit(solution)/shard_map/ppermute | solution.py:298
  35.7 0.5 %collective-permute-start.9 = (f32[128,128]{1,0:T(8,128)S(1)}, f32[128,128]{1,0:T(8,128)S(1)}, u32[]{:S(2)}, u32[]{:S(2)}) collective-permute-start(f32[128,128]{1,0:T(8,128)S(1)} %group_sum.1.refs_0_), channel_id=1, source_target_pairs={{0,4},{1,5},{2,6},{3,7},{4,0},{5,1},{6,2},{7,3},{8,12},{9,13},{10,... | collective-permute-start | bytes 196616 | tf_op jit(solution)/shard_map/ppermute | solution.py:298
  36.2 0.5 %collective-permute-start.8 = (f32[128,128]{1,0:T(8,128)S(1)}, f32[128,128]{1,0:T(8,128)S(1)}, u32[]{:S(2)}, u32[]{:S(2)}) collective-permute-start(f32[128,128]{1,0:T(8,128)S(1)} %group_sum.1.refs_0_), channel_id=1, source_target_pairs={{0,2},{1,3},{2,0},{3,1},{4,6},{5,7},{6,4},{7,5},{8,10},{9,11},{10,... | collective-permute-start | bytes 196616 | tf_op jit(solution)/shard_map/ppermute | solution.py:298
  36.7 2.8 %gram_inverse.1.refs_4_ = f32[128,128]{1,0:T(8,128)S(1)} custom-call(f32[64,64]{1,0:T(8,128)S(1)} %get-tuple-element.29.gram_ref, f32[64,64]{1,0:T(8,128)S(1)} %get-tuple-element.30.mat_ref), custom_call_target="tpu_custom_call" | custom-call | flops 3000000000 | bytes 100000 | tf_op jit(solution)/shard_map/gram_inverse/pallas_call | solution.py:302
  39.5 0.0 collective-permute-done.10.refs_3_
  39.5 0.4 collective-permute-done.9.refs_2_
  40.0 0.5 %collective-permute-done.8.refs_1_ = f32[128,128]{1,0:T(8,128)S(1)} collective-permute-done((f32[128,128]{1,0:T(8,128)S(1)}, f32[128,128]{1,0:T(8,128)S(1)}, u32[]{:S(2)}, u32[]{:S(2)}) %collective-permute-start.8) | collective-permute-done | bytes 65568 | tf_op jit(solution)/shard_map/ppermute | solution.py:298
  40.5 0.2 set_coeffs.1.mine_ref
  40.7 0.1 collective-permute-start.11
  40.7 1.2 %collective-permute-done.11.other_ref = f32[128,128]{1,0:T(8,128)S(1)} collective-permute-done((f32[128,128]{1,0:T(8,128)S(1)}, f32[128,128]{1,0:T(8,128)S(1)}, u32[]{:S(2)}, u32[]{:S(2)}) %collective-permute-start.11) | collective-permute-done | bytes 65568 | tf_op jit(solution)/shard_map/ppermute | solution.py:298
  42.0 2.7 %set_exposure.1 = (f32[2,256,512]{2,1,0:T(8,128)}, f32[2,256]{1,0:T(2,128)}) custom-call(f32[128,128]{1,0:T(8,128)S(1)} %set_coeffs.1.mine_ref, f32[128,128]{1,0:T(8,128)S(1)} %collective-permute-done.11.other_ref, f32[256,128]{1,0:T(8,128)S(1)} %get-tuple-element.31.limits_ref, f32[72,512]{1,0:T(8,128)S(1)} %copy-done, ...), custom_call_target="tpu_custom_call" | custom-call | flops 2000000000 | bytes 100000 | tf_op jit(solution)/shard_map/set_exposure/pallas_call | solution.py:302
  (2 shorter events, 0.0 us)
Async XLA Ops:
  0.6 6.3 %copy-start.1 = (f32[2,512,32]{1,2,0:T(8,128)S(1)}, f32[2,512,32]{1,2,0:T(8,128)}, u32[]{:S(2)}) copy-start(f32[2,512,32]{1,2,0:T(8,128)} %param.10) | copy-start | bytes 393220
  0.6 6.3 %copy-start.2 = (f32[512,32]{0,1:T(8,128)S(1)}, f32[512,32]{0,1:T(8,128)}, u32[]{:S(2)}) copy-start(f32[512,32]{0,1:T(8,128)} %param.9) | copy-start | bytes 196612
  0.7 6.3 %copy-start.3 = (f32[8192]{0:T(1024)S(1)}, f32[8192]{0:T(1024)}, u32[]{:S(2)}) copy-start(f32[8192]{0:T(1024)} %param.12) | copy-start | bytes 98308
  0.7 6.3 %copy-start.4 = (f32[8192]{0:T(1024)S(1)}, f32[8192]{0:T(1024)}, u32[]{:S(2)}) copy-start(f32[8192]{0:T(1024)} %param.13) | copy-start | bytes 98308
  0.7 6.3 %copy-start.5 = (s32[8192]{0:T(1024)S(1)}, s32[8192]{0:T(1024)}, u32[]{:S(2)}) copy-start(s32[8192]{0:T(1024)} %param.14) | copy-start | bytes 98308
  2.4 4.5 %collective-permute-start = (f32[104,512]{1,0:T(8,128)}, f32[104,512]{1,0:T(8,128)S(1)}, u32[]{:S(2)}, u32[]{:S(2)}) collective-permute-start(f32[104,512]{1,0:T(8,128)} %get-tuple-element.18), channel_id=1, source_target_pairs={{0,1},{1,0},{2,3},{3,2},{4,5},{5,4},{6,7},{7,6},{8,9},{9,8},{10,11... | collective-permute-start | bytes 638984 | tf_op jit(solution)/shard_map/ppermute | solution.py:298
  2.9 19.7 %collective-permute-start.3 = (f32[72,512]{1,0:T(8,128)}, f32[72,512]{1,0:T(8,128)S(1)}, u32[]{:S(2)}, u32[]{:S(2)}) collective-permute-start(f32[72,512]{1,0:T(8,128)} %get-tuple-element.17.refs_0_), channel_id=1, source_target_pairs={{0,6},{1,7},{2,4},{3,5},{4,2},{5,3},{6,0},{7,1},{8,14},{9,15},{10,... | collective-permute-start | bytes 442376 | tf_op jit(solution)/shard_map/ppermute | solution.py:298
  6.3 16.2 %collective-permute-start.2 = (f32[72,512]{1,0:T(8,128)}, f32[72,512]{1,0:T(8,128)S(1)}, u32[]{:S(2)}, u32[]{:S(2)}) collective-permute-start(f32[72,512]{1,0:T(8,128)} %get-tuple-element.17.refs_0_), channel_id=1, source_target_pairs={{0,4},{1,5},{2,6},{3,7},{4,0},{5,1},{6,2},{7,3},{8,12},{9,13},{10,... | collective-permute-start | bytes 442376 | tf_op jit(solution)/shard_map/ppermute | solution.py:298
  6.8 15.7 %collective-permute-start.1 = (f32[72,512]{1,0:T(8,128)}, f32[72,512]{1,0:T(8,128)S(1)}, u32[]{:S(2)}, u32[]{:S(2)}) collective-permute-start(f32[72,512]{1,0:T(8,128)} %get-tuple-element.17.refs_0_), channel_id=1, source_target_pairs={{0,2},{1,3},{2,0},{3,1},{4,6},{5,7},{6,4},{7,5},{8,10},{9,11},{10,... | collective-permute-start | bytes 442376 | tf_op jit(solution)/shard_map/ppermute | solution.py:298
  7.0 0.7 %copy-start.6 = (s32[512]{0:T(512)S(1)}, s32[512]{0:T(512)}, u32[]{:S(2)}) copy-start(s32[512]{0:T(512)} %param.16) | copy-start | bytes 6148
  22.6 4.7 %copy-start = (f32[72,512]{1,0:T(8,128)S(1)}, f32[72,512]{1,0:T(8,128)}, u32[]{:S(2)}) copy-start(f32[72,512]{1,0:T(8,128)} %get-tuple-element.17.refs_0_) | copy-start | bytes 442372
  22.6 4.6 %collective-permute-start.4 = (f32[3,72,512]{2,1,0:T(8,128)S(1)}, f32[3,72,512]{2,1,0:T(8,128)S(1)}, u32[]{:S(2)}, u32[]{:S(2)}) collective-permute-start(f32[3,72,512]{2,1,0:T(8,128)S(1)} %pad_maximum_fusion), channel_id=1, source_target_pairs={{0,1},{1,0},{2,3},{3,2},{4,5},{5,4},{6,7},{7,6},{8,9},{9,8},{10,11... | collective-permute-start | bytes 1327112 | tf_op jit(solution)/shard_map/ppermute | solution.py:298
  22.7 8.7 %collective-permute-start.5 = (f32[128,128]{1,0:T(8,128)S(1)}, f32[128,128]{1,0:T(8,128)S(1)}, u32[]{:S(2)}, u32[]{:S(2)}) collective-permute-start(f32[128,128]{1,0:T(8,128)S(1)} %get-tuple-element.26), channel_id=1, source_target_pairs={{0,8},{8,0},{16,24},{24,16},{1,9},{9,1},{17,25},{25,17},{2,10},{10... | collective-permute-start | bytes 196616 | tf_op jit(solution)/shard_map/ppermute | solution.py:298
  24.7 8.4 %collective-permute-start.6 = (f32[128,128]{1,0:T(8,128)S(1)}, f32[128,128]{1,0:T(8,128)S(1)}, u32[]{:S(2)}, u32[]{:S(2)}) collective-permute-start(f32[128,128]{1,0:T(8,128)S(1)} %get-tuple-element.27), channel_id=1, source_target_pairs={{0,16},{8,24},{16,0},{24,8},{1,17},{9,25},{17,1},{25,9},{2,18},{10... | collective-permute-start | bytes 196616 | tf_op jit(solution)/shard_map/ppermute | solution.py:298
  25.8 1.4 %copy-start.7 = (s32[256]{0:T(256)S(1)}, s32[256]{0:T(256)}, u32[]{:S(2)}) copy-start(s32[256]{0:T(256)} %param.17) | copy-start | bytes 3076
  25.8 7.3 %collective-permute-start.7 = (f32[128,128]{1,0:T(8,128)S(1)}, f32[128,128]{1,0:T(8,128)S(1)}, u32[]{:S(2)}, u32[]{:S(2)}) collective-permute-start(f32[128,128]{1,0:T(8,128)S(1)} %get-tuple-element.28), channel_id=1, source_target_pairs={{0,24},{8,16},{16,8},{24,0},{1,25},{9,17},{17,9},{25,1},{2,26},{10... | collective-permute-start | bytes 196616 | tf_op jit(solution)/shard_map/ppermute | solution.py:298
  33.2 6.3 %collective-permute-start.10 = (f32[128,128]{1,0:T(8,128)S(1)}, f32[128,128]{1,0:T(8,128)S(1)}, u32[]{:S(2)}, u32[]{:S(2)}) collective-permute-start(f32[128,128]{1,0:T(8,128)S(1)} %group_sum.1.refs_0_), channel_id=1, source_target_pairs={{0,6},{1,7},{2,4},{3,5},{4,2},{5,3},{6,0},{7,1},{8,14},{9,15},{10,... | collective-permute-start | bytes 196616 | tf_op jit(solution)/shard_map/ppermute | solution.py:298
  35.7 4.3 %collective-permute-start.9 = (f32[128,128]{1,0:T(8,128)S(1)}, f32[128,128]{1,0:T(8,128)S(1)}, u32[]{:S(2)}, u32[]{:S(2)}) collective-permute-start(f32[128,128]{1,0:T(8,128)S(1)} %group_sum.1.refs_0_), channel_id=1, source_target_pairs={{0,4},{1,5},{2,6},{3,7},{4,0},{5,1},{6,2},{7,3},{8,12},{9,13},{10,... | collective-permute-start | bytes 196616 | tf_op jit(solution)/shard_map/ppermute | solution.py:298
  36.2 4.3 %collective-permute-start.8 = (f32[128,128]{1,0:T(8,128)S(1)}, f32[128,128]{1,0:T(8,128)S(1)}, u32[]{:S(2)}, u32[]{:S(2)}) collective-permute-start(f32[128,128]{1,0:T(8,128)S(1)} %group_sum.1.refs_0_), channel_id=1, source_target_pairs={{0,2},{1,3},{2,0},{3,1},{4,6},{5,7},{6,4},{7,5},{8,10},{9,11},{10,... | collective-permute-start | bytes 196616 | tf_op jit(solution)/shard_map/ppermute | solution.py:298
  40.7 1.3 %collective-permute-start.11 = (f32[128,128]{1,0:T(8,128)S(1)}, f32[128,128]{1,0:T(8,128)S(1)}, u32[]{:S(2)}, u32[]{:S(2)}) collective-permute-start(f32[128,128]{1,0:T(8,128)S(1)} %set_coeffs.1.mine_ref), channel_id=1, source_target_pairs={{0,1},{1,0},{2,3},{3,2},{4,5},{5,4},{6,7},{7,6},{8,9},{9,8},{10,11... | collective-permute-start | bytes 196616 | tf_op jit(solution)/shard_map/ppermute | solution.py:298
